TPU v7x, 512 devices: a whole 4x8x8 slice. The times are simulated.
512 devices in a mesh: wide: 64 (over z, y_lo, core), narrow: 8 (over y_hi, x).
Axes of the slice: x: 4, y: 8 (y_hi: 2, y_lo: 4; y = y_hi * 4 + y_lo), z: 8, core: 2. Of those that a mesh axis runs over, the one named last changes fastest.
Arguments:
- volume: float32 [256, 128, 1024], P('wide', 'narrow'), may hold values from -12 to 12
Outputs:
- smoothed: float32 [256, 128, 1024], P('wide', 'narrow')
All inputs are finite; a program needn't handle non-finite values.
Results may differ from a plain program's by a relative error of at most 0.00019.
Values sent between devices are 32-bit elements; how exact they have to be, the bound alone decides.
No kernel may reach another device: no remote copies, remote signals or barrier semaphores. Data moves between devices by JAX's collectives and lax.ppermute only.
A program may use at most 64 MiB of HBM per device.

v0:
```python
import jax
import jax.numpy as jnp
from jax import lax
from jax.sharding import PartitionSpec as P

step_weight = 300.0
contrast_sq = 9.0


def with_halo(shard, sides, width):
    for axis, dim in sides:
        count, length = (lax.axis_size(axis), shard.shape[dim])
        up = [(i, (i + 1) % count) for i in range(count - 1)]
        down = [(j, i) for i, j in up]
        last = lax.slice_in_dim(shard, length - width, length, axis=dim)
        first = lax.slice_in_dim(shard, 0, width, axis=dim)
        before = lax.ppermute(last, axis, up)
        after = lax.ppermute(first, axis, down)
        shard = jnp.concatenate([before, shard, after], axis=dim)
    return shard


def cyclic_solve(lower, diag, upper, values):
    length = values.shape[0]
    if length == 1:
        return values / diag
    middle = length // 2

    def halves(field):
        paired = field.reshape((middle, 2) + field.shape[1:])
        return (paired[:, 0], paired[:, 1])

    def after(field, filler):
        return jnp.concatenate([field[1:], jnp.full_like(field[:1], filler)], 0)

    lower_even, lower_odd = halves(lower)
    diag_even, diag_odd = halves(diag)
    upper_even, upper_odd = halves(upper)
    value_even, value_odd = halves(values)
    factor_left = -lower_odd / diag_even
    factor_right = -upper_odd / after(diag_even, 1.0)
    odd_part = cyclic_solve(
        factor_left * lower_even,
        diag_odd + factor_left * upper_even + factor_right * after(lower_even, 0.0),
        factor_right * after(upper_even, 0.0),
        value_odd + factor_left * value_even + factor_right * after(value_even, 0.0),
    )
    previous = jnp.concatenate([jnp.zeros_like(odd_part[:1]), odd_part[:-1]], 0)
    even_part = (value_even - lower_even * previous - upper_even * odd_part) / diag_even
    return jnp.stack([even_part, odd_part], 1).reshape(values.shape)


def diffuse(values, cond):
    between = 0.5 * (cond[:-1] + cond[1:])
    edge = jnp.zeros_like(cond[:1])
    lower = jnp.concatenate([edge, -step_weight * between], 0)
    upper = jnp.concatenate([-step_weight * between, edge], 0)
    return cyclic_solve(lower, 1.0 - lower - upper, upper, values)


def per_device(volume):
    inl, crs, tms = volume.shape
    wide_count = lax.axis_size("wide")
    narrow_count = lax.axis_size("narrow")
    wide_rank = lax.axis_index("wide")
    narrow_rank = lax.axis_index("narrow")
    padded = with_halo(volume, (("wide", 0), ("narrow", 1)), 1)
    first_row = jnp.where(wide_rank == 0, padded[1:2], padded[0:1])
    final_row = jnp.where(wide_rank == wide_count - 1, padded[-2:-1], padded[-1:])
    padded = jnp.concatenate([first_row, padded[1:-1], final_row], 0)
    first_col = jnp.where(narrow_rank == 0, padded[:, 1:2], padded[:, 0:1])
    final_col = jnp.where(narrow_rank == narrow_count - 1, padded[:, -2:-1], padded[:, -1:])
    padded = jnp.concatenate([first_col, padded[:, 1:-1], final_col], 1)
    power = (0.5 * (padded[2:, 1:-1] - padded[:-2, 1:-1])) ** 2
    power = power + (0.5 * (padded[1:-1, 2:] - padded[1:-1, :-2])) ** 2
    timed = jnp.concatenate([volume[:, :, :1], volume, volume[:, :, -1:]], 2)
    power = power + (0.5 * (timed[:, :, 2:] - timed[:, :, :-2])) ** 2
    cond = 1.0 / (1.0 + power / contrast_sq)
    traces = inl * crs
    solved = diffuse(volume.reshape(traces, tms).T, cond.reshape(traces, tms).T)
    along_time = solved.T.reshape(inl, crs, tms)
    columns = crs * tms
    lines = (
        lax.all_to_all(
            volume.reshape(inl, columns), "wide", split_axis=1, concat_axis=0, tiled=True
        ),
        lax.all_to_all(cond.reshape(inl, columns), "wide", split_axis=1, concat_axis=0, tiled=True),
    )
    solved = diffuse(lines[0], lines[1])
    along_inline = lax.all_to_all(solved, "wide", split_axis=0, concat_axis=1, tiled=True).reshape(
        inl, crs, tms
    )
    lines = (
        lax.all_to_all(volume, "narrow", split_axis=2, concat_axis=1, tiled=True),
        lax.all_to_all(cond, "narrow", split_axis=2, concat_axis=1, tiled=True),
    )
    solved = diffuse(jnp.transpose(lines[0], (1, 0, 2)), jnp.transpose(lines[1], (1, 0, 2)))
    along_cross = lax.all_to_all(
        jnp.transpose(solved, (1, 0, 2)), "narrow", split_axis=1, concat_axis=2, tiled=True
    )
    lateral = along_inline + along_cross
    return (lateral + along_time) / 3.0


def solution(mesh):
    placed = (P("wide", "narrow", None),)
    return jax.shard_map(
        per_device, mesh=mesh, in_specs=placed, out_specs=P("wide", "narrow", None), check_vma=False
    )
```

profile of v0, /device:TPU:1, one launch (start us, length us, event | category | flops | bytes accessed | tf_op | source)
XLA Modules:
  0.0 156.7 jit_solution(9909950086737457264)
XLA Ops:
  0.0 0.9 fusion.175
  0.9 4.6 %collective-permute-start = (f32[1,16,1024]{2,1,0:T(8,128)S(1)}, f32[1,16,1024]{2,1,0:T(8,128)S(1)}, u32[]{:S(2)}, u32[]{:S(2)}) collective-permute-start(f32[1,16,1024]{2,1,0:T(8,128)S(1)} %get-tuple-element.81), channel_id=1, source_target_pairs={{0,8},{8,16},{16,24},{24,32},{32,40},{40,48},{48,56},{56,64},{64,7... | collective-permute-start | bytes 196616 | tf_op jit(solution)/shard_map/ppermute | solution.py:17
  5.5 5.6 %collective-permute-start.1 = (f32[1,16,1024]{2,1,0:T(8,128)S(1)}, f32[1,16,1024]{2,1,0:T(8,128)S(1)}, u32[]{:S(2)}, u32[]{:S(2)}) collective-permute-start(f32[1,16,1024]{2,1,0:T(8,128)S(1)} %get-tuple-element.80), channel_id=1, source_target_pairs={{8,0},{16,8},{24,16},{32,24},{40,32},{48,40},{56,48},{64,56},{72,6... | collective-permute-start | bytes 196616 | tf_op jit(solution)/shard_map/ppermute | solution.py:18
  11.1 1.7 %copy.1462 = f32[4,16,1024]{1,0,2:T(4,128)S(1)} copy(f32[4,16,1024]{2,1,0:T(8,128)} %param.1) | data formatting | bytes 524288 | tf_op args[0]
  12.8 2.3 %reshape.948 = f32[8,1,8192]{2,1,0:T(1,128)} reshape(f32[1024,4,16]{2,1,0:T(4,128)S(1)} %bitcast.1584) | data formatting | bytes 524288
  15.1 4.8 %all-to-all-start.3 = ((f32[8,1,8192]{2,1,0:T(1,128)}), f32[8,1,8192]{2,1,0:T(1,128)S(1)}, u32[]{:S(2)}, u32[]{:S(2)}) async-start(f32[8,1,8192]{2,1,0:T(1,128)} %reshape.948), calls=%async_computation.3 | async-start | bytes 524288 | tf_op jit(solution)/shard_map/all_to_all | solution.py:94
  20.1 1.1 fusion.156
  21.4 3.4 %collective-permute-start.2 = (f32[6,1,1024]{2,1,0:T(1,128)S(1)}, f32[6,1,1024]{2,1,0:T(1,128)S(1)}, u32[]{:S(2)}, u32[]{:S(2)}) collective-permute-start(f32[6,1,1024]{2,1,0:T(1,128)S(1)} %get-tuple-element.38), channel_id=1, source_target_pairs={{0,1},{1,2},{2,3},{3,4},{4,5},{5,6},{6,7},{8,9},{9,10},{10,11},{11... | collective-permute-start | bytes 73736 | tf_op jit(solution)/shard_map/ppermute | solution.py:17
  24.7 1.3 collective-permute-start.3
  26.4 0.9 copy.1373
  27.3 2.4 %collective-permute-done.3 = f32[6,1,1024]{2,1,0:T(1,128)S(1)} collective-permute-done((f32[6,1,1024]{2,1,0:T(1,128)S(1)}, f32[6,1,1024]{2,1,0:T(1,128)S(1)}, u32[]{:S(2)}, u32[]{:S(2)}) %collective-permute-start.3) | collective-permute-done | bytes 24608 | tf_op jit(solution)/shard_map/ppermute | solution.py:18
  30.9 1.1 fusion.157
  32.2 0.4 fusion.160
  38.5 18.1 %all-to-all-start = ((f32[4,64,256]{2,0,1:T(4,128)}), f32[4,64,256]{2,0,1:T(4,128)}, u32[]{:S(2)}, u32[]{:S(2)}) async-start(f32[4,64,256]{2,0,1:T(4,128)} %copy.1373), calls=%async_computation | async-start | bytes 524288 | tf_op jit(solution)/shard_map/all_to_all | solution.py:84
  56.6 0.6 divide_bitcast_fusion.3
  57.2 0.8 copy.1466
  58.0 2.3 %reshape.946 = f32[8,1,8192]{2,1,0:T(1,128)} reshape(f32[1024,4,16]{2,1,0:T(4,128)S(1)} %bitcast.1585) | data formatting | bytes 524288
  60.3 0.8 pad_maximum_fusion.20
  61.1 0.8 divide_bitcast_fusion.2
  62.0 8.0 %all-to-all-done = f32[4,64,256]{2,0,1:T(4,128)} async-done(((f32[4,64,256]{2,0,1:T(4,128)}), f32[4,64,256]{2,0,1:T(4,128)}, u32[]{:S(2)}, u32[]{:S(2)}) %all-to-all-start) | async-done | bytes 262176 | tf_op jit(solution)/shard_map/all_to_all | solution.py:84
  70.0 13.6 %all-to-all-start.4 = ((f32[8,1,8192]{2,1,0:T(1,128)}), f32[8,1,8192]{2,1,0:T(1,128)}, u32[]{:S(2)}, u32[]{:S(2)}) async-start(f32[8,1,8192]{2,1,0:T(1,128)} %reshape.946), calls=%async_computation.4 | async-start | bytes 524288 | tf_op jit(solution)/shard_map/all_to_all | solution.py:95
  83.6 1.0 subtract_divide_fusion.2
  84.6 0.9 copy.1375
  85.7 0.7 copy.1654
  86.4 0.6 broadcast.298
  87.0 1.3 reduce.1
  88.3 1.5 reshape.949
  89.8 0.8 copy.1665
  90.6 0.7 slice.1916
  91.3 0.9 fusion.163
  92.2 1.2 reshape.840
  93.4 0.8 slice.1816
  94.2 7.3 %all-to-all-start.1 = ((f32[4,64,256]{2,0,1:T(4,128)}), f32[4,64,256]{2,0,1:T(4,128)}, u32[]{:S(2)}, u32[]{:S(2)}) async-start(f32[4,64,256]{2,0,1:T(4,128)} %copy.1375), calls=%async_computation.1 | async-start | bytes 524288 | tf_op jit(solution)/shard_map/all_to_all | solution.py:87
  101.5 2.3 %reduce = f32[8,8192]{1,0:T(8,128)S(1)} reduce(f32[8,1,8192]{2,1,0:T(1,128)} %all-to-all-done.4, f32[]{:T(128)} %broadcast.298), dimensions={1}, to_apply=%all_to_all.91.reduce_sub_computation | reduce | bytes 524292 | tf_op jit(solution)/shard_map/all_to_all | solution.py:95
  103.7 1.5 reshape.947
  105.2 0.8 copy.1667
  106.5 0.5 fusion.162
  109.8 0.9 copy.1542
  110.7 4.2 %all-to-all-done.1 = f32[4,64,256]{2,0,1:T(4,128)} async-done(((f32[4,64,256]{2,0,1:T(4,128)}), f32[4,64,256]{2,0,1:T(4,128)}, u32[]{:S(2)}, u32[]{:S(2)}) %all-to-all-start.1) | async-done | bytes 262176 | tf_op jit(solution)/shard_map/all_to_all | solution.py:87
  114.9 7.8 %all-to-all-start.5 = ((f32[4,128,128]{2,0,1:T(4,128)}), f32[4,128,128]{2,0,1:T(4,128)S(1)}, u32[]{:S(2)}, u32[]{:S(2)}) async-start(f32[4,128,128]{2,0,1:T(4,128)} %copy.1542), calls=%async_computation.5 | async-start | bytes 524288 | tf_op jit(solution)/shard_map/all_to_all | solution.py:98
  122.7 1.0 all_to_all.83
  124.1 0.4 fusion.166
  124.9 0.4 fusion.169
  130.0 0.9 all_to_all.84
  130.9 1.8 %all-to-all-done.5 = f32[4,128,128]{2,0,1:T(4,128)S(1)} async-done(((f32[4,128,128]{2,0,1:T(4,128)}), f32[4,128,128]{2,0,1:T(4,128)S(1)}, u32[]{:S(2)}, u32[]{:S(2)}) %all-to-all-start.5) | async-done | bytes 262176 | tf_op jit(solution)/shard_map/all_to_all | solution.py:98
  132.8 9.6 %all-to-all-start.2 = ((f32[64,4,256]{2,1,0:T(4,128)}), f32[64,4,256]{2,1,0:T(4,128)S(1)}, u32[]{:S(2)}, u32[]{:S(2)}) async-start(f32[64,4,256]{2,1,0:T(4,128)} %all_to_all.84), calls=%async_computation.2 | async-start | bytes 524288 | tf_op jit(solution)/shard_map/all_to_all | solution.py:90
  143.6 12.3 %all-to-all-done.2 = f32[64,4,256]{2,1,0:T(4,128)S(1)} async-done(((f32[64,4,256]{2,1,0:T(4,128)}), f32[64,4,256]{2,1,0:T(4,128)S(1)}, u32[]{:S(2)}, u32[]{:S(2)}) %all-to-all-start.2) | async-done | bytes 262176 | tf_op jit(solution)/shard_map/all_to_all | solution.py:90
  156.0 0.7 fusion.1
  (458 shorter events, 15.3 us)
Async XLA Ops:
  0.9 20.4 %collective-permute-start = (f32[1,16,1024]{2,1,0:T(8,128)S(1)}, f32[1,16,1024]{2,1,0:T(8,128)S(1)}, u32[]{:S(2)}, u32[]{:S(2)}) collective-permute-start(f32[1,16,1024]{2,1,0:T(8,128)S(1)} %get-tuple-element.81), channel_id=1, source_target_pairs={{0,8},{8,16},{16,24},{24,32},{32,40},{40,48},{48,56},{56,64},{64,7... | collective-permute-start | bytes 196616 | tf_op jit(solution)/shard_map/ppermute | solution.py:17
  5.5 14.4 %copy-start = (f32[4,16,1024]{2,1,0:T(8,128)S(1)}, f32[4,16,1024]{2,1,0:T(8,128)}, u32[]{:S(2)}) copy-start(f32[4,16,1024]{2,1,0:T(8,128)} %param.1) | copy-start | bytes 786436
  5.5 15.8 %collective-permute-start.1 = (f32[1,16,1024]{2,1,0:T(8,128)S(1)}, f32[1,16,1024]{2,1,0:T(8,128)S(1)}, u32[]{:S(2)}, u32[]{:S(2)}) collective-permute-start(f32[1,16,1024]{2,1,0:T(8,128)S(1)} %get-tuple-element.80), channel_id=1, source_target_pairs={{8,0},{16,8},{24,16},{32,24},{40,32},{48,40},{56,48},{64,56},{72,6... | collective-permute-start | bytes 196616 | tf_op jit(solution)/shard_map/ppermute | solution.py:18
  15.1 23.3 %all-to-all-start.3 = ((f32[8,1,8192]{2,1,0:T(1,128)}), f32[8,1,8192]{2,1,0:T(1,128)S(1)}, u32[]{:S(2)}, u32[]{:S(2)}) async-start(f32[8,1,8192]{2,1,0:T(1,128)} %reshape.948), calls=%async_computation.3 | async-start | bytes 524288 | tf_op jit(solution)/shard_map/all_to_all | solution.py:94
  21.4 5.9 %collective-permute-start.2 = (f32[6,1,1024]{2,1,0:T(1,128)S(1)}, f32[6,1,1024]{2,1,0:T(1,128)S(1)}, u32[]{:S(2)}, u32[]{:S(2)}) collective-permute-start(f32[6,1,1024]{2,1,0:T(1,128)S(1)} %get-tuple-element.38), channel_id=1, source_target_pairs={{0,1},{1,2},{2,3},{3,4},{4,5},{5,6},{6,7},{8,9},{9,10},{10,11},{11... | collective-permute-start | bytes 73736 | tf_op jit(solution)/shard_map/ppermute | solution.py:17
  24.7 4.9 %collective-permute-start.3 = (f32[6,1,1024]{2,1,0:T(1,128)S(1)}, f32[6,1,1024]{2,1,0:T(1,128)S(1)}, u32[]{:S(2)}, u32[]{:S(2)}) collective-permute-start(f32[6,1,1024]{2,1,0:T(1,128)S(1)} %get-tuple-element.39), channel_id=1, source_target_pairs={{1,0},{2,1},{3,2},{4,3},{5,4},{6,5},{7,6},{9,8},{10,9},{11,10},{12... | collective-permute-start | bytes 73736 | tf_op jit(solution)/shard_map/ppermute | solution.py:18
  32.9 1.0 copy-start.11
  33.0 1.0 copy-start.12
  34.4 1.2 copy-start.4
  35.0 0.7 copy-start.6
  35.4 0.8 copy-start.9
  35.8 1.2 copy-start.16
  36.0 1.1 copy-start.13
  36.2 0.9 copy-start.17
  36.4 1.1 copy-start.18
  36.6 1.8 %copy-start.23 = (f32[64,1,64]{2,1,0:T(1,128)}, f32[64,1,64]{2,1,0:T(1,128)S(1)}, u32[]{:S(2)}) copy-start(f32[64,1,64]{2,1,0:T(1,128)S(1)} %get-tuple-element.144) | copy-start | bytes 49156
  36.7 1.7 %copy-start.20 = (f32[64,1,64]{2,1,0:T(1,128)}, f32[64,1,64]{2,1,0:T(1,128)S(1)}, u32[]{:S(2)}) copy-start(f32[64,1,64]{2,1,0:T(1,128)S(1)} %get-tuple-element.146) | copy-start | bytes 49156
  36.8 19.7 %copy-start.24 = (f32[64,1,64]{2,1,0:T(1,128)}, f32[64,1,64]{2,1,0:T(1,128)S(1)}, u32[]{:S(2)}) copy-start(f32[64,1,64]{2,1,0:T(1,128)S(1)} %get-tuple-element.141) | copy-start | bytes 49156
  37.0 19.6 %copy-start.25 = (f32[64,1,64]{2,1,0:T(1,128)}, f32[64,1,64]{2,1,0:T(1,128)S(1)}, u32[]{:S(2)}) copy-start(f32[64,1,64]{2,1,0:T(1,128)S(1)} %get-tuple-element.148) | copy-start | bytes 49156
  38.4 18.1 %copy-start.14 = (f32[8,1,8192]{2,1,0:T(1,128)}, f32[8,1,8192]{2,1,0:T(1,128)S(1)}, u32[]{:S(2)}) copy-start(f32[8,1,8192]{2,1,0:T(1,128)S(1)} %all-to-all-done.3) | copy-start | bytes 786436
  38.5 31.5 %all-to-all-start = ((f32[4,64,256]{2,0,1:T(4,128)}), f32[4,64,256]{2,0,1:T(4,128)}, u32[]{:S(2)}, u32[]{:S(2)}) async-start(f32[4,64,256]{2,0,1:T(4,128)} %copy.1373), calls=%async_computation | async-start | bytes 524288 | tf_op jit(solution)/shard_map/all_to_all | solution.py:84
  60.3 26.7 %copy-start.15 = (f32[8,1,8192]{2,1,0:T(1,128)S(1)}, f32[8,1,8192]{2,1,0:T(1,128)}, u32[]{:S(2)}) copy-start(f32[8,1,8192]{2,1,0:T(1,128)} %copy-done.14) | copy-start | bytes 786436
  70.0 24.2 %all-to-all-start.4 = ((f32[8,1,8192]{2,1,0:T(1,128)}), f32[8,1,8192]{2,1,0:T(1,128)}, u32[]{:S(2)}, u32[]{:S(2)}) async-start(f32[8,1,8192]{2,1,0:T(1,128)} %reshape.946), calls=%async_computation.4 | async-start | bytes 524288 | tf_op jit(solution)/shard_map/all_to_all | solution.py:95
  93.4 8.1 %copy-start.2 = (f32[128,2,256]{2,1,0:T(2,128)}, f32[128,2,256]{2,1,0:T(2,128)S(1)}, u32[]{:S(2)}) copy-start(f32[128,2,256]{2,1,0:T(2,128)S(1)} %reshape.840) | copy-start | bytes 786436
  94.2 20.7 %all-to-all-start.1 = ((f32[4,64,256]{2,0,1:T(4,128)}), f32[4,64,256]{2,0,1:T(4,128)}, u32[]{:S(2)}, u32[]{:S(2)}) async-start(f32[4,64,256]{2,0,1:T(4,128)} %copy.1375), calls=%async_computation.1 | async-start | bytes 524288 | tf_op jit(solution)/shard_map/all_to_all | solution.py:87
  106.0 1.1 copy-start.22
  106.0 1.2 copy-start.8
  106.1 1.2 copy-start.19
  109.8 14.3 %copy-start.3 = (f32[128,2,256]{2,1,0:T(2,128)S(1)}, f32[128,2,256]{2,1,0:T(2,128)}, u32[]{:S(2)}) copy-start(f32[128,2,256]{2,1,0:T(2,128)} %copy-done.2) | copy-start | bytes 786436
  114.9 17.9 %all-to-all-start.5 = ((f32[4,128,128]{2,0,1:T(4,128)}), f32[4,128,128]{2,0,1:T(4,128)S(1)}, u32[]{:S(2)}, u32[]{:S(2)}) async-start(f32[4,128,128]{2,0,1:T(4,128)} %copy.1542), calls=%async_computation.5 | async-start | bytes 524288 | tf_op jit(solution)/shard_map/all_to_all | solution.py:98
  124.1 1.4 copy-start.21
  129.3 13.0 %copy-start.1 = (f32[128,2,64]{2,1,0:T(2,128)S(1)}, f32[128,2,64]{2,1,0:T(2,128)}, u32[]{:S(2)}) copy-start(f32[128,2,64]{2,1,0:T(2,128)} %copy.1654) | copy-start | bytes 196612
  129.3 13.0 %copy-start.5 = (f32[256,1,64]{2,1,0:T(1,128)S(1)}, f32[256,1,64]{2,1,0:T(1,128)}, u32[]{:S(2)}) copy-start(f32[256,1,64]{2,1,0:T(1,128)} %copy-done.4) | copy-start | bytes 196612
  129.3 13.0 %copy-start.7 = (f32[256,1,64]{2,1,0:T(1,128)S(1)}, f32[256,1,64]{2,1,0:T(1,128)}, u32[]{:S(2)}) copy-start(f32[256,1,64]{2,1,0:T(1,128)} %copy-done.6) | copy-start | bytes 196612
  129.3 13.0 %copy-start.10 = (f32[256,1,64]{2,1,0:T(1,128)S(1)}, f32[256,1,64]{2,1,0:T(1,128)}, u32[]{:S(2)}) copy-start(f32[256,1,64]{2,1,0:T(1,128)} %copy-done.9) | copy-start | bytes 196612
  132.8 23.1 %all-to-all-start.2 = ((f32[64,4,256]{2,1,0:T(4,128)}), f32[64,4,256]{2,1,0:T(4,128)S(1)}, u32[]{:S(2)}, u32[]{:S(2)}) async-start(f32[64,4,256]{2,1,0:T(4,128)} %all_to_all.84), calls=%async_computation.2 | async-start | bytes 524288 | tf_op jit(solution)/shard_map/all_to_all | solution.py:90
where the time goes:
time: 158 us; the launch traced here: 157 us
  starting transfers between devices  76 us (48%)
  local copies, waits for them, and re-layouts  37.5 us (24%)
  waiting for transfers between devices  28.7 us (18%)
  other arithmetic  11.2 us (7%)
  between operations  3.48 us (2%)
    all_to_all x1, starting transfers between devices, per_device(): lax.all_to_all(volume.reshape(inl, columns), 'wide', split_axis=1, concat...  18.1 us
    all_to_all x1, starting transfers between devices, per_device(): lax.all_to_all(cond, 'narrow', split_axis=2, concat_axis=1, tiled=True)  13.6 us
    all_to_all x1, waiting for transfers between devices, per_device(): lax.all_to_all(solved, 'wide', split_axis=0, concat_axis=1, tiled=True)  12.3 us
    unnamed x116, local copies, waits for them, and re-layouts  10.2 us
    all_to_all x1, starting transfers between devices, per_device(): lax.all_to_all(solved, 'wide', split_axis=0, concat_axis=1, tiled=True)  9.56 us
    slice x69, local copies, waits for them, and re-layouts, halves(): return (paired[:, 0], paired[:, 1])  8.12 us
    all_to_all x1, waiting for transfers between devices, per_device(): lax.all_to_all(volume.reshape(inl, columns), 'wide', split_axis=1, concat...  7.98 us
    ppermute x2, starting transfers between devices, with_halo(): before = lax.ppermute(last, axis, up)  7.96 us
  transfers between devices with their start and end apart: 10, of which 5 were waited for; matrix products, arithmetic and copies ran while one was open for 28% of the time, Pallas kernels for 0%

commit v1 on v0

v1 whole, which is shorter than its diff:
```python
import jax
import jax.numpy as jnp
from jax import lax
from jax.experimental import pallas as pl
from jax.experimental.pallas import tpu as pltpu
from jax.sharding import PartitionSpec as P

half_weight = 150.0
contrast_sq = 9.0

WIDE = 64
NARROW = 8
INL = 4
CRS = 16
NT = 1024
LANES = 128
TILES = NT // LANES
ROWS = INL * TILES
GROUP = 8
PORTS = 7


def condense(mass, rhs, link):
    mass, rhs, right = list(mass), list(rhs), list(link)
    alive, steps = list(range(len(mass))), []
    while len(alive) > 2:
        gone = set()
        for at in range(1, len(alive) - 1, 2):
            l, k, r = alive[at - 1 : at + 2]
            inverse = 1.0 / (right[l] + right[k] + mass[k])
            to_left, to_right = right[l] * inverse, right[k] * inverse
            mass[l] = mass[l] + to_left * mass[k]
            rhs[l] = rhs[l] + to_left * rhs[k]
            mass[r] = mass[r] + to_right * mass[k]
            rhs[r] = rhs[r] + to_right * rhs[k]
            right[l] = to_left * right[k]
            steps.append((l, k, r, to_left, to_right, rhs[k] * inverse))
            gone.add(k)
        alive = [k for k in alive if k not in gone]
    return mass[0], rhs[0], mass[-1], rhs[-1], right[0], steps


def expand(first, last, steps, count):
    x = [None] * count
    x[0], x[-1] = first, last
    for l, k, r, to_left, to_right, base in reversed(steps):
        x[k] = base + to_left * x[l] + to_right * x[r]
    return x


def links(cond):
    return [half_weight * (a + b) for a, b in zip(cond[:-1], cond[1:])]


def halving(mass, rhs, before, after, shift, count):
    step = 1
    while step < count:
        inverse = 1.0 / (before + after + mass)
        to_left, to_right = before * inverse, after * inverse
        across = to_left * after
        mass, rhs = (
            mass + shift(to_right * mass, step) + shift(to_left * mass, -step),
            rhs + shift(to_right * rhs, step) + shift(to_left * rhs, -step),
        )
        before, after = shift(across, step), shift(across, -step)
        step *= 2
    return rhs / mass


def iota(shape, dim):
    return lax.broadcasted_iota(jnp.int32, shape, dim)


def lane_tile(t):
    return slice(t * LANES, (t + 1) * LANES)


def prepare_kernel(
    axes, vol, before, after, left, right, cond, wide_out, narrow_out, cells_v, cells_c
):
    wide_axes, narrow_axes = axes
    wide_rank, narrow_rank = lax.axis_index(wide_axes), lax.axis_index(narrow_axes)
    col = iota((CRS, NT), 1)
    row = iota((CRS, NT), 0)
    for i in range(INL):
        here = vol[i]
        if i == 0:
            up = jnp.where(wide_rank == 0, here, before[0])
        else:
            up = vol[i - 1]
        if i == INL - 1:
            down = jnp.where(wide_rank == WIDE - 1, here, after[0])
        else:
            down = vol[i + 1]
        power = (0.5 * (down - up)) ** 2
        edge = jnp.where(narrow_rank == 0, here[:1], left[i])
        lower = jnp.where(row == 0, edge, pltpu.roll(here, 1, 0))
        edge = jnp.where(narrow_rank == NARROW - 1, here[CRS - 1 :], right[i])
        upper = jnp.where(row == CRS - 1, edge, pltpu.roll(here, CRS - 1, 0))
        power = power + (0.5 * (upper - lower)) ** 2
        earlier = jnp.where(col == 0, here, pltpu.roll(here, 1, 1))
        later = jnp.where(col == NT - 1, here, pltpu.roll(here, NT - 1, 1))
        power = power + (0.5 * (later - earlier)) ** 2
        value = contrast_sq / (contrast_sq + power)
        cond[i] = value
        for t in range(TILES):
            where = pl.ds(i * TILES + t, CRS, stride=ROWS)
            cells_v[where, :] = here[:, lane_tile(t)]
            cells_c[where, :] = value[:, lane_tile(t)]
    ones = jnp.ones((ROWS, LANES), jnp.float32)
    v = [cells_v[pl.ds(c * ROWS, ROWS), :] for c in range(CRS)]
    k = [cells_c[pl.ds(c * ROWS, ROWS), :] for c in range(CRS)]
    m0, d0, m1, d1, g, _ = condense([ones] * CRS, v, links(k))
    for p, value in enumerate((g, m0, m1, d0, d1, k[0], k[-1])):
        narrow_out[p * ROWS : (p + 1) * ROWS, :] = value
    ones = jnp.ones((GROUP, LANES), jnp.float32)
    for t in range(TILES):
        for u in range(CRS // GROUP):
            at = (slice(u * GROUP, (u + 1) * GROUP), lane_tile(t))
            v = [vol[(i, *at)] for i in range(INL)]
            k = [cond[(i, *at)] for i in range(INL)]
            m0, d0, m1, d1, g, _ = condense([ones] * INL, v, links(k))
            for p, value in enumerate((g, m0, m1, d0, d1, k[0], k[-1])):
                start = t * GROUP * 2 * PORTS + p * 2 + u
                wide_out[pl.ds(start, GROUP, stride=2 * PORTS), :] = value


def sublane_shift(x, s):
    return pltpu.roll(x, s % GROUP, 0)


def wide_kernel(ports, out):
    part = WIDE // GROUP
    sub = iota((GROUP, LANES), 0)
    zero = jnp.zeros((GROUP, LANES), jnp.float32)
    for u in range(2):

        def port(p, j):
            return ports[pl.ds(j * 2 * PORTS + p * 2 + u, GROUP, stride=part * 2 * PORTS), :]

        last_cond = sublane_shift(port(6, part - 1), 1)
        mass, rhs, link = [zero], [zero], []
        for j in range(part):
            joined = half_weight * (last_cond + port(5, j))
            if j == 0:
                joined = jnp.where(sub == 0, 0.0, joined)
            link += [joined, port(0, j)]
            mass += [port(1, j), port(2, j)]
            rhs += [port(3, j), port(4, j)]
            last_cond = port(6, j)
        count = len(mass)
        m0, d0, m1, d1, g, steps = condense(mass, rhs, link)
        last = halving(
            m1 + sublane_shift(m0, -1),
            d1 + sublane_shift(d0, -1),
            g,
            sublane_shift(g, -1),
            sublane_shift,
            GROUP,
        )
        x = expand(sublane_shift(last, 1), last, steps, count)
        for j in range(part):
            for e in range(2):
                out[pl.ds(j * 4 + e * 2 + u, GROUP, stride=part * 4), :] = x[1 + 2 * j + e]


def time_kernel(vol, cond, out, cells_v, cells_c, link_s, tmp):
    lines = INL * CRS
    half = NT // 2
    blocks = half // LANES
    for b in range(blocks):
        for source, cells in ((vol, cells_v), (cond, cells_c)):
            stacked = jnp.concatenate(
                [
                    source[:, :, b * LANES : (b + 1) * LANES].reshape(lines, LANES),
                    source[:, :, half + b * LANES : half + (b + 1) * LANES].reshape(lines, LANES),
                ],
                0,
            )
            cells[b * LANES : (b + 1) * LANES, :] = stacked.T
    lane = iota((GROUP, LANES), 1)
    sub = iota((GROUP, LANES), 0)
    low = lane < lines

    def swap(x):
        return pltpu.roll(x, lines, 1)

    for s in range(half // GROUP):
        here = cells_c[s * GROUP : (s + 1) * GROUP, :]
        if s:
            edge = cells_c[s * GROUP - 1 : s * GROUP, :]
        else:
            edge = swap(cells_c[half - GROUP : half, :])[GROUP - 1 :]
        value = half_weight * (here + jnp.where(sub == 0, edge, pltpu.roll(here, 1, 0)))
        if s == 0:
            value = jnp.where((sub == 0) & low, 0.0, value)
        link_s[s * GROUP : (s + 1) * GROUP, :] = value

    def chain_shift(x, s):
        n = x.shape[0]
        if abs(s) == n:
            return swap(x)
        rolled = pltpu.roll(x, s % n, 0)
        place = iota(x.shape, 0)
        wrapped = place < s if s > 0 else place >= n + s
        return jnp.where(wrapped, swap(rolled), rolled)

    runs = half // GROUP
    zero = jnp.zeros((runs, LANES), jnp.float32)
    ones = jnp.ones((runs, LANES), jnp.float32)
    v = [cells_v[pl.ds(k, runs, stride=GROUP), :] for k in range(GROUP)]
    link = [link_s[pl.ds(k, runs, stride=GROUP), :] for k in range(GROUP)]
    m0, d0, m1, d1, g, steps = condense([zero] + [ones] * GROUP, [zero] + v, link)
    tmp[0] = m1 + chain_shift(m0, -1)
    tmp[1] = d1 + chain_shift(d0, -1)
    tmp[2] = g
    zero = jnp.zeros((GROUP, LANES), jnp.float32)

    def take(p):
        return [tmp[p, pl.ds(k, GROUP, stride=GROUP), :] for k in range(GROUP)]

    m0, d0, m1, d1, g, inner = condense([zero] + take(0), [zero] + take(1), take(2))
    last = halving(
        m1 + chain_shift(m0, -1),
        d1 + chain_shift(d0, -1),
        g,
        chain_shift(g, -1),
        chain_shift,
        2 * GROUP,
    )
    x = expand(chain_shift(last, 1), last, inner, GROUP + 1)
    for k in range(GROUP):
        tmp[0, pl.ds(k, GROUP, stride=GROUP), :] = x[k + 1]
    last = tmp[0]
    x = expand(chain_shift(last, 1), last, steps, GROUP + 1)
    for k in range(GROUP):
        cells_v[pl.ds(k, runs, stride=GROUP), :] = x[k + 1]
    for b in range(blocks):
        turned = cells_v[b * LANES : (b + 1) * LANES, :].T
        for h in range(2):
            out[:, :, h * half + b * LANES : h * half + (b + 1) * LANES] = turned[
                h * lines : (h + 1) * lines
            ].reshape(INL, CRS, LANES)


def cross_kernel(axes, gathered, cells_v, cells_c, timed, out, ends, cells_x):
    rank = lax.axis_index(axes[1])
    ports = [
        [gathered[n, p * ROWS : (p + 1) * ROWS, :] for p in range(PORTS)] for n in range(NARROW)
    ]
    mass, rhs, link = [], [], []
    for n, (g, m0, m1, d0, d1, _, _) in enumerate(ports):
        mass += [m0, m1]
        rhs += [d0, d1]
        link.append(g)
        if n < NARROW - 1:
            link.append(half_weight * (ports[n][6] + ports[n + 1][5]))
    m0, d0, m1, d1, g, steps = condense(mass, rhs, link)
    inverse = 1.0 / (m0 * m1 + g * (m0 + m1))
    first = (d0 * (m1 + g) + g * d1) * inverse
    last = (d1 * (m0 + g) + g * d0) * inverse
    for n, value in enumerate(expand(first, last, steps, 2 * NARROW)):
        ends[n] = value
    v = [cells_v[pl.ds(c * ROWS, ROWS), :] for c in range(CRS)]
    k = [cells_c[pl.ds(c * ROWS, ROWS), :] for c in range(CRS)]
    ones = jnp.ones((ROWS, LANES), jnp.float32)
    _, _, _, _, _, steps = condense([ones] * CRS, v, links(k))
    x = expand(ends[2 * rank], ends[2 * rank + 1], steps, CRS)
    for c in range(CRS):
        cells_x[c * ROWS : (c + 1) * ROWS, :] = x[c]
    for i in range(INL):
        for t in range(TILES):
            out[i, :, lane_tile(t)] = (
                timed[i, :, lane_tile(t)] + cells_x[pl.ds(i * TILES + t, CRS, stride=ROWS), :]
            )


def finish_kernel(vol, cond, ends, others, out):
    ones = jnp.ones((GROUP, LANES), jnp.float32)
    for t in range(TILES):
        for u in range(CRS // GROUP):
            at = (slice(u * GROUP, (u + 1) * GROUP), lane_tile(t))
            v = [vol[(i, *at)] for i in range(INL)]
            k = [cond[(i, *at)] for i in range(INL)]
            steps = condense([ones] * INL, v, links(k))[-1]
            first = ends[pl.ds(t * GROUP * 4 + u, GROUP, stride=4), :]
            last = ends[pl.ds(t * GROUP * 4 + 2 + u, GROUP, stride=4), :]
            for i, x in enumerate(expand(first, last, steps, INL)):
                out[(i, *at)] = (x + others[(i, *at)]) * (1.0 / 3.0)


def f32(*shape):
    return jax.ShapeDtypeStruct(shape, jnp.float32)


def call(kernel, out, *args, scratch=()):
    return pl.pallas_call(
        kernel,
        out_shape=out,
        scratch_shapes=[pltpu.VMEM(s, jnp.float32) for s in scratch],
        compiler_params=pltpu.CompilerParams(vmem_limit_bytes=16 * 2**20),
    )(*args)


def per_device(axes, volume):
    wide_axes, narrow_axes = axes

    def neighbour(x, axis, count, step):
        pairs = [(i, i + step) for i in range(count) if 0 <= i + step < count]
        return lax.ppermute(x, axis, pairs)

    before = neighbour(volume[-1:], wide_axes, WIDE, 1)
    after = neighbour(volume[:1], wide_axes, WIDE, -1)
    left = neighbour(volume[:, -1:], narrow_axes, NARROW, 1)
    right = neighbour(volume[:, :1], narrow_axes, NARROW, -1)
    cells = CRS * ROWS
    cond, wide_ports, narrow_ports, cells_v, cells_c = call(
        lambda *refs: prepare_kernel(axes, *refs),
        (
            f32(INL, CRS, NT),
            f32(WIDE * PORTS * 2, LANES),
            f32(PORTS * ROWS, LANES),
            f32(cells, LANES),
            f32(cells, LANES),
        ),
        volume,
        before,
        after,
        left,
        right,
    )
    lines = lax.all_to_all(
        wide_ports.reshape(WIDE, PORTS, 2, LANES), wide_axes, split_axis=0, concat_axis=0, tiled=True
    )
    spread = jnp.broadcast_to(narrow_ports[None], (NARROW, PORTS * ROWS, LANES))
    gathered = lax.all_to_all(spread, narrow_axes, split_axis=0, concat_axis=0, tiled=True)
    timed = call(
        time_kernel,
        f32(INL, CRS, NT),
        volume,
        cond,
        scratch=(
            (NT // 2, LANES),
            (NT // 2, LANES),
            (NT // 2, LANES),
            (3, NT // 2 // GROUP, LANES),
        ),
    )
    solved = call(
        wide_kernel, f32(WIDE * 4, LANES), lines.reshape(WIDE * PORTS * 2, LANES)
    )
    ends = lax.all_to_all(
        solved.reshape(WIDE, 2, 2, LANES), wide_axes, split_axis=0, concat_axis=0, tiled=True
    )
    others = call(
        lambda *refs: cross_kernel(axes, *refs),
        f32(INL, CRS, NT),
        gathered,
        cells_v,
        cells_c,
        timed,
        scratch=((2 * NARROW, ROWS, LANES), (cells, LANES)),
    )
    return call(
        finish_kernel, f32(INL, CRS, NT), volume, cond, ends.reshape(WIDE * 4, LANES), others
    )


def solution(mesh):
    axes = ("wide", "narrow")
    return jax.shard_map(
        lambda volume: per_device(axes, volume),
        mesh=mesh,
        in_specs=(P("wide", "narrow", None),),
        out_specs=P("wide", "narrow", None),
        check_vma=False,
    )
```

time: 158 us -> 108 us (0.68)
  starting transfers between devices: 76 us -> 34.6 us
  local copies, waits for them, and re-layouts: 37.5 us -> 1.94 us
  blocking collectives: 0 us -> 31.9 us
  other arithmetic: 11.2 us -> 0 us
  waiting for transfers between devices: 28.7 us -> 34.6 us
  Pallas kernels: 0 us -> 4.1 us
  between operations: 3.48 us -> 0.09 us
    all_to_all x6 -> x2, starting transfers between devices: 61.1 us -> 21.9 us  [the longest x1 14 us: per_device(): lax.all_to_all(spread, narrow_axes, split_axis=0, concat_axis=0, tiled=True)]
    all_to_all x0 -> x1, blocking collectives: none -> 31.9 us  [per_device(): lax.all_to_all(wide_ports.reshape(WIDE, PORTS, 2, LANES), wide_axes, spli...]
    slice x172 -> x2, local copies, waits for them, and re-layouts: 13.6 us -> 0.95 us  [the longest x1 0.92 us: per_device(): after = neighbour(volume[:1], wide_axes, WIDE, -1)]
    unnamed x116 -> x2, local copies, waits for them, and re-layouts: 10.2 us -> 0.01 us
    all_to_all x11 -> x0, local copies, waits for them, and re-layouts: 6.02 us -> none  [the longest x3 1.99 us: per_device(): lax.all_to_all(cond.reshape(inl, columns), 'wide', split_axis=1, concat_a...]
    all_to_all x6 -> x2, waiting for transfers between devices: 26.3 us -> 31.3 us  [the longest x1 22 us: per_device(): lax.all_to_all(spread, narrow_axes, split_axis=0, concat_axis=0, tiled=True)]
    pallas_call x0 -> x5, Pallas kernels: none -> 4.1 us  [call(): pl.pallas_call(kernel, out_shape=out, scratch_shapes=[pltpu.VMEM(s, jnp.f...]
    all_to_all x2 -> x0, other arithmetic: 3.54 us -> none  [the longest x1 2.25 us: per_device(): lax.all_to_all(cond, 'narrow', split_axis=2, concat_axis=1, tiled=True)]
  transfers between devices with their start and end apart: 10 -> 6, of which waited for: 5 -> 3; matrix products, arithmetic and copies ran while one was open for 28% -> 0% of each run, Pallas kernels for 0% -> 2%
where the time goes in v1:
time: 108 us; the launch traced here: 107 us
  starting transfers between devices  34.6 us (32%)
  waiting for transfers between devices  34.6 us (32%)
  blocking collectives  31.9 us (30%)
  Pallas kernels  4.1 us (4%)
  local copies, waits for them, and re-layouts  1.94 us (2%)
    all_to_all x1, blocking collectives, per_device(): lax.all_to_all(wide_ports.reshape(WIDE, PORTS, 2, LANES), wide_axes, spli...  31.9 us
    all_to_all x1, waiting for transfers between devices, per_device(): lax.all_to_all(spread, narrow_axes, split_axis=0, concat_axis=0, tiled=True)  22 us
    all_to_all x1, starting transfers between devices, per_device(): lax.all_to_all(spread, narrow_axes, split_axis=0, concat_axis=0, tiled=True)  14 us
    ppermute x4, starting transfers between devices, neighbour(): return lax.ppermute(x, axis, pairs)  12.7 us
    all_to_all x1, waiting for transfers between devices, per_device(): lax.all_to_all(solved.reshape(WIDE, 2, 2, LANES), wide_axes, split_axis=0...  9.22 us
    all_to_all x1, starting transfers between devices, per_device(): lax.all_to_all(solved.reshape(WIDE, 2, 2, LANES), wide_axes, split_axis=0...  7.9 us
    pallas_call x5, Pallas kernels, call(): pl.pallas_call(kernel, out_shape=out, scratch_shapes=[pltpu.VMEM(s, jnp.f...  4.1 us
    ppermute x4, waiting for transfers between devices, neighbour(): return lax.ppermute(x, axis, pairs)  3.34 us
  transfers between devices with their start and end apart: 6, of which 3 were waited for; matrix products, arithmetic and copies ran while one was open for 0% of the time, Pallas kernels for 2%

profile of v1, /device:TPU:1, one launch (start us, length us, event | category | flops | bytes accessed | tf_op | source)
XLA Modules:
  0.0 107.2 jit_solution(7185671529503461261)
XLA Ops:
  0.0 0.0 copy-start
  0.0 0.9 fusion.1
  0.9 4.6 %collective-permute-start = (f32[1,16,1024]{2,1,0:T(8,128)S(1)}, f32[1,16,1024]{2,1,0:T(8,128)S(1)}, u32[]{:S(2)}, u32[]{:S(2)}) collective-permute-start(f32[1,16,1024]{2,1,0:T(8,128)S(1)} %get-tuple-element.18), channel_id=1, source_target_pairs={{0,8},{8,16},{16,24},{24,32},{32,40},{40,48},{48,56},{56,64},{64,7... | collective-permute-start | bytes 196616 | tf_op jit(solution)/shard_map/ppermute | solution.py:310
  5.5 5.5 %collective-permute-start.1 = (f32[1,16,1024]{2,1,0:T(8,128)S(1)}, f32[1,16,1024]{2,1,0:T(8,128)S(1)}, u32[]{:S(2)}, u32[]{:S(2)}) collective-permute-start(f32[1,16,1024]{2,1,0:T(8,128)S(1)} %get-tuple-element.17), channel_id=1, source_target_pairs={{8,0},{16,8},{24,16},{32,24},{40,32},{48,40},{56,48},{64,56},{72,6... | collective-permute-start | bytes 196616 | tf_op jit(solution)/shard_map/ppermute | solution.py:310
  11.0 0.0 copy-done
  11.1 1.3 %collective-permute-start.2 = (f32[4,1,1024]{2,1,0:T(1,128)S(1)}, f32[4,1,1024]{2,1,0:T(1,128)S(1)}, u32[]{:S(2)}, u32[]{:S(2)}) collective-permute-start(f32[4,1,1024]{2,1,0:T(1,128)S(1)} %get-tuple-element.16), channel_id=1, source_target_pairs={{0,1},{1,2},{2,3},{3,4},{4,5},{5,6},{6,7},{8,9},{9,10},{10,11},{11... | collective-permute-start | bytes 49160 | tf_op jit(solution)/shard_map/ppermute | solution.py:310
  12.4 1.3 %collective-permute-start.3 = (f32[4,1,1024]{2,1,0:T(1,128)S(1)}, f32[4,1,1024]{2,1,0:T(1,128)S(1)}, u32[]{:S(2)}, u32[]{:S(2)}) collective-permute-start(f32[4,1,1024]{2,1,0:T(1,128)S(1)} %get-tuple-element.15), channel_id=1, source_target_pairs={{1,0},{2,1},{3,2},{4,3},{5,4},{6,5},{7,6},{9,8},{10,9},{11,10},{12... | collective-permute-start | bytes 49160 | tf_op jit(solution)/shard_map/ppermute | solution.py:310
  13.7 0.0 collective-permute-done.2.refs_3_
  13.7 3.3 %collective-permute-done.3.refs_4_ = f32[4,1,1024]{2,1,0:T(1,128)S(1)} collective-permute-done((f32[4,1,1024]{2,1,0:T(1,128)S(1)}, f32[4,1,1024]{2,1,0:T(1,128)S(1)}, u32[]{:S(2)}, u32[]{:S(2)}) %collective-permute-start.3) | collective-permute-done | bytes 16416 | tf_op jit(solution)/shard_map/ppermute | solution.py:310
  17.0 0.0 collective-permute-done.refs_1_
  17.0 0.0 collective-permute-done.1.refs_2_
  17.0 0.8 shard_map.17
  17.8 31.9 %all_to_all.15 = f32[64,7,2,128]{3,2,1,0:T(2,128)S(1)} all-to-all(f32[64,7,2,128]{3,2,1,0:T(2,128)S(1)} %bitcast.6), channel_id=1, replica_groups=mesh['wide'=64,'narrow'=8] {'wide'}, dimensions={0} | all-to-all | bytes 917504 | tf_op jit(solution)/shard_map/all_to_all | solution.py:332
  49.7 1.0 broadcast_in_dim.2
  50.7 14.0 %all-to-all-start.2 = ((f32[8,224,128]{2,1,0:T(8,128)}), f32[8,224,128]{2,1,0:T(8,128)S(1)}, u32[]{:S(2)}, u32[]{:S(2)}) async-start(f32[8,224,128]{2,1,0:T(8,128)} %broadcast_in_dim.2), calls=%async_computation.2 | async-start | bytes 1835008 | tf_op jit(solution)/shard_map/all_to_all | solution.py:336
  64.7 0.9 shard_map.18
  65.6 22.0 %all-to-all-done.2.refs_0_ = f32[8,224,128]{2,1,0:T(8,128)S(1)} async-done(((f32[8,224,128]{2,1,0:T(8,128)}), f32[8,224,128]{2,1,0:T(8,128)S(1)}, u32[]{:S(2)}, u32[]{:S(2)}) %all-to-all-start.2) | async-done | bytes 917536 | tf_op jit(solution)/shard_map/all_to_all | solution.py:336
  87.7 7.9 %all-to-all-start.1 = ((f32[64,2,2,128]{3,2,1,0:T(2,128)}), f32[64,2,2,128]{3,2,1,0:T(2,128)S(1)}, u32[]{:S(2)}, u32[]{:S(2)}) async-start(f32[64,2,2,128]{3,2,1,0:T(2,128)} %bitcast.2), calls=%async_computation.1 | async-start | bytes 262144 | tf_op jit(solution)/shard_map/all_to_all | solution.py:352
  95.6 1.1 %shard_map.19.refs_3_ = f32[4,16,1024]{2,1,0:T(8,128)S(1)} custom-call(f32[4,16,1024]{2,1,0:T(8,128)S(1)} %copy-done, f32[4,16,1024]{2,1,0:T(8,128)S(1)} %get-tuple-element.10.cond), custom_call_target="tpu_custom_call" | custom-call | tf_op jit(solution)/shard_map/pallas_call | solution.py:297
  96.7 0.5 shard_map.20.others
  97.2 9.2 %all-to-all-done.1 = f32[64,2,2,128]{3,2,1,0:T(2,128)S(1)} async-done(((f32[64,2,2,128]{3,2,1,0:T(2,128)}), f32[64,2,2,128]{3,2,1,0:T(2,128)S(1)}, u32[]{:S(2)}, u32[]{:S(2)}) %all-to-all-start.1) | async-done | bytes 131104 | tf_op jit(solution)/shard_map/all_to_all | solution.py:352
  106.4 0.8 shard_map.21
  (1 shorter events, 0.0 us)
Async XLA Ops:
  0.0 11.0 %copy-start = (f32[4,16,1024]{2,1,0:T(8,128)S(1)}, f32[4,16,1024]{2,1,0:T(8,128)}, u32[]{:S(2)}) copy-start(f32[4,16,1024]{2,1,0:T(8,128)} %vol.3) | copy-start | bytes 786436
  0.9 16.1 %collective-permute-start = (f32[1,16,1024]{2,1,0:T(8,128)S(1)}, f32[1,16,1024]{2,1,0:T(8,128)S(1)}, u32[]{:S(2)}, u32[]{:S(2)}) collective-permute-start(f32[1,16,1024]{2,1,0:T(8,128)S(1)} %get-tuple-element.18), channel_id=1, source_target_pairs={{0,8},{8,16},{16,24},{24,32},{32,40},{40,48},{48,56},{56,64},{64,7... | collective-permute-start | bytes 196616 | tf_op jit(solution)/shard_map/ppermute | solution.py:310
  5.5 11.5 %collective-permute-start.1 = (f32[1,16,1024]{2,1,0:T(8,128)S(1)}, f32[1,16,1024]{2,1,0:T(8,128)S(1)}, u32[]{:S(2)}, u32[]{:S(2)}) collective-permute-start(f32[1,16,1024]{2,1,0:T(8,128)S(1)} %get-tuple-element.17), channel_id=1, source_target_pairs={{8,0},{16,8},{24,16},{32,24},{40,32},{48,40},{56,48},{64,56},{72,6... | collective-permute-start | bytes 196616 | tf_op jit(solution)/shard_map/ppermute | solution.py:310
  11.1 2.6 %collective-permute-start.2 = (f32[4,1,1024]{2,1,0:T(1,128)S(1)}, f32[4,1,1024]{2,1,0:T(1,128)S(1)}, u32[]{:S(2)}, u32[]{:S(2)}) collective-permute-start(f32[4,1,1024]{2,1,0:T(1,128)S(1)} %get-tuple-element.16), channel_id=1, source_target_pairs={{0,1},{1,2},{2,3},{3,4},{4,5},{5,6},{6,7},{8,9},{9,10},{10,11},{11... | collective-permute-start | bytes 49160 | tf_op jit(solution)/shard_map/ppermute | solution.py:310
  12.4 4.6 %collective-permute-start.3 = (f32[4,1,1024]{2,1,0:T(1,128)S(1)}, f32[4,1,1024]{2,1,0:T(1,128)S(1)}, u32[]{:S(2)}, u32[]{:S(2)}) collective-permute-start(f32[4,1,1024]{2,1,0:T(1,128)S(1)} %get-tuple-element.15), channel_id=1, source_target_pairs={{1,0},{2,1},{3,2},{4,3},{5,4},{6,5},{7,6},{9,8},{10,9},{11,10},{12... | collective-permute-start | bytes 49160 | tf_op jit(solution)/shard_map/ppermute | solution.py:310
  50.7 37.0 %all-to-all-start.2 = ((f32[8,224,128]{2,1,0:T(8,128)}), f32[8,224,128]{2,1,0:T(8,128)S(1)}, u32[]{:S(2)}, u32[]{:S(2)}) async-start(f32[8,224,128]{2,1,0:T(8,128)} %broadcast_in_dim.2), calls=%async_computation.2 | async-start | bytes 1835008 | tf_op jit(solution)/shard_map/all_to_all | solution.py:336
  87.7 18.7 %all-to-all-start.1 = ((f32[64,2,2,128]{3,2,1,0:T(2,128)}), f32[64,2,2,128]{3,2,1,0:T(2,128)S(1)}, u32[]{:S(2)}, u32[]{:S(2)}) async-start(f32[64,2,2,128]{3,2,1,0:T(2,128)} %bitcast.2), calls=%async_computation.1 | async-start | bytes 262144 | tf_op jit(solution)/shard_map/all_to_all | solution.py:352

commit v2 on v1

--- a/solution.py
+++ b/solution.py
@@ -18,6 +18,7 @@
 ROWS = INL * TILES
 GROUP = 8
 PORTS = 7
+RUN = 4
 
 
 def condense(mass, rhs, link):
@@ -243,29 +244,53 @@
             ].reshape(INL, CRS, LANES)
 
 
-def cross_kernel(axes, gathered, cells_v, cells_c, timed, out, ends, cells_x):
-    rank = lax.axis_index(axes[1])
-    ports = [
-        [gathered[n, p * ROWS : (p + 1) * ROWS, :] for p in range(PORTS)] for n in range(NARROW)
-    ]
+def ports_of(ref):
+    return [ref[p * ROWS : (p + 1) * ROWS, :] for p in range(PORTS)]
+
+
+def chain_of(ports):
     mass, rhs, link = [], [], []
     for n, (g, m0, m1, d0, d1, _, _) in enumerate(ports):
         mass += [m0, m1]
         rhs += [d0, d1]
         link.append(g)
-        if n < NARROW - 1:
+        if n < len(ports) - 1:
             link.append(half_weight * (ports[n][6] + ports[n + 1][5]))
-    m0, d0, m1, d1, g, steps = condense(mass, rhs, link)
+    return mass, rhs, link
+
+
+def merge_kernel(axes, own, by1, by2, by3, held, merged):
+    place = lax.rem(lax.axis_index(axes[1]), RUN)
+    for step, ref in enumerate((own, by1, by2, by3)):
+        held[place ^ step] = ref[...]
+    ports = [ports_of(held.at[n]) for n in range(RUN)]
+    m0, d0, m1, d1, g, _ = condense(*chain_of(ports))
+    for p, value in enumerate((g, m0, m1, d0, d1, ports[0][5], ports[-1][6])):
+        merged[p * ROWS : (p + 1) * ROWS, :] = value
+
+
+def cross_kernel(axes, held, merged, other, cells_v, cells_c, timed, out, ends, cells_x):
+    rank = lax.axis_index(axes[1])
+    place, high = lax.rem(rank, RUN), rank >= RUN
+    own, far = ports_of(merged), ports_of(other)
+    pair = [
+        [jnp.where(high, b, a) for a, b in zip(own, far)],
+        [jnp.where(high, a, b) for a, b in zip(own, far)],
+    ]
+    m0, d0, m1, d1, g, steps = condense(*chain_of(pair))
     inverse = 1.0 / (m0 * m1 + g * (m0 + m1))
     first = (d0 * (m1 + g) + g * d1) * inverse
     last = (d1 * (m0 + g) + g * d0) * inverse
-    for n, value in enumerate(expand(first, last, steps, 2 * NARROW)):
+    x = expand(first, last, steps, 4)
+    first, last = jnp.where(high, x[2], x[0]), jnp.where(high, x[3], x[1])
+    steps = condense(*chain_of([ports_of(held.at[n]) for n in range(RUN)]))[-1]
+    for n, value in enumerate(expand(first, last, steps, 2 * RUN)):
         ends[n] = value
     v = [cells_v[pl.ds(c * ROWS, ROWS), :] for c in range(CRS)]
     k = [cells_c[pl.ds(c * ROWS, ROWS), :] for c in range(CRS)]
     ones = jnp.ones((ROWS, LANES), jnp.float32)
-    _, _, _, _, _, steps = condense([ones] * CRS, v, links(k))
-    x = expand(ends[2 * rank], ends[2 * rank + 1], steps, CRS)
+    steps = condense([ones] * CRS, v, links(k))[-1]
+    x = expand(ends[2 * place], ends[2 * place + 1], steps, CRS)
     for c in range(CRS):
         cells_x[c * ROWS : (c + 1) * ROWS, :] = x[c]
     for i in range(INL):
@@ -332,8 +357,17 @@
     lines = lax.all_to_all(
         wide_ports.reshape(WIDE, PORTS, 2, LANES), wide_axes, split_axis=0, concat_axis=0, tiled=True
     )
-    spread = jnp.broadcast_to(narrow_ports[None], (NARROW, PORTS * ROWS, LANES))
-    gathered = lax.all_to_all(spread, narrow_axes, split_axis=0, concat_axis=0, tiled=True)
+
+    def swapped(x, step):
+        return lax.ppermute(x, narrow_axes, [(n, n ^ step) for n in range(NARROW)])
+
+    held, merged = call(
+        lambda *refs: merge_kernel(axes, *refs),
+        (f32(RUN, PORTS * ROWS, LANES), f32(PORTS * ROWS, LANES)),
+        narrow_ports,
+        *[swapped(narrow_ports, step) for step in range(1, RUN)],
+    )
+    other = swapped(merged, RUN)
     timed = call(
         time_kernel,
         f32(INL, CRS, NT),
@@ -346,6 +380,7 @@
             (3, NT // 2 // GROUP, LANES),
         ),
     )
+    lines, held, timed = lax.optimization_barrier((lines, held, timed))
     solved = call(
         wide_kernel, f32(WIDE * 4, LANES), lines.reshape(WIDE * PORTS * 2, LANES)
     )
@@ -355,11 +390,13 @@
     others = call(
         lambda *refs: cross_kernel(axes, *refs),
         f32(INL, CRS, NT),
-        gathered,
+        held,
+        merged,
+        other,
         cells_v,
         cells_c,
         timed,
-        scratch=((2 * NARROW, ROWS, LANES), (cells, LANES)),
+        scratch=((2 * RUN, ROWS, LANES), (cells, LANES)),
     )
     return call(
         finish_kernel, f32(INL, CRS, NT), volume, cond, ends.reshape(WIDE * 4, LANES), others

time: 108 us -> 85.2 us (0.79)
  the two profiles are of different devices: /device:TPU:1 before, /device:TPU:17 now
where the time goes in v2:
time: 85.2 us; the launch traced here: 84.8 us
  starting transfers between devices  60.7 us (71%)
  waiting for transfers between devices  18.1 us (21%)
  Pallas kernels  4.88 us (6%)
  local copies, waits for them, and re-layouts  0.95 us (1%)
    ppermute x4, starting transfers between devices, swapped(): return lax.ppermute(x, narrow_axes, [(n, n ^ step) for n in range(NARROW)])  21.6 us
    all_to_all x1, starting transfers between devices, per_device(): lax.all_to_all(wide_ports.reshape(WIDE, PORTS, 2, LANES), wide_axes, spli...  16.7 us
    ppermute x4, waiting for transfers between devices, swapped(): return lax.ppermute(x, narrow_axes, [(n, n ^ step) for n in range(NARROW)])  14.9 us
    all_to_all x1, starting transfers between devices, per_device(): lax.all_to_all(solved.reshape(WIDE, 2, 2, LANES), wide_axes, split_axis=0...  12.3 us
    ppermute x4, starting transfers between devices, neighbour(): return lax.ppermute(x, axis, pairs)  10.1 us
    pallas_call x6, Pallas kernels, call(): pl.pallas_call(kernel, out_shape=out, scratch_shapes=[pltpu.VMEM(s, jnp.f...  4.88 us
    ppermute x4, waiting for transfers between devices, neighbour(): return lax.ppermute(x, axis, pairs)  3.18 us
  transfers between devices with their start and end apart: 10, of which 4 were waited for; matrix products, arithmetic and copies ran while one was open for 0% of the time, Pallas kernels for 2%

profile of v2, /device:TPU:17, one launch (start us, length us, event | category | flops | bytes accessed | tf_op | source)
XLA Modules:
  0.0 84.8 jit_solution(12146046905455993638)
XLA Ops:
  0.0 0.0 copy-start
  0.0 0.9 %fusion.1 = (f32[1,16,1024]{2,1,0:T(8,128)S(1)}, f32[1,16,1024]{2,1,0:T(8,128)S(1)}) fusion(f32[4,16,1024]{2,1,0:T(8,128)} %vol.3), kind=kLoop, calls=%fused_computation.1 | loop fusion | bytes 262144 | tf_op jit(solution)/shard_map/slice | solution.py:338
  0.9 3.8 %collective-permute-start = (f32[1,16,1024]{2,1,0:T(8,128)S(1)}, f32[1,16,1024]{2,1,0:T(8,128)S(1)}, u32[]{:S(2)}, u32[]{:S(2)}) collective-permute-start(f32[1,16,1024]{2,1,0:T(8,128)S(1)} %get-tuple-element.28), channel_id=1, source_target_pairs={{0,8},{8,16},{16,24},{24,32},{32,40},{40,48},{48,56},{56,64},{64,7... | collective-permute-start | bytes 196616 | tf_op jit(solution)/shard_map/ppermute | solution.py:335
  4.7 1.9 %collective-permute-start.1 = (f32[1,16,1024]{2,1,0:T(8,128)S(1)}, f32[1,16,1024]{2,1,0:T(8,128)S(1)}, u32[]{:S(2)}, u32[]{:S(2)}) collective-permute-start(f32[1,16,1024]{2,1,0:T(8,128)S(1)} %get-tuple-element.27), channel_id=1, source_target_pairs={{8,0},{16,8},{24,16},{32,24},{40,32},{48,40},{56,48},{64,56},{72,6... | collective-permute-start | bytes 196616 | tf_op jit(solution)/shard_map/ppermute | solution.py:335
  6.6 0.0 copy-done
  6.7 3.1 %collective-permute-start.2 = (f32[4,1,1024]{2,1,0:T(1,128)S(1)}, f32[4,1,1024]{2,1,0:T(1,128)S(1)}, u32[]{:S(2)}, u32[]{:S(2)}) collective-permute-start(f32[4,1,1024]{2,1,0:T(1,128)S(1)} %get-tuple-element.26), channel_id=1, source_target_pairs={{0,1},{1,2},{2,3},{3,4},{4,5},{5,6},{6,7},{8,9},{9,10},{10,11},{11... | collective-permute-start | bytes 49160 | tf_op jit(solution)/shard_map/ppermute | solution.py:335
  9.8 1.3 %collective-permute-start.3 = (f32[4,1,1024]{2,1,0:T(1,128)S(1)}, f32[4,1,1024]{2,1,0:T(1,128)S(1)}, u32[]{:S(2)}, u32[]{:S(2)}) collective-permute-start(f32[4,1,1024]{2,1,0:T(1,128)S(1)} %get-tuple-element.25), channel_id=1, source_target_pairs={{1,0},{2,1},{3,2},{4,3},{5,4},{6,5},{7,6},{9,8},{10,9},{11,10},{12... | collective-permute-start | bytes 49160 | tf_op jit(solution)/shard_map/ppermute | solution.py:335
  11.1 0.0 collective-permute-done.2.refs_3_
  11.1 3.2 %collective-permute-done.3.refs_4_ = f32[4,1,1024]{2,1,0:T(1,128)S(1)} collective-permute-done((f32[4,1,1024]{2,1,0:T(1,128)S(1)}, f32[4,1,1024]{2,1,0:T(1,128)S(1)}, u32[]{:S(2)}, u32[]{:S(2)}) %collective-permute-start.3) | collective-permute-done | bytes 16416 | tf_op jit(solution)/shard_map/ppermute | solution.py:335
  14.3 0.0 collective-permute-done.refs_1_
  14.3 0.0 collective-permute-done.1.refs_2_
  14.3 1.5 %shard_map.17 = (f32[4,16,1024]{2,1,0:T(8,128)S(1)}, f32[896,128]{1,0:T(8,128)}, f32[224,128]{1,0:T(8,128)S(1)}, f32[512,128]{1,0:T(8,128)S(1)}, f32[512,128]{1,0:T(8,128)S(1)}) custom-call(f32[4,16,1024]{2,1,0:T(8,128)S(1)} %copy-done, f32[1,16,1024]{2,1,0:T(8,128)S(1)} %collective-permute-done.refs_1_, f32[1,16,1024]{2,1,0:T(8,128)S(1)} %collective-permute-done.1.refs_2_, ...), custom_call_target="tpu_custom_call" | custom-call | tf_op jit(solution)/shard_map/pallas_call | solution.py:322
  15.8 16.7 %all-to-all-start = ((f32[64,7,2,128]{3,2,1,0:T(2,128)}), f32[64,7,2,128]{3,2,1,0:T(2,128)S(1)}, u32[]{:S(2)}, u32[]{:S(2)}) async-start(f32[64,7,2,128]{3,2,1,0:T(2,128)} %bitcast), calls=%async_computation | async-start | bytes 917504 | tf_op jit(solution)/shard_map/all_to_all | solution.py:357
  32.5 3.1 %collective-permute-start.4 = (f32[224,128]{1,0:T(8,128)S(1)}, f32[224,128]{1,0:T(8,128)S(1)}, u32[]{:S(2)}, u32[]{:S(2)}) collective-permute-start(f32[224,128]{1,0:T(8,128)S(1)} %get-tuple-element.17.refs_0_), channel_id=1, source_target_pairs={{0,1},{1,0},{2,3},{3,2},{4,5},{5,4},{6,7},{7,6},{8,9},{9,8},{10,11... | collective-permute-start | bytes 344072 | tf_op jit(solution)/shard_map/ppermute | solution.py:362
  35.6 14.6 %collective-permute-start.5 = (f32[224,128]{1,0:T(8,128)S(1)}, f32[224,128]{1,0:T(8,128)S(1)}, u32[]{:S(2)}, u32[]{:S(2)}) collective-permute-start(f32[224,128]{1,0:T(8,128)S(1)} %get-tuple-element.17.refs_0_), channel_id=1, source_target_pairs={{0,2},{1,3},{2,0},{3,1},{4,6},{5,7},{6,4},{7,5},{8,10},{9,11},{10,... | collective-permute-start | bytes 344072 | tf_op jit(solution)/shard_map/ppermute | solution.py:362
  50.3 1.9 %collective-permute-start.6 = (f32[224,128]{1,0:T(8,128)S(1)}, f32[224,128]{1,0:T(8,128)S(1)}, u32[]{:S(2)}, u32[]{:S(2)}) collective-permute-start(f32[224,128]{1,0:T(8,128)S(1)} %get-tuple-element.17.refs_0_), channel_id=1, source_target_pairs={{0,3},{1,2},{2,1},{3,0},{4,7},{5,6},{6,5},{7,4},{8,11},{9,10},{10,... | collective-permute-start | bytes 344072 | tf_op jit(solution)/shard_map/ppermute | solution.py:362
  52.2 1.1 %shard_map.19.refs_5_ = f32[4,16,1024]{2,1,0:T(8,128)S(1)} custom-call(f32[4,16,1024]{2,1,0:T(8,128)S(1)} %copy-done, f32[4,16,1024]{2,1,0:T(8,128)S(1)} %get-tuple-element.15.cond), custom_call_target="tpu_custom_call" | custom-call | tf_op jit(solution)/shard_map/pallas_call | solution.py:322
  53.3 0.0 collective-permute-done.4.refs_1_
  53.3 0.7 collective-permute-done.5.refs_2_
  54.0 3.0 %collective-permute-done.6.refs_3_ = f32[224,128]{1,0:T(8,128)S(1)} collective-permute-done((f32[224,128]{1,0:T(8,128)S(1)}, f32[224,128]{1,0:T(8,128)S(1)}, u32[]{:S(2)}, u32[]{:S(2)}) %collective-permute-start.6) | collective-permute-done | bytes 114720 | tf_op jit(solution)/shard_map/ppermute | solution.py:362
  57.0 0.1 shard_map.18
  57.1 0.0 all-to-all-done
  57.1 0.9 %shard_map.20 = f32[256,128]{1,0:T(8,128)} custom-call(f32[896,128]{1,0:T(8,128)S(1)} %bitcast.4), custom_call_target="tpu_custom_call" | custom-call | tf_op jit(solution)/shard_map/pallas_call | solution.py:322
  58.1 12.3 %all-to-all-start.1 = ((f32[64,2,2,128]{3,2,1,0:T(2,128)}), f32[64,2,2,128]{3,2,1,0:T(2,128)S(1)}, u32[]{:S(2)}, u32[]{:S(2)}) async-start(f32[64,2,2,128]{3,2,1,0:T(2,128)} %bitcast.2), calls=%async_computation.1 | async-start | bytes 262144 | tf_op jit(solution)/shard_map/all_to_all | solution.py:387
  70.4 1.9 %collective-permute-start.7 = (f32[224,128]{1,0:T(8,128)S(1)}, f32[224,128]{1,0:T(8,128)S(1)}, u32[]{:S(2)}, u32[]{:S(2)}) collective-permute-start(f32[224,128]{1,0:T(8,128)S(1)} %get-tuple-element.21.refs_1_), channel_id=1, source_target_pairs={{0,4},{1,5},{2,6},{3,7},{4,0},{5,1},{6,2},{7,3},{8,12},{9,13},{10,... | collective-permute-start | bytes 344072 | tf_op jit(solution)/shard_map/ppermute | solution.py:362
  72.3 11.2 %collective-permute-done.7.refs_2_ = f32[224,128]{1,0:T(8,128)S(1)} collective-permute-done((f32[224,128]{1,0:T(8,128)S(1)}, f32[224,128]{1,0:T(8,128)S(1)}, u32[]{:S(2)}, u32[]{:S(2)}) %collective-permute-start.7) | collective-permute-done | bytes 114720 | tf_op jit(solution)/shard_map/ppermute | solution.py:362
  83.5 0.4 shard_map.21.others
  84.0 0.0 all-to-all-done.1
  84.0 0.8 shard_map.22
  (1 shorter events, 0.0 us)
Async XLA Ops:
  0.0 6.6 %copy-start = (f32[4,16,1024]{2,1,0:T(8,128)S(1)}, f32[4,16,1024]{2,1,0:T(8,128)}, u32[]{:S(2)}) copy-start(f32[4,16,1024]{2,1,0:T(8,128)} %vol.3) | copy-start | bytes 786436
  0.9 13.4 %collective-permute-start = (f32[1,16,1024]{2,1,0:T(8,128)S(1)}, f32[1,16,1024]{2,1,0:T(8,128)S(1)}, u32[]{:S(2)}, u32[]{:S(2)}) collective-permute-start(f32[1,16,1024]{2,1,0:T(8,128)S(1)} %get-tuple-element.28), channel_id=1, source_target_pairs={{0,8},{8,16},{16,24},{24,32},{32,40},{40,48},{48,56},{56,64},{64,7... | collective-permute-start | bytes 196616 | tf_op jit(solution)/shard_map/ppermute | solution.py:335
  4.7 9.6 %collective-permute-start.1 = (f32[1,16,1024]{2,1,0:T(8,128)S(1)}, f32[1,16,1024]{2,1,0:T(8,128)S(1)}, u32[]{:S(2)}, u32[]{:S(2)}) collective-permute-start(f32[1,16,1024]{2,1,0:T(8,128)S(1)} %get-tuple-element.27), channel_id=1, source_target_pairs={{8,0},{16,8},{24,16},{32,24},{40,32},{48,40},{56,48},{64,56},{72,6... | collective-permute-start | bytes 196616 | tf_op jit(solution)/shard_map/ppermute | solution.py:335
  6.7 4.4 %collective-permute-start.2 = (f32[4,1,1024]{2,1,0:T(1,128)S(1)}, f32[4,1,1024]{2,1,0:T(1,128)S(1)}, u32[]{:S(2)}, u32[]{:S(2)}) collective-permute-start(f32[4,1,1024]{2,1,0:T(1,128)S(1)} %get-tuple-element.26), channel_id=1, source_target_pairs={{0,1},{1,2},{2,3},{3,4},{4,5},{5,6},{6,7},{8,9},{9,10},{10,11},{11... | collective-permute-start | bytes 49160 | tf_op jit(solution)/shard_map/ppermute | solution.py:335
  9.8 4.5 %collective-permute-start.3 = (f32[4,1,1024]{2,1,0:T(1,128)S(1)}, f32[4,1,1024]{2,1,0:T(1,128)S(1)}, u32[]{:S(2)}, u32[]{:S(2)}) collective-permute-start(f32[4,1,1024]{2,1,0:T(1,128)S(1)} %get-tuple-element.25), channel_id=1, source_target_pairs={{1,0},{2,1},{3,2},{4,3},{5,4},{6,5},{7,6},{9,8},{10,9},{11,10},{12... | collective-permute-start | bytes 49160 | tf_op jit(solution)/shard_map/ppermute | solution.py:335
  15.8 41.3 %all-to-all-start = ((f32[64,7,2,128]{3,2,1,0:T(2,128)}), f32[64,7,2,128]{3,2,1,0:T(2,128)S(1)}, u32[]{:S(2)}, u32[]{:S(2)}) async-start(f32[64,7,2,128]{3,2,1,0:T(2,128)} %bitcast), calls=%async_computation | async-start | bytes 917504 | tf_op jit(solution)/shard_map/all_to_all | solution.py:357
  32.5 20.8 %collective-permute-start.4 = (f32[224,128]{1,0:T(8,128)S(1)}, f32[224,128]{1,0:T(8,128)S(1)}, u32[]{:S(2)}, u32[]{:S(2)}) collective-permute-start(f32[224,128]{1,0:T(8,128)S(1)} %get-tuple-element.17.refs_0_), channel_id=1, source_target_pairs={{0,1},{1,0},{2,3},{3,2},{4,5},{5,4},{6,7},{7,6},{8,9},{9,8},{10,11... | collective-permute-start | bytes 344072 | tf_op jit(solution)/shard_map/ppermute | solution.py:362
  35.6 18.3 %collective-permute-start.5 = (f32[224,128]{1,0:T(8,128)S(1)}, f32[224,128]{1,0:T(8,128)S(1)}, u32[]{:S(2)}, u32[]{:S(2)}) collective-permute-start(f32[224,128]{1,0:T(8,128)S(1)} %get-tuple-element.17.refs_0_), channel_id=1, source_target_pairs={{0,2},{1,3},{2,0},{3,1},{4,6},{5,7},{6,4},{7,5},{8,10},{9,11},{10,... | collective-permute-start | bytes 344072 | tf_op jit(solution)/shard_map/ppermute | solution.py:362
  50.3 6.7 %collective-permute-start.6 = (f32[224,128]{1,0:T(8,128)S(1)}, f32[224,128]{1,0:T(8,128)S(1)}, u32[]{:S(2)}, u32[]{:S(2)}) collective-permute-start(f32[224,128]{1,0:T(8,128)S(1)} %get-tuple-element.17.refs_0_), channel_id=1, source_target_pairs={{0,3},{1,2},{2,1},{3,0},{4,7},{5,6},{6,5},{7,4},{8,11},{9,10},{10,... | collective-permute-start | bytes 344072 | tf_op jit(solution)/shard_map/ppermute | solution.py:362
  58.1 25.9 %all-to-all-start.1 = ((f32[64,2,2,128]{3,2,1,0:T(2,128)}), f32[64,2,2,128]{3,2,1,0:T(2,128)S(1)}, u32[]{:S(2)}, u32[]{:S(2)}) async-start(f32[64,2,2,128]{3,2,1,0:T(2,128)} %bitcast.2), calls=%async_computation.1 | async-start | bytes 262144 | tf_op jit(solution)/shard_map/all_to_all | solution.py:387
  70.4 13.1 %collective-permute-start.7 = (f32[224,128]{1,0:T(8,128)S(1)}, f32[224,128]{1,0:T(8,128)S(1)}, u32[]{:S(2)}, u32[]{:S(2)}) collective-permute-start(f32[224,128]{1,0:T(8,128)S(1)} %get-tuple-element.21.refs_1_), channel_id=1, source_target_pairs={{0,4},{1,5},{2,6},{3,7},{4,0},{5,1},{6,2},{7,3},{8,12},{9,13},{10,... | collective-permute-start | bytes 344072 | tf_op jit(solution)/shard_map/ppermute | solution.py:362

commit v3 on v2

--- a/solution.py
+++ b/solution.py
@@ -77,26 +77,31 @@
 
 
 def prepare_kernel(
-    axes, vol, before, after, left, right, cond, wide_out, narrow_out, cells_v, cells_c
+    axes, vol, wide0, wide1, narrow0, narrow1, cond, wide_out, narrow_out, cells_v, cells_c
 ):
     wide_axes, narrow_axes = axes
     wide_rank, narrow_rank = lax.axis_index(wide_axes), lax.axis_index(narrow_axes)
+    wide_even, narrow_even = lax.rem(wide_rank, 2) == 0, lax.rem(narrow_rank, 2) == 0
     col = iota((CRS, NT), 1)
     row = iota((CRS, NT), 0)
     for i in range(INL):
         here = vol[i]
         if i == 0:
-            up = jnp.where(wide_rank == 0, here, before[0])
+            up = jnp.where(wide_even, wide1[0], wide0[0])
+            up = jnp.where(wide_rank == 0, here, up)
         else:
             up = vol[i - 1]
         if i == INL - 1:
-            down = jnp.where(wide_rank == WIDE - 1, here, after[0])
+            down = jnp.where(wide_even, wide0[0], wide1[0])
+            down = jnp.where(wide_rank == WIDE - 1, here, down)
         else:
             down = vol[i + 1]
         power = (0.5 * (down - up)) ** 2
-        edge = jnp.where(narrow_rank == 0, here[:1], left[i])
+        edge = jnp.where(narrow_even, narrow1[i], narrow0[i])
+        edge = jnp.where(narrow_rank == 0, here[:1], edge)
         lower = jnp.where(row == 0, edge, pltpu.roll(here, 1, 0))
-        edge = jnp.where(narrow_rank == NARROW - 1, here[CRS - 1 :], right[i])
+        edge = jnp.where(narrow_even, narrow0[i], narrow1[i])
+        edge = jnp.where(narrow_rank == NARROW - 1, here[CRS - 1 :], edge)
         upper = jnp.where(row == CRS - 1, edge, pltpu.roll(here, CRS - 1, 0))
         power = power + (0.5 * (upper - lower)) ** 2
         earlier = jnp.where(col == 0, here, pltpu.roll(here, 1, 1))
@@ -263,27 +268,31 @@
     place = lax.rem(lax.axis_index(axes[1]), RUN)
     for step, ref in enumerate((own, by1, by2, by3)):
         held[place ^ step] = ref[...]
+    _, edge = facing(held, lax.axis_index(axes[1]) >= RUN)
+    for p, value in enumerate(edge):
+        merged[p * ROWS : (p + 1) * ROWS, :] = value
+
+
+def facing(held, high):
     ports = [ports_of(held.at[n]) for n in range(RUN)]
-    m0, d0, m1, d1, g, _ = condense(*chain_of(ports))
-    for p, value in enumerate((g, m0, m1, d0, d1, ports[0][5], ports[-1][6])):
-        merged[p * ROWS : (p + 1) * ROWS, :] = value
-
-
-def cross_kernel(axes, held, merged, other, cells_v, cells_c, timed, out, ends, cells_x):
+    m0, d0, m1, d1, g, steps = condense(*chain_of(ports))
+    here_m, here_d = jnp.where(high, m0, m1), jnp.where(high, d0, d1)
+    away_m, away_d = jnp.where(high, m1, m0), jnp.where(high, d1, d0)
+    inverse = 1.0 / (g + away_m)
+    slope, base = g * inverse, away_d * inverse
+    edge = (here_m + slope * away_m, here_d + slope * away_d, jnp.where(high, ports[0][5], ports[-1][6]))
+    return (slope, base, steps), edge
+
+
+def cross_kernel(axes, held, other, cells_v, cells_c, timed, out, ends, cells_x):
     rank = lax.axis_index(axes[1])
     place, high = lax.rem(rank, RUN), rank >= RUN
-    own, far = ports_of(merged), ports_of(other)
-    pair = [
-        [jnp.where(high, b, a) for a, b in zip(own, far)],
-        [jnp.where(high, a, b) for a, b in zip(own, far)],
-    ]
-    m0, d0, m1, d1, g, steps = condense(*chain_of(pair))
-    inverse = 1.0 / (m0 * m1 + g * (m0 + m1))
-    first = (d0 * (m1 + g) + g * d1) * inverse
-    last = (d1 * (m0 + g) + g * d0) * inverse
-    x = expand(first, last, steps, 4)
-    first, last = jnp.where(high, x[2], x[0]), jnp.where(high, x[3], x[1])
-    steps = condense(*chain_of([ports_of(held.at[n]) for n in range(RUN)]))[-1]
+    (slope, base, steps), (m0, d0, c0) = facing(held, high)
+    m1, d1, c1 = [other[p * ROWS : (p + 1) * ROWS, :] for p in range(3)]
+    link = half_weight * (c0 + c1)
+    here = (d0 * (m1 + link) + link * d1) / (m0 * m1 + link * (m0 + m1))
+    away = base + slope * here
+    first, last = jnp.where(high, here, away), jnp.where(high, away, here)
     for n, value in enumerate(expand(first, last, steps, 2 * RUN)):
         ends[n] = value
     v = [cells_v[pl.ds(c * ROWS, ROWS), :] for c in range(CRS)]
@@ -330,14 +339,17 @@
 def per_device(axes, volume):
     wide_axes, narrow_axes = axes
 
-    def neighbour(x, axis, count, step):
-        pairs = [(i, i + step) for i in range(count) if 0 <= i + step < count]
-        return lax.ppermute(x, axis, pairs)
-
-    before = neighbour(volume[-1:], wide_axes, WIDE, 1)
-    after = neighbour(volume[:1], wide_axes, WIDE, -1)
-    left = neighbour(volume[:, -1:], narrow_axes, NARROW, 1)
-    right = neighbour(volume[:, :1], narrow_axes, NARROW, -1)
+    def exchanged(dim, axis, count):
+        odd = lax.rem(lax.axis_index(axis), 2)
+        end = volume.shape[dim] - 1
+        got = []
+        for start in range(2):
+            pairs = [(i, i + 1) for i in range(start, count - 1, 2)]
+            at = end * (odd ^ 1 ^ start)
+            layer = lax.dynamic_slice_in_dim(volume, at, 1, dim)
+            got.append(lax.ppermute(layer, axis, pairs + [(j, i) for i, j in pairs]))
+        return got
+
     cells = CRS * ROWS
     cond, wide_ports, narrow_ports, cells_v, cells_c = call(
         lambda *refs: prepare_kernel(axes, *refs),
@@ -349,10 +361,8 @@
             f32(cells, LANES),
         ),
         volume,
-        before,
-        after,
-        left,
-        right,
+        *exchanged(0, wide_axes, WIDE),
+        *exchanged(1, narrow_axes, NARROW),
     )
     lines = lax.all_to_all(
         wide_ports.reshape(WIDE, PORTS, 2, LANES), wide_axes, split_axis=0, concat_axis=0, tiled=True
@@ -363,7 +373,7 @@
 
     held, merged = call(
         lambda *refs: merge_kernel(axes, *refs),
-        (f32(RUN, PORTS * ROWS, LANES), f32(PORTS * ROWS, LANES)),
+        (f32(RUN, PORTS * ROWS, LANES), f32(3 * ROWS, LANES)),
         narrow_ports,
         *[swapped(narrow_ports, step) for step in range(1, RUN)],
     )
@@ -391,7 +401,6 @@
         lambda *refs: cross_kernel(axes, *refs),
         f32(INL, CRS, NT),
         held,
-        merged,
         other,
         cells_v,
         cells_c,

time: 85.2 us -> 76.5 us (0.90)
  the two profiles are of different devices: /device:TPU:17 before, /device:TPU:1 now
where the time goes in v3:
time: 76.5 us; the launch traced here: 76.1 us
  starting transfers between devices  58.3 us (76%)
  waiting for transfers between devices  11.8 us (15%)
  Pallas kernels  4.88 us (6%)
  local copies, waits for them, and re-layouts  0.96 us (1%)
    ppermute x4, starting transfers between devices, swapped(): return lax.ppermute(x, narrow_axes, [(n, n ^ step) for n in range(NARROW)])  22.3 us
    ppermute x4, starting transfers between devices, exchanged(): got.append(lax.ppermute(layer, axis, pairs + [(j, i) for i, j in pairs]))  13.3 us
    all_to_all x1, starting transfers between devices, per_device(): lax.all_to_all(solved.reshape(WIDE, 2, 2, LANES), wide_axes, split_axis=0...  12.3 us
    all_to_all x1, starting transfers between devices, per_device(): lax.all_to_all(wide_ports.reshape(WIDE, PORTS, 2, LANES), wide_axes, spli...  10.4 us
    ppermute x4, waiting for transfers between devices, swapped(): return lax.ppermute(x, narrow_axes, [(n, n ^ step) for n in range(NARROW)])  8.48 us
    pallas_call x6, Pallas kernels, call(): pl.pallas_call(kernel, out_shape=out, scratch_shapes=[pltpu.VMEM(s, jnp.f...  4.88 us
    ppermute x4, waiting for transfers between devices, exchanged(): got.append(lax.ppermute(layer, axis, pairs + [(j, i) for i, j in pairs]))  1.89 us
  transfers between devices with their start and end apart: 10, of which 5 were waited for; matrix products, arithmetic and copies ran while one was open for 0% of the time, Pallas kernels for 2%

profile of v3, /device:TPU:1, one launch (start us, length us, event | category | flops | bytes accessed | tf_op | source)
XLA Modules:
  0.0 76.1 jit_solution(17408230535723157405)
XLA Ops:
  0.0 0.0 copy-start
  0.0 0.9 %constant_dynamic-slice_fusion.2 = (f32[1,16,1024]{2,1,0:T(8,128)S(1)}, f32[1,16,1024]{2,1,0:T(8,128)S(1)}) fusion(f32[4,16,1024]{2,1,0:T(8,128)} %vol.3, s32[]{:T(128)S(6)} %select_n.13, s32[]{:T(128)S(6)} %select_n.12), kind=kLoop, calls=%fused_computation.2 | loop fusion | bytes 262152 | tf_op jit(solution)/shard_map/dynamic_slice | solution.py:349
  0.9 8.8 %collective-permute-start = (f32[1,16,1024]{2,1,0:T(8,128)S(1)}, f32[1,16,1024]{2,1,0:T(8,128)S(1)}, u32[]{:S(2)}, u32[]{:S(2)}) collective-permute-start(f32[1,16,1024]{2,1,0:T(8,128)S(1)} %get-tuple-element.28), channel_id=1, source_target_pairs={{0,8},{16,24},{32,40},{48,56},{64,72},{80,88},{96,104},{112,120},{... | collective-permute-start | bytes 196616 | tf_op jit(solution)/shard_map/ppermute | solution.py:350
  9.7 1.9 %collective-permute-start.1 = (f32[1,16,1024]{2,1,0:T(8,128)S(1)}, f32[1,16,1024]{2,1,0:T(8,128)S(1)}, u32[]{:S(2)}, u32[]{:S(2)}) collective-permute-start(f32[1,16,1024]{2,1,0:T(8,128)S(1)} %get-tuple-element.27), channel_id=1, source_target_pairs={{8,16},{24,32},{40,48},{56,64},{72,80},{88,96},{104,112},{120,128}... | collective-permute-start | bytes 196616 | tf_op jit(solution)/shard_map/ppermute | solution.py:350
  11.7 0.0 copy-done
  11.7 1.9 %collective-permute-start.2 = (f32[4,1,1024]{2,1,0:T(1,128)S(1)}, f32[4,1,1024]{2,1,0:T(1,128)S(1)}, u32[]{:S(2)}, u32[]{:S(2)}) collective-permute-start(f32[4,1,1024]{2,1,0:T(1,128)S(1)} %get-tuple-element.26), channel_id=1, source_target_pairs={{0,1},{2,3},{4,5},{6,7},{1,0},{3,2},{5,4},{7,6},{8,9},{10,11},{12,... | collective-permute-start | bytes 49160 | tf_op jit(solution)/shard_map/ppermute | solution.py:350
  13.6 0.7 collective-permute-start.3
  14.3 1.9 %collective-permute-done.2.refs_3_ = f32[4,1,1024]{2,1,0:T(1,128)S(1)} collective-permute-done((f32[4,1,1024]{2,1,0:T(1,128)S(1)}, f32[4,1,1024]{2,1,0:T(1,128)S(1)}, u32[]{:S(2)}, u32[]{:S(2)}) %collective-permute-start.2) | collective-permute-done | bytes 16416 | tf_op jit(solution)/shard_map/ppermute | solution.py:350
  16.2 0.0 collective-permute-done.3.refs_4_
  16.2 0.0 collective-permute-done.refs_1_
  16.2 0.0 collective-permute-done.1.refs_2_
  16.2 1.5 %shard_map.17 = (f32[4,16,1024]{2,1,0:T(8,128)S(1)}, f32[896,128]{1,0:T(8,128)}, f32[224,128]{1,0:T(8,128)S(1)}, f32[512,128]{1,0:T(8,128)S(1)}, f32[512,128]{1,0:T(8,128)S(1)}) custom-call(f32[4,16,1024]{2,1,0:T(8,128)S(1)} %copy-done, f32[1,16,1024]{2,1,0:T(8,128)S(1)} %collective-permute-done.refs_1_, f32[1,16,1024]{2,1,0:T(8,128)S(1)} %collective-permute-done.1.refs_2_, ...), custom_call_target="tpu_custom_call" | custom-call | tf_op jit(solution)/shard_map/pallas_call | solution.py:331
  17.7 10.4 %all-to-all-start = ((f32[64,7,2,128]{3,2,1,0:T(2,128)}), f32[64,7,2,128]{3,2,1,0:T(2,128)S(1)}, u32[]{:S(2)}, u32[]{:S(2)}) async-start(f32[64,7,2,128]{3,2,1,0:T(2,128)} %bitcast), calls=%async_computation | async-start | bytes 917504 | tf_op jit(solution)/shard_map/all_to_all | solution.py:367
  28.2 5.6 %collective-permute-start.4 = (f32[224,128]{1,0:T(8,128)S(1)}, f32[224,128]{1,0:T(8,128)S(1)}, u32[]{:S(2)}, u32[]{:S(2)}) collective-permute-start(f32[224,128]{1,0:T(8,128)S(1)} %get-tuple-element.17.refs_0_), channel_id=1, source_target_pairs={{0,1},{1,0},{2,3},{3,2},{4,5},{5,4},{6,7},{7,6},{8,9},{9,8},{10,11... | collective-permute-start | bytes 344072 | tf_op jit(solution)/shard_map/ppermute | solution.py:372
  33.8 10.5 %collective-permute-start.5 = (f32[224,128]{1,0:T(8,128)S(1)}, f32[224,128]{1,0:T(8,128)S(1)}, u32[]{:S(2)}, u32[]{:S(2)}) collective-permute-start(f32[224,128]{1,0:T(8,128)S(1)} %get-tuple-element.17.refs_0_), channel_id=1, source_target_pairs={{0,2},{1,3},{2,0},{3,1},{4,6},{5,7},{6,4},{7,5},{8,10},{9,11},{10,... | collective-permute-start | bytes 344072 | tf_op jit(solution)/shard_map/ppermute | solution.py:372
  44.3 1.9 %collective-permute-start.6 = (f32[224,128]{1,0:T(8,128)S(1)}, f32[224,128]{1,0:T(8,128)S(1)}, u32[]{:S(2)}, u32[]{:S(2)}) collective-permute-start(f32[224,128]{1,0:T(8,128)S(1)} %get-tuple-element.17.refs_0_), channel_id=1, source_target_pairs={{0,3},{1,2},{2,1},{3,0},{4,7},{5,6},{6,5},{7,4},{8,11},{9,10},{10,... | collective-permute-start | bytes 344072 | tf_op jit(solution)/shard_map/ppermute | solution.py:372
  46.2 1.1 %shard_map.19.refs_4_ = f32[4,16,1024]{2,1,0:T(8,128)S(1)} custom-call(f32[4,16,1024]{2,1,0:T(8,128)S(1)} %copy-done, f32[4,16,1024]{2,1,0:T(8,128)S(1)} %get-tuple-element.15.cond), custom_call_target="tpu_custom_call" | custom-call | tf_op jit(solution)/shard_map/pallas_call | solution.py:331
  47.4 0.0 collective-permute-done.4.refs_1_
  47.4 0.6 collective-permute-done.5.refs_2_
  48.0 3.1 %collective-permute-done.6.refs_3_ = f32[224,128]{1,0:T(8,128)S(1)} collective-permute-done((f32[224,128]{1,0:T(8,128)S(1)}, f32[224,128]{1,0:T(8,128)S(1)}, u32[]{:S(2)}, u32[]{:S(2)}) %collective-permute-start.6) | collective-permute-done | bytes 114720 | tf_op jit(solution)/shard_map/ppermute | solution.py:372
  51.1 0.1 shard_map.18
  51.2 0.0 all-to-all-done
  51.2 0.9 %shard_map.20 = f32[256,128]{1,0:T(8,128)} custom-call(f32[896,128]{1,0:T(8,128)S(1)} %bitcast.4), custom_call_target="tpu_custom_call" | custom-call | tf_op jit(solution)/shard_map/pallas_call | solution.py:331
  52.1 12.3 %all-to-all-start.1 = ((f32[64,2,2,128]{3,2,1,0:T(2,128)}), f32[64,2,2,128]{3,2,1,0:T(2,128)S(1)}, u32[]{:S(2)}, u32[]{:S(2)}) async-start(f32[64,2,2,128]{3,2,1,0:T(2,128)} %bitcast.2), calls=%async_computation.1 | async-start | bytes 262144 | tf_op jit(solution)/shard_map/all_to_all | solution.py:397
  64.5 4.3 %collective-permute-start.7 = (f32[96,128]{1,0:T(8,128)S(1)}, f32[96,128]{1,0:T(8,128)S(1)}, u32[]{:S(2)}, u32[]{:S(2)}) collective-permute-start(f32[96,128]{1,0:T(8,128)S(1)} %get-tuple-element.21), channel_id=1, source_target_pairs={{0,4},{1,5},{2,6},{3,7},{4,0},{5,1},{6,2},{7,3},{8,12},{9,13},{10,... | collective-permute-start | bytes 147464 | tf_op jit(solution)/shard_map/ppermute | solution.py:372
  68.7 4.8 %collective-permute-done.7.refs_1_ = f32[96,128]{1,0:T(8,128)S(1)} collective-permute-done((f32[96,128]{1,0:T(8,128)S(1)}, f32[96,128]{1,0:T(8,128)S(1)}, u32[]{:S(2)}, u32[]{:S(2)}) %collective-permute-start.7) | collective-permute-done | bytes 49184 | tf_op jit(solution)/shard_map/ppermute | solution.py:372
  73.5 0.4 shard_map.21.others
  73.9 1.4 %all-to-all-done.1 = f32[64,2,2,128]{3,2,1,0:T(2,128)S(1)} async-done(((f32[64,2,2,128]{3,2,1,0:T(2,128)}), f32[64,2,2,128]{3,2,1,0:T(2,128)S(1)}, u32[]{:S(2)}, u32[]{:S(2)}) %all-to-all-start.1) | async-done | bytes 131104 | tf_op jit(solution)/shard_map/all_to_all | solution.py:397
  75.3 0.8 %shard_map.22 = f32[4,16,1024]{2,1,0:T(8,128)} custom-call(f32[4,16,1024]{2,1,0:T(8,128)S(1)} %copy-done, f32[4,16,1024]{2,1,0:T(8,128)S(1)} %get-tuple-element.15.cond, f32[256,128]{1,0:T(8,128)S(1)} %bitcast.5, f32[4,16,1024]{2,1,0:T(8,128)S(1)} %shard_map.21.others), custom_call_target="tpu_custom_call" | custom-call | tf_op jit(solution)/shard_map/pallas_call | solution.py:331
  (1 shorter events, 0.0 us)
Async XLA Ops:
  0.0 11.7 %copy-start = (f32[4,16,1024]{2,1,0:T(8,128)S(1)}, f32[4,16,1024]{2,1,0:T(8,128)}, u32[]{:S(2)}) copy-start(f32[4,16,1024]{2,1,0:T(8,128)} %vol.3) | copy-start | bytes 786436
  0.9 15.3 %collective-permute-start = (f32[1,16,1024]{2,1,0:T(8,128)S(1)}, f32[1,16,1024]{2,1,0:T(8,128)S(1)}, u32[]{:S(2)}, u32[]{:S(2)}) collective-permute-start(f32[1,16,1024]{2,1,0:T(8,128)S(1)} %get-tuple-element.28), channel_id=1, source_target_pairs={{0,8},{16,24},{32,40},{48,56},{64,72},{80,88},{96,104},{112,120},{... | collective-permute-start | bytes 196616 | tf_op jit(solution)/shard_map/ppermute | solution.py:350
  9.7 6.5 %collective-permute-start.1 = (f32[1,16,1024]{2,1,0:T(8,128)S(1)}, f32[1,16,1024]{2,1,0:T(8,128)S(1)}, u32[]{:S(2)}, u32[]{:S(2)}) collective-permute-start(f32[1,16,1024]{2,1,0:T(8,128)S(1)} %get-tuple-element.27), channel_id=1, source_target_pairs={{8,16},{24,32},{40,48},{56,64},{72,80},{88,96},{104,112},{120,128}... | collective-permute-start | bytes 196616 | tf_op jit(solution)/shard_map/ppermute | solution.py:350
  11.7 4.5 %collective-permute-start.2 = (f32[4,1,1024]{2,1,0:T(1,128)S(1)}, f32[4,1,1024]{2,1,0:T(1,128)S(1)}, u32[]{:S(2)}, u32[]{:S(2)}) collective-permute-start(f32[4,1,1024]{2,1,0:T(1,128)S(1)} %get-tuple-element.26), channel_id=1, source_target_pairs={{0,1},{2,3},{4,5},{6,7},{1,0},{3,2},{5,4},{7,6},{8,9},{10,11},{12,... | collective-permute-start | bytes 49160 | tf_op jit(solution)/shard_map/ppermute | solution.py:350
  13.6 2.6 %collective-permute-start.3 = (f32[4,1,1024]{2,1,0:T(1,128)S(1)}, f32[4,1,1024]{2,1,0:T(1,128)S(1)}, u32[]{:S(2)}, u32[]{:S(2)}) collective-permute-start(f32[4,1,1024]{2,1,0:T(1,128)S(1)} %get-tuple-element.25), channel_id=1, source_target_pairs={{1,2},{3,4},{5,6},{2,1},{4,3},{6,5},{9,10},{11,12},{13,14},{10,9},... | collective-permute-start | bytes 49160 | tf_op jit(solution)/shard_map/ppermute | solution.py:350
  17.7 33.5 %all-to-all-start = ((f32[64,7,2,128]{3,2,1,0:T(2,128)}), f32[64,7,2,128]{3,2,1,0:T(2,128)S(1)}, u32[]{:S(2)}, u32[]{:S(2)}) async-start(f32[64,7,2,128]{3,2,1,0:T(2,128)} %bitcast), calls=%async_computation | async-start | bytes 917504 | tf_op jit(solution)/shard_map/all_to_all | solution.py:367
  28.2 19.2 %collective-permute-start.4 = (f32[224,128]{1,0:T(8,128)S(1)}, f32[224,128]{1,0:T(8,128)S(1)}, u32[]{:S(2)}, u32[]{:S(2)}) collective-permute-start(f32[224,128]{1,0:T(8,128)S(1)} %get-tuple-element.17.refs_0_), channel_id=1, source_target_pairs={{0,1},{1,0},{2,3},{3,2},{4,5},{5,4},{6,7},{7,6},{8,9},{9,8},{10,11... | collective-permute-start | bytes 344072 | tf_op jit(solution)/shard_map/ppermute | solution.py:372
  33.8 14.2 %collective-permute-start.5 = (f32[224,128]{1,0:T(8,128)S(1)}, f32[224,128]{1,0:T(8,128)S(1)}, u32[]{:S(2)}, u32[]{:S(2)}) collective-permute-start(f32[224,128]{1,0:T(8,128)S(1)} %get-tuple-element.17.refs_0_), channel_id=1, source_target_pairs={{0,2},{1,3},{2,0},{3,1},{4,6},{5,7},{6,4},{7,5},{8,10},{9,11},{10,... | collective-permute-start | bytes 344072 | tf_op jit(solution)/shard_map/ppermute | solution.py:372
  44.3 6.7 %collective-permute-start.6 = (f32[224,128]{1,0:T(8,128)S(1)}, f32[224,128]{1,0:T(8,128)S(1)}, u32[]{:S(2)}, u32[]{:S(2)}) collective-permute-start(f32[224,128]{1,0:T(8,128)S(1)} %get-tuple-element.17.refs_0_), channel_id=1, source_target_pairs={{0,3},{1,2},{2,1},{3,0},{4,7},{5,6},{6,5},{7,4},{8,11},{9,10},{10,... | collective-permute-start | bytes 344072 | tf_op jit(solution)/shard_map/ppermute | solution.py:372
  52.1 23.1 %all-to-all-start.1 = ((f32[64,2,2,128]{3,2,1,0:T(2,128)}), f32[64,2,2,128]{3,2,1,0:T(2,128)S(1)}, u32[]{:S(2)}, u32[]{:S(2)}) async-start(f32[64,2,2,128]{3,2,1,0:T(2,128)} %bitcast.2), calls=%async_computation.1 | async-start | bytes 262144 | tf_op jit(solution)/shard_map/all_to_all | solution.py:397
  64.5 9.0 %collective-permute-start.7 = (f32[96,128]{1,0:T(8,128)S(1)}, f32[96,128]{1,0:T(8,128)S(1)}, u32[]{:S(2)}, u32[]{:S(2)}) collective-permute-start(f32[96,128]{1,0:T(8,128)S(1)} %get-tuple-element.21), channel_id=1, source_target_pairs={{0,4},{1,5},{2,6},{3,7},{4,0},{5,1},{6,2},{7,3},{8,12},{9,13},{10,... | collective-permute-start | bytes 147464 | tf_op jit(solution)/shard_map/ppermute | solution.py:372

commit v4 on v3

--- a/solution.py
+++ b/solution.py
@@ -76,8 +76,19 @@
     return slice(t * LANES, (t + 1) * LANES)
 
 
+def faces_kernel(axes, vol, narrow1, wide1, narrow0, wide0):
+    wide_even, narrow_even = [lax.rem(lax.axis_index(axis), 2) == 0 for axis in axes]
+    first, last = vol[0], vol[INL - 1]
+    wide1[0] = jnp.where(wide_even, first, last)
+    wide0[0] = jnp.where(wide_even, last, first)
+    for i in range(INL):
+        first, last = vol[i, :1], vol[i, CRS - 1 :]
+        narrow1[i] = jnp.where(narrow_even, first, last)
+        narrow0[i] = jnp.where(narrow_even, last, first)
+
+
 def prepare_kernel(
-    axes, vol, wide0, wide1, narrow0, narrow1, cond, wide_out, narrow_out, cells_v, cells_c
+    axes, vol, narrow1, wide1, narrow0, wide0, cond, wide_out, narrow_out, cells_v, cells_c
 ):
     wide_axes, narrow_axes = axes
     wide_rank, narrow_rank = lax.axis_index(wide_axes), lax.axis_index(narrow_axes)
@@ -264,7 +275,7 @@
     return mass, rhs, link
 
 
-def merge_kernel(axes, own, by1, by2, by3, held, merged):
+def merge_kernel(axes, own, by2, by1, by3, held, merged):
     place = lax.rem(lax.axis_index(axes[1]), RUN)
     for step, ref in enumerate((own, by1, by2, by3)):
         held[place ^ step] = ref[...]
@@ -339,17 +350,20 @@
 def per_device(axes, volume):
     wide_axes, narrow_axes = axes
 
-    def exchanged(dim, axis, count):
-        odd = lax.rem(lax.axis_index(axis), 2)
-        end = volume.shape[dim] - 1
-        got = []
-        for start in range(2):
-            pairs = [(i, i + 1) for i in range(start, count - 1, 2)]
-            at = end * (odd ^ 1 ^ start)
-            layer = lax.dynamic_slice_in_dim(volume, at, 1, dim)
-            got.append(lax.ppermute(layer, axis, pairs + [(j, i) for i, j in pairs]))
-        return got
-
+    def exchanged(layer, axis, count, start):
+        pairs = [(i, i + 1) for i in range(start, count - 1, 2)]
+        return lax.ppermute(layer, axis, pairs + [(j, i) for i, j in pairs])
+
+    inline_face, cross_face = f32(1, CRS, NT), f32(INL, 1, NT)
+    narrow1, wide1, narrow0, wide0 = call(
+        lambda *refs: faces_kernel(axes, *refs),
+        (cross_face, inline_face, cross_face, inline_face),
+        volume,
+    )
+    narrow1 = exchanged(narrow1, narrow_axes, NARROW, 1)
+    wide1 = exchanged(wide1, wide_axes, WIDE, 1)
+    narrow0 = exchanged(narrow0, narrow_axes, NARROW, 0)
+    wide0 = exchanged(wide0, wide_axes, WIDE, 0)
     cells = CRS * ROWS
     cond, wide_ports, narrow_ports, cells_v, cells_c = call(
         lambda *refs: prepare_kernel(axes, *refs),
@@ -361,8 +375,10 @@
             f32(cells, LANES),
         ),
         volume,
-        *exchanged(0, wide_axes, WIDE),
-        *exchanged(1, narrow_axes, NARROW),
+        narrow1,
+        wide1,
+        narrow0,
+        wide0,
     )
     lines = lax.all_to_all(
         wide_ports.reshape(WIDE, PORTS, 2, LANES), wide_axes, split_axis=0, concat_axis=0, tiled=True
@@ -375,7 +391,7 @@
         lambda *refs: merge_kernel(axes, *refs),
         (f32(RUN, PORTS * ROWS, LANES), f32(3 * ROWS, LANES)),
         narrow_ports,
-        *[swapped(narrow_ports, step) for step in range(1, RUN)],
+        *[swapped(narrow_ports, step) for step in (2, 1, 3)],
     )
     other = swapped(merged, RUN)
     timed = call(
@@ -390,7 +406,7 @@
             (3, NT // 2 // GROUP, LANES),
         ),
     )
-    lines, held, timed = lax.optimization_barrier((lines, held, timed))
+    lines, held, timed, other = lax.optimization_barrier((lines, held, timed, other))
     solved = call(
         wide_kernel, f32(WIDE * 4, LANES), lines.reshape(WIDE * PORTS * 2, LANES)
     )

time: 76.5 us -> 85.5 us (1.12)
  waiting for transfers between devices: 11.8 us -> 21.1 us
    all_to_all x1, waiting for transfers between devices: 1.39 us -> 10.4 us  [per_device(): lax.all_to_all(solved.reshape(WIDE, 2, 2, LANES), wide_axes, split_axis=0...]
    ppermute x4, starting transfers between devices: 22.3 us -> 17.4 us  [swapped(): return lax.ppermute(x, narrow_axes, [(n, n ^ step) for n in range(NARROW)])]
    all_to_all x1, starting transfers between devices: 10.4 us -> 14.4 us  [per_device(): lax.all_to_all(wide_ports.reshape(WIDE, PORTS, 2, LANES), wide_axes, spli...]
    all_to_all x1, starting transfers between devices: 12.3 us -> 13.5 us  [per_device(): lax.all_to_all(solved.reshape(WIDE, 2, 2, LANES), wide_axes, split_axis=0...]
    dynamic_slice x2 -> x0, local copies, waits for them, and re-layouts: 0.96 us -> none  [exchanged(): layer = lax.dynamic_slice_in_dim(volume, at, 1, dim)]
    unnamed x2 -> x4, local copies, waits for them, and re-layouts: 0.01 us -> 0.96 us
    pallas_call x6 -> x7, Pallas kernels: 4.88 us -> 4.9 us  [call(): pl.pallas_call(kernel, out_shape=out, scratch_shapes=[pltpu.VMEM(s, jnp.f...]
where the time goes in v4:
time: 85.5 us; the launch traced here: 85.1 us
  starting transfers between devices  58 us (68%)
  waiting for transfers between devices  21.1 us (25%)
  Pallas kernels  4.9 us (6%)
  local copies, waits for them, and re-layouts  0.96 us (1%)
    ppermute x4, starting transfers between devices, swapped(): return lax.ppermute(x, narrow_axes, [(n, n ^ step) for n in range(NARROW)])  17.4 us
    all_to_all x1, starting transfers between devices, per_device(): lax.all_to_all(wide_ports.reshape(WIDE, PORTS, 2, LANES), wide_axes, spli...  14.4 us
    all_to_all x1, starting transfers between devices, per_device(): lax.all_to_all(solved.reshape(WIDE, 2, 2, LANES), wide_axes, split_axis=0...  13.5 us
    ppermute x4, starting transfers between devices, exchanged(): return lax.ppermute(layer, axis, pairs + [(j, i) for i, j in pairs])  12.8 us
    all_to_all x1, waiting for transfers between devices, per_device(): lax.all_to_all(solved.reshape(WIDE, 2, 2, LANES), wide_axes, split_axis=0...  10.4 us
    ppermute x4, waiting for transfers between devices, swapped(): return lax.ppermute(x, narrow_axes, [(n, n ^ step) for n in range(NARROW)])  8.8 us
    pallas_call x7, Pallas kernels, call(): pl.pallas_call(kernel, out_shape=out, scratch_shapes=[pltpu.VMEM(s, jnp.f...  4.9 us
    ppermute x4, waiting for transfers between devices, exchanged(): return lax.ppermute(layer, axis, pairs + [(j, i) for i, j in pairs])  1.83 us
  transfers between devices with their start and end apart: 10, of which 5 were waited for; matrix products, arithmetic and copies ran while one was open for 0% of the time, Pallas kernels for 2%

profile of v4, /device:TPU:1, one launch (start us, length us, event | category | flops | bytes accessed | tf_op | source)
XLA Modules:
  0.0 85.1 jit_solution(336480918106396026)
XLA Ops:
  0.0 0.0 copy-start
  0.0 0.9 %copy-done = f32[4,16,1024]{2,1,0:T(8,128)S(1)} copy-done((f32[4,16,1024]{2,1,0:T(8,128)S(1)}, f32[4,16,1024]{2,1,0:T(8,128)}, u32[]{:S(2)}) %copy-start) | copy-done | bytes 262168
  1.0 4.6 %collective-permute-start.1 = (f32[1,16,1024]{2,1,0:T(8,128)S(1)}, f32[1,16,1024]{2,1,0:T(8,128)S(1)}, u32[]{:S(2)}, u32[]{:S(2)}) collective-permute-start(f32[1,16,1024]{2,1,0:T(8,128)S(1)} %get-tuple-element.21), channel_id=1, source_target_pairs={{8,16},{24,32},{40,48},{56,64},{72,80},{88,96},{104,112},{120,128}... | collective-permute-start | bytes 196616 | tf_op jit(solution)/shard_map/ppermute | solution.py:355
  5.6 4.9 %collective-permute-start.3 = (f32[1,16,1024]{2,1,0:T(8,128)S(1)}, f32[1,16,1024]{2,1,0:T(8,128)S(1)}, u32[]{:S(2)}, u32[]{:S(2)}) collective-permute-start(f32[1,16,1024]{2,1,0:T(8,128)S(1)} %get-tuple-element.23), channel_id=1, source_target_pairs={{0,8},{16,24},{32,40},{48,56},{64,72},{80,88},{96,104},{112,120},{... | collective-permute-start | bytes 196616 | tf_op jit(solution)/shard_map/ppermute | solution.py:355
  10.4 0.7 collective-permute-start
  11.1 2.6 %collective-permute-start.2 = (f32[4,1,1024]{2,1,0:T(1,128)S(1)}, f32[4,1,1024]{2,1,0:T(1,128)S(1)}, u32[]{:S(2)}, u32[]{:S(2)}) collective-permute-start(f32[4,1,1024]{2,1,0:T(1,128)S(1)} %get-tuple-element.22), channel_id=1, source_target_pairs={{0,1},{2,3},{4,5},{6,7},{1,0},{3,2},{5,4},{7,6},{8,9},{10,11},{12,... | collective-permute-start | bytes 49160 | tf_op jit(solution)/shard_map/ppermute | solution.py:355
  13.8 0.0 collective-permute-done.refs_1_
  13.8 1.8 %collective-permute-done.2.refs_3_ = f32[4,1,1024]{2,1,0:T(1,128)S(1)} collective-permute-done((f32[4,1,1024]{2,1,0:T(1,128)S(1)}, f32[4,1,1024]{2,1,0:T(1,128)S(1)}, u32[]{:S(2)}, u32[]{:S(2)}) %collective-permute-start.2) | collective-permute-done | bytes 16416 | tf_op jit(solution)/shard_map/ppermute | solution.py:355
  15.6 0.0 collective-permute-done.1.refs_2_
  15.6 0.0 collective-permute-done.3.refs_4_
  15.6 1.5 %shard_map.18 = (f32[4,16,1024]{2,1,0:T(8,128)S(1)}, f32[896,128]{1,0:T(8,128)}, f32[224,128]{1,0:T(8,128)S(1)}, f32[512,128]{1,0:T(8,128)S(1)}, f32[512,128]{1,0:T(8,128)S(1)}) custom-call(f32[4,16,1024]{2,1,0:T(8,128)S(1)} %copy-done, f32[4,1,1024]{2,1,0:T(1,128)S(1)} %collective-permute-done.refs_1_, f32[1,16,1024]{2,1,0:T(8,128)S(1)} %collective-permute-done.1.refs_2_, ...), custom_call_target="tpu_custom_call" | custom-call | tf_op jit(solution)/shard_map/pallas_call | solution.py:342
  17.1 14.4 %all-to-all-start = ((f32[64,7,2,128]{3,2,1,0:T(2,128)}), f32[64,7,2,128]{3,2,1,0:T(2,128)S(1)}, u32[]{:S(2)}, u32[]{:S(2)}) async-start(f32[64,7,2,128]{3,2,1,0:T(2,128)} %bitcast), calls=%async_computation | async-start | bytes 917504 | tf_op jit(solution)/shard_map/all_to_all | solution.py:383
  31.5 0.0 copy-start.1
  31.5 8.7 %collective-permute-start.4 = (f32[224,128]{1,0:T(8,128)S(1)}, f32[224,128]{1,0:T(8,128)S(1)}, u32[]{:S(2)}, u32[]{:S(2)}) collective-permute-start(f32[224,128]{1,0:T(8,128)S(1)} %get-tuple-element.26.refs_0_), channel_id=1, source_target_pairs={{0,2},{1,3},{2,0},{3,1},{4,6},{5,7},{6,4},{7,5},{8,10},{9,11},{10,... | collective-permute-start | bytes 344072 | tf_op jit(solution)/shard_map/ppermute | solution.py:388
  40.3 3.0 %collective-permute-start.5 = (f32[224,128]{1,0:T(8,128)S(1)}, f32[224,128]{1,0:T(8,128)S(1)}, u32[]{:S(2)}, u32[]{:S(2)}) collective-permute-start(f32[224,128]{1,0:T(8,128)S(1)} %get-tuple-element.26.refs_0_), channel_id=1, source_target_pairs={{0,1},{1,0},{2,3},{3,2},{4,5},{5,4},{6,7},{7,6},{8,9},{9,8},{10,11... | collective-permute-start | bytes 344072 | tf_op jit(solution)/shard_map/ppermute | solution.py:388
  43.3 1.9 %collective-permute-start.6 = (f32[224,128]{1,0:T(8,128)S(1)}, f32[224,128]{1,0:T(8,128)S(1)}, u32[]{:S(2)}, u32[]{:S(2)}) collective-permute-start(f32[224,128]{1,0:T(8,128)S(1)} %get-tuple-element.26.refs_0_), channel_id=1, source_target_pairs={{0,3},{1,2},{2,1},{3,0},{4,7},{5,6},{6,5},{7,4},{8,11},{9,10},{10,... | collective-permute-start | bytes 344072 | tf_op jit(solution)/shard_map/ppermute | solution.py:388
  45.2 0.0 collective-permute-done.4.refs_1_
  45.2 1.3 %collective-permute-done.5.refs_2_ = f32[224,128]{1,0:T(8,128)S(1)} collective-permute-done((f32[224,128]{1,0:T(8,128)S(1)}, f32[224,128]{1,0:T(8,128)S(1)}, u32[]{:S(2)}, u32[]{:S(2)}) %collective-permute-start.5) | collective-permute-done | bytes 114720 | tf_op jit(solution)/shard_map/ppermute | solution.py:388
  46.5 3.5 %collective-permute-done.6.refs_3_ = f32[224,128]{1,0:T(8,128)S(1)} collective-permute-done((f32[224,128]{1,0:T(8,128)S(1)}, f32[224,128]{1,0:T(8,128)S(1)}, u32[]{:S(2)}, u32[]{:S(2)}) %collective-permute-start.6) | collective-permute-done | bytes 114720 | tf_op jit(solution)/shard_map/ppermute | solution.py:388
  50.1 0.1 shard_map.19
  50.2 3.7 %collective-permute-start.7 = (f32[96,128]{1,0:T(8,128)S(1)}, f32[96,128]{1,0:T(8,128)S(1)}, u32[]{:S(2)}, u32[]{:S(2)}) collective-permute-start(f32[96,128]{1,0:T(8,128)S(1)} %get-tuple-element.28), channel_id=1, source_target_pairs={{0,4},{1,5},{2,6},{3,7},{4,0},{5,1},{6,2},{7,3},{8,12},{9,13},{10,... | collective-permute-start | bytes 147464 | tf_op jit(solution)/shard_map/ppermute | solution.py:388
  53.8 0.0 copy-done.1
  53.8 1.1 %shard_map.20.refs_4_ = f32[4,16,1024]{2,1,0:T(8,128)S(1)} custom-call(f32[4,16,1024]{2,1,0:T(8,128)S(1)} %copy-done.1, f32[4,16,1024]{2,1,0:T(8,128)S(1)} %get-tuple-element.24.cond), custom_call_target="tpu_custom_call" | custom-call | tf_op jit(solution)/shard_map/pallas_call | solution.py:342
  55.0 4.0 %collective-permute-done.7.refs_1_ = f32[96,128]{1,0:T(8,128)S(1)} collective-permute-done((f32[96,128]{1,0:T(8,128)S(1)}, f32[96,128]{1,0:T(8,128)S(1)}, u32[]{:S(2)}, u32[]{:S(2)}) %collective-permute-start.7) | collective-permute-done | bytes 49184 | tf_op jit(solution)/shard_map/ppermute | solution.py:388
  58.9 0.0 all-to-all-done
  58.9 0.9 %shard_map.21 = f32[256,128]{1,0:T(8,128)} custom-call(f32[896,128]{1,0:T(8,128)S(1)} %bitcast.4), custom_call_target="tpu_custom_call" | custom-call | tf_op jit(solution)/shard_map/pallas_call | solution.py:342
  59.9 13.5 %all-to-all-start.1 = ((f32[64,2,2,128]{3,2,1,0:T(2,128)}), f32[64,2,2,128]{3,2,1,0:T(2,128)S(1)}, u32[]{:S(2)}, u32[]{:S(2)}) async-start(f32[64,2,2,128]{3,2,1,0:T(2,128)} %bitcast.2), calls=%async_computation.1 | async-start | bytes 262144 | tf_op jit(solution)/shard_map/all_to_all | solution.py:413
  73.4 0.4 shard_map.22.others
  73.8 10.4 %all-to-all-done.1 = f32[64,2,2,128]{3,2,1,0:T(2,128)S(1)} async-done(((f32[64,2,2,128]{3,2,1,0:T(2,128)}), f32[64,2,2,128]{3,2,1,0:T(2,128)S(1)}, u32[]{:S(2)}, u32[]{:S(2)}) %all-to-all-start.1) | async-done | bytes 131104 | tf_op jit(solution)/shard_map/all_to_all | solution.py:413
  84.2 0.8 shard_map.23
  (1 shorter events, 0.0 us)
Async XLA Ops:
  0.0 0.9 %copy-start = (f32[4,16,1024]{2,1,0:T(8,128)S(1)}, f32[4,16,1024]{2,1,0:T(8,128)}, u32[]{:S(2)}) copy-start(f32[4,16,1024]{2,1,0:T(8,128)} %vol.3) | copy-start | bytes 786436
  1.0 14.6 %collective-permute-start.1 = (f32[1,16,1024]{2,1,0:T(8,128)S(1)}, f32[1,16,1024]{2,1,0:T(8,128)S(1)}, u32[]{:S(2)}, u32[]{:S(2)}) collective-permute-start(f32[1,16,1024]{2,1,0:T(8,128)S(1)} %get-tuple-element.21), channel_id=1, source_target_pairs={{8,16},{24,32},{40,48},{56,64},{72,80},{88,96},{104,112},{120,128}... | collective-permute-start | bytes 196616 | tf_op jit(solution)/shard_map/ppermute | solution.py:355
  5.6 10.0 %collective-permute-start.3 = (f32[1,16,1024]{2,1,0:T(8,128)S(1)}, f32[1,16,1024]{2,1,0:T(8,128)S(1)}, u32[]{:S(2)}, u32[]{:S(2)}) collective-permute-start(f32[1,16,1024]{2,1,0:T(8,128)S(1)} %get-tuple-element.23), channel_id=1, source_target_pairs={{0,8},{16,24},{32,40},{48,56},{64,72},{80,88},{96,104},{112,120},{... | collective-permute-start | bytes 196616 | tf_op jit(solution)/shard_map/ppermute | solution.py:355
  10.4 3.3 %collective-permute-start = (f32[4,1,1024]{2,1,0:T(1,128)S(1)}, f32[4,1,1024]{2,1,0:T(1,128)S(1)}, u32[]{:S(2)}, u32[]{:S(2)}) collective-permute-start(f32[4,1,1024]{2,1,0:T(1,128)S(1)} %get-tuple-element.20), channel_id=1, source_target_pairs={{1,2},{3,4},{5,6},{2,1},{4,3},{6,5},{9,10},{11,12},{13,14},{10,9},... | collective-permute-start | bytes 49160 | tf_op jit(solution)/shard_map/ppermute | solution.py:355
  11.1 4.5 %collective-permute-start.2 = (f32[4,1,1024]{2,1,0:T(1,128)S(1)}, f32[4,1,1024]{2,1,0:T(1,128)S(1)}, u32[]{:S(2)}, u32[]{:S(2)}) collective-permute-start(f32[4,1,1024]{2,1,0:T(1,128)S(1)} %get-tuple-element.22), channel_id=1, source_target_pairs={{0,1},{2,3},{4,5},{6,7},{1,0},{3,2},{5,4},{7,6},{8,9},{10,11},{12,... | collective-permute-start | bytes 49160 | tf_op jit(solution)/shard_map/ppermute | solution.py:355
  17.1 41.8 %all-to-all-start = ((f32[64,7,2,128]{3,2,1,0:T(2,128)}), f32[64,7,2,128]{3,2,1,0:T(2,128)S(1)}, u32[]{:S(2)}, u32[]{:S(2)}) async-start(f32[64,7,2,128]{3,2,1,0:T(2,128)} %bitcast), calls=%async_computation | async-start | bytes 917504 | tf_op jit(solution)/shard_map/all_to_all | solution.py:383
  31.5 22.3 %copy-start.1 = (f32[4,16,1024]{2,1,0:T(8,128)S(1)}, f32[4,16,1024]{2,1,0:T(8,128)}, u32[]{:S(2)}) copy-start(f32[4,16,1024]{2,1,0:T(8,128)} %vol.3) | copy-start | bytes 786436
  31.5 13.7 %collective-permute-start.4 = (f32[224,128]{1,0:T(8,128)S(1)}, f32[224,128]{1,0:T(8,128)S(1)}, u32[]{:S(2)}, u32[]{:S(2)}) collective-permute-start(f32[224,128]{1,0:T(8,128)S(1)} %get-tuple-element.26.refs_0_), channel_id=1, source_target_pairs={{0,2},{1,3},{2,0},{3,1},{4,6},{5,7},{6,4},{7,5},{8,10},{9,11},{10,... | collective-permute-start | bytes 344072 | tf_op jit(solution)/shard_map/ppermute | solution.py:388
  40.3 6.2 %collective-permute-start.5 = (f32[224,128]{1,0:T(8,128)S(1)}, f32[224,128]{1,0:T(8,128)S(1)}, u32[]{:S(2)}, u32[]{:S(2)}) collective-permute-start(f32[224,128]{1,0:T(8,128)S(1)} %get-tuple-element.26.refs_0_), channel_id=1, source_target_pairs={{0,1},{1,0},{2,3},{3,2},{4,5},{5,4},{6,7},{7,6},{8,9},{9,8},{10,11... | collective-permute-start | bytes 344072 | tf_op jit(solution)/shard_map/ppermute | solution.py:388
  43.3 6.7 %collective-permute-start.6 = (f32[224,128]{1,0:T(8,128)S(1)}, f32[224,128]{1,0:T(8,128)S(1)}, u32[]{:S(2)}, u32[]{:S(2)}) collective-permute-start(f32[224,128]{1,0:T(8,128)S(1)} %get-tuple-element.26.refs_0_), channel_id=1, source_target_pairs={{0,3},{1,2},{2,1},{3,0},{4,7},{5,6},{6,5},{7,4},{8,11},{9,10},{10,... | collective-permute-start | bytes 344072 | tf_op jit(solution)/shard_map/ppermute | solution.py:388
  50.2 8.8 %collective-permute-start.7 = (f32[96,128]{1,0:T(8,128)S(1)}, f32[96,128]{1,0:T(8,128)S(1)}, u32[]{:S(2)}, u32[]{:S(2)}) collective-permute-start(f32[96,128]{1,0:T(8,128)S(1)} %get-tuple-element.28), channel_id=1, source_target_pairs={{0,4},{1,5},{2,6},{3,7},{4,0},{5,1},{6,2},{7,3},{8,12},{9,13},{10,... | collective-permute-start | bytes 147464 | tf_op jit(solution)/shard_map/ppermute | solution.py:388
  59.9 24.4 %all-to-all-start.1 = ((f32[64,2,2,128]{3,2,1,0:T(2,128)}), f32[64,2,2,128]{3,2,1,0:T(2,128)S(1)}, u32[]{:S(2)}, u32[]{:S(2)}) async-start(f32[64,2,2,128]{3,2,1,0:T(2,128)} %bitcast.2), calls=%async_computation.1 | async-start | bytes 262144 | tf_op jit(solution)/shard_map/all_to_all | solution.py:413

commit v5 on v4

--- a/solution.py
+++ b/solution.py
@@ -18,6 +18,7 @@
 ROWS = INL * TILES
 GROUP = 8
 PORTS = 7
+WPORTS = INL + 2
 RUN = 4
 
 
@@ -136,10 +137,10 @@
             at = (slice(u * GROUP, (u + 1) * GROUP), lane_tile(t))
             v = [vol[(i, *at)] for i in range(INL)]
             k = [cond[(i, *at)] for i in range(INL)]
-            m0, d0, m1, d1, g, _ = condense([ones] * INL, v, links(k))
-            for p, value in enumerate((g, m0, m1, d0, d1, k[0], k[-1])):
-                start = t * GROUP * 2 * PORTS + p * 2 + u
-                wide_out[pl.ds(start, GROUP, stride=2 * PORTS), :] = value
+            _, d0, _, d1, _, _ = condense([ones] * INL, v, links(k))
+            for p, value in enumerate((*k, d0, d1)):
+                start = t * GROUP * 2 * WPORTS + p * 2 + u
+                wide_out[pl.ds(start, GROUP, stride=2 * WPORTS), :] = value
 
 
 def sublane_shift(x, s):
@@ -150,21 +151,24 @@
     part = WIDE // GROUP
     sub = iota((GROUP, LANES), 0)
     zero = jnp.zeros((GROUP, LANES), jnp.float32)
+    ones = jnp.ones((GROUP, LANES), jnp.float32)
     for u in range(2):
 
         def port(p, j):
-            return ports[pl.ds(j * 2 * PORTS + p * 2 + u, GROUP, stride=part * 2 * PORTS), :]
-
-        last_cond = sublane_shift(port(6, part - 1), 1)
+            return ports[pl.ds(j * 2 * WPORTS + p * 2 + u, GROUP, stride=part * 2 * WPORTS), :]
+
+        last_cond = sublane_shift(port(INL - 1, part - 1), 1)
         mass, rhs, link = [zero], [zero], []
         for j in range(part):
-            joined = half_weight * (last_cond + port(5, j))
+            k = [port(p, j) for p in range(INL)]
+            joined = half_weight * (last_cond + k[0])
             if j == 0:
                 joined = jnp.where(sub == 0, 0.0, joined)
-            link += [joined, port(0, j)]
-            mass += [port(1, j), port(2, j)]
-            rhs += [port(3, j), port(4, j)]
-            last_cond = port(6, j)
+            m0, _, m1, _, g, _ = condense([ones] * INL, [zero] * INL, links(k))
+            link += [joined, g]
+            mass += [m0, m1]
+            rhs += [port(INL, j), port(INL + 1, j)]
+            last_cond = k[-1]
         count = len(mass)
         m0, d0, m1, d1, g, steps = condense(mass, rhs, link)
         last = halving(
@@ -275,42 +279,64 @@
     return mass, rhs, link
 
 
-def merge_kernel(axes, own, by2, by1, by3, held, merged):
-    place = lax.rem(lax.axis_index(axes[1]), RUN)
-    for step, ref in enumerate((own, by1, by2, by3)):
-        held[place ^ step] = ref[...]
-    _, edge = facing(held, lax.axis_index(axes[1]) >= RUN)
-    for p, value in enumerate(edge):
-        merged[p * ROWS : (p + 1) * ROWS, :] = value
-
-
-def facing(held, high):
-    ports = [ports_of(held.at[n]) for n in range(RUN)]
-    m0, d0, m1, d1, g, steps = condense(*chain_of(ports))
-    here_m, here_d = jnp.where(high, m0, m1), jnp.where(high, d0, d1)
-    away_m, away_d = jnp.where(high, m1, m0), jnp.where(high, d1, d0)
+def in_order(mine, theirs, first):
+    return [
+        [jnp.where(first, a, b) for a, b in zip(mine, theirs)],
+        [jnp.where(first, b, a) for a, b in zip(mine, theirs)],
+    ]
+
+
+def places(axes):
+    rank = lax.axis_index(axes[1])
+    return lax.rem(rank, 2) == 0, lax.rem(rank, RUN) < 2, rank < RUN
+
+
+def join_kernel(axes, own, beside, joined):
+    pair = in_order(ports_of(own), ports_of(beside), places(axes)[0])
+    m0, d0, m1, d1, g, _ = condense(*chain_of(pair))
+    for p, value in enumerate((g, m0, m1, d0, d1, pair[0][5], pair[1][6])):
+        joined[p * ROWS : (p + 1) * ROWS, :] = value
+
+
+def facing(run, low):
+    m0, d0, m1, d1, g, steps = condense(*chain_of(run))
+    here_m, here_d = jnp.where(low, m1, m0), jnp.where(low, d1, d0)
+    away_m, away_d = jnp.where(low, m0, m1), jnp.where(low, d0, d1)
     inverse = 1.0 / (g + away_m)
     slope, base = g * inverse, away_d * inverse
-    edge = (here_m + slope * away_m, here_d + slope * away_d, jnp.where(high, ports[0][5], ports[-1][6]))
+    edge = (here_m + slope * away_m, here_d + slope * away_d, jnp.where(low, run[-1][6], run[0][5]))
     return (slope, base, steps), edge
 
 
-def cross_kernel(axes, held, other, cells_v, cells_c, timed, out, ends, cells_x):
-    rank = lax.axis_index(axes[1])
-    place, high = lax.rem(rank, RUN), rank >= RUN
-    (slope, base, steps), (m0, d0, c0) = facing(held, high)
+def edge_kernel(axes, joined, across, out):
+    _, second, low = places(axes)
+    _, edge = facing(in_order(ports_of(joined), ports_of(across), second), low)
+    for p, value in enumerate(edge):
+        out[p * ROWS : (p + 1) * ROWS, :] = value
+
+
+def half_of(x, first):
+    return jnp.where(first, x[0], x[2]), jnp.where(first, x[1], x[3])
+
+
+def cross_kernel(
+    axes, own, beside, joined, across, other, cells_v, cells_c, timed, out, cells_x
+):
+    first, second, low = places(axes)
+    run = in_order(ports_of(joined), ports_of(across), second)
+    (slope, base, steps), (m0, d0, c0) = facing(run, low)
     m1, d1, c1 = [other[p * ROWS : (p + 1) * ROWS, :] for p in range(3)]
     link = half_weight * (c0 + c1)
     here = (d0 * (m1 + link) + link * d1) / (m0 * m1 + link * (m0 + m1))
     away = base + slope * here
-    first, last = jnp.where(high, here, away), jnp.where(high, away, here)
-    for n, value in enumerate(expand(first, last, steps, 2 * RUN)):
-        ends[n] = value
+    x = expand(jnp.where(low, away, here), jnp.where(low, here, away), steps, 4)
+    steps = condense(*chain_of(in_order(ports_of(own), ports_of(beside), first)))[-1]
+    x = expand(*half_of(x, second), steps, 4)
     v = [cells_v[pl.ds(c * ROWS, ROWS), :] for c in range(CRS)]
     k = [cells_c[pl.ds(c * ROWS, ROWS), :] for c in range(CRS)]
     ones = jnp.ones((ROWS, LANES), jnp.float32)
     steps = condense([ones] * CRS, v, links(k))[-1]
-    x = expand(ends[2 * place], ends[2 * place + 1], steps, CRS)
+    x = expand(*half_of(x, first), steps, CRS)
     for c in range(CRS):
         cells_x[c * ROWS : (c + 1) * ROWS, :] = x[c]
     for i in range(INL):
@@ -369,7 +395,7 @@
         lambda *refs: prepare_kernel(axes, *refs),
         (
             f32(INL, CRS, NT),
-            f32(WIDE * PORTS * 2, LANES),
+            f32(WIDE * WPORTS * 2, LANES),
             f32(PORTS * ROWS, LANES),
             f32(cells, LANES),
             f32(cells, LANES),
@@ -381,19 +407,19 @@
         wide0,
     )
     lines = lax.all_to_all(
-        wide_ports.reshape(WIDE, PORTS, 2, LANES), wide_axes, split_axis=0, concat_axis=0, tiled=True
+        wide_ports.reshape(WIDE, WPORTS, 2, LANES), wide_axes, split_axis=0, concat_axis=0, tiled=True
     )
 
     def swapped(x, step):
         return lax.ppermute(x, narrow_axes, [(n, n ^ step) for n in range(NARROW)])
 
-    held, merged = call(
-        lambda *refs: merge_kernel(axes, *refs),
-        (f32(RUN, PORTS * ROWS, LANES), f32(3 * ROWS, LANES)),
-        narrow_ports,
-        *[swapped(narrow_ports, step) for step in (2, 1, 3)],
-    )
-    other = swapped(merged, RUN)
+    beside = swapped(narrow_ports, 1)
+    joined = call(
+        lambda *refs: join_kernel(axes, *refs), f32(PORTS * ROWS, LANES), narrow_ports, beside
+    )
+    across = swapped(joined, 2)
+    edge = call(lambda *refs: edge_kernel(axes, *refs), f32(3 * ROWS, LANES), joined, across)
+    other = swapped(edge, RUN)
     timed = call(
         time_kernel,
         f32(INL, CRS, NT),
@@ -406,9 +432,9 @@
             (3, NT // 2 // GROUP, LANES),
         ),
     )
-    lines, held, timed, other = lax.optimization_barrier((lines, held, timed, other))
+    lines, edge, timed = lax.optimization_barrier((lines, edge, timed))
     solved = call(
-        wide_kernel, f32(WIDE * 4, LANES), lines.reshape(WIDE * PORTS * 2, LANES)
+        wide_kernel, f32(WIDE * 4, LANES), lines.reshape(WIDE * WPORTS * 2, LANES)
     )
     ends = lax.all_to_all(
         solved.reshape(WIDE, 2, 2, LANES), wide_axes, split_axis=0, concat_axis=0, tiled=True
@@ -416,12 +442,15 @@
     others = call(
         lambda *refs: cross_kernel(axes, *refs),
         f32(INL, CRS, NT),
-        held,
+        narrow_ports,
+        beside,
+        joined,
+        across,
         other,
         cells_v,
         cells_c,
         timed,
-        scratch=((2 * RUN, ROWS, LANES), (cells, LANES)),
+        scratch=((cells, LANES),),
     )
     return call(
         finish_kernel, f32(INL, CRS, NT), volume, cond, ends.reshape(WIDE * 4, LANES), others

time: 85.5 us -> 74.8 us (0.87)
  waiting for transfers between devices: 21.1 us -> 10.1 us
    all_to_all x1, waiting for transfers between devices: 10.4 us -> 1.39 us  [per_device(): lax.all_to_all(solved.reshape(WIDE, 2, 2, LANES), wide_axes, split_axis=0...]
    ppermute x4 -> x3, waiting for transfers between devices: 8.8 us -> 6.85 us  [swapped(): return lax.ppermute(x, narrow_axes, [(n, n ^ step) for n in range(NARROW)])]
    ppermute x4 -> x3, starting transfers between devices: 17.4 us -> 19.1 us  [swapped(): return lax.ppermute(x, narrow_axes, [(n, n ^ step) for n in range(NARROW)])]
    all_to_all x1, starting transfers between devices: 13.5 us -> 11.9 us  [per_device(): lax.all_to_all(solved.reshape(WIDE, 2, 2, LANES), wide_axes, split_axis=0...]
    pallas_call x7 -> x8, Pallas kernels: 4.9 us -> 4.94 us  [call(): pl.pallas_call(kernel, out_shape=out, scratch_shapes=[pltpu.VMEM(s, jnp.f...]
  transfers between devices with their start and end apart: 10 -> 9, of which waited for: 5 -> 5; matrix products, arithmetic and copies ran while one was open for 0% -> 0% of each run, Pallas kernels for 2% -> 2%
where the time goes in v5:
time: 74.8 us; the launch traced here: 74.2 us
  starting transfers between devices  58.1 us (78%)
  waiting for transfers between devices  10.1 us (14%)
  Pallas kernels  4.94 us (7%)
  local copies, waits for them, and re-layouts  0.96 us (1%)
    ppermute x3, starting transfers between devices, swapped(): return lax.ppermute(x, narrow_axes, [(n, n ^ step) for n in range(NARROW)])  19.1 us
    all_to_all x1, starting transfers between devices, per_device(): lax.all_to_all(wide_ports.reshape(WIDE, WPORTS, 2, LANES), wide_axes, spl...  14.4 us
    ppermute x4, starting transfers between devices, exchanged(): return lax.ppermute(layer, axis, pairs + [(j, i) for i, j in pairs])  12.8 us
    all_to_all x1, starting transfers between devices, per_device(): lax.all_to_all(solved.reshape(WIDE, 2, 2, LANES), wide_axes, split_axis=0...  11.9 us
    ppermute x3, waiting for transfers between devices, swapped(): return lax.ppermute(x, narrow_axes, [(n, n ^ step) for n in range(NARROW)])  6.85 us
    pallas_call x8, Pallas kernels, call(): pl.pallas_call(kernel, out_shape=out, scratch_shapes=[pltpu.VMEM(s, jnp.f...  4.94 us
    ppermute x4, waiting for transfers between devices, exchanged(): return lax.ppermute(layer, axis, pairs + [(j, i) for i, j in pairs])  1.83 us
  transfers between devices with their start and end apart: 9, of which 5 were waited for; matrix products, arithmetic and copies ran while one was open for 0% of the time, Pallas kernels for 2%

profile of v5, /device:TPU:1, one launch (start us, length us, event | category | flops | bytes accessed | tf_op | source)
XLA Modules:
  0.0 74.2 jit_solution(16094967907492429458)
XLA Ops:
  0.0 0.0 copy-start
  0.0 0.9 %copy-done = f32[4,16,1024]{2,1,0:T(8,128)S(1)} copy-done((f32[4,16,1024]{2,1,0:T(8,128)S(1)}, f32[4,16,1024]{2,1,0:T(8,128)}, u32[]{:S(2)}) %copy-start) | copy-done | bytes 262168
  1.0 4.6 %collective-permute-start.1 = (f32[1,16,1024]{2,1,0:T(8,128)S(1)}, f32[1,16,1024]{2,1,0:T(8,128)S(1)}, u32[]{:S(2)}, u32[]{:S(2)}) collective-permute-start(f32[1,16,1024]{2,1,0:T(8,128)S(1)} %get-tuple-element.17), channel_id=1, source_target_pairs={{8,16},{24,32},{40,48},{56,64},{72,80},{88,96},{104,112},{120,128}... | collective-permute-start | bytes 196616 | tf_op jit(solution)/shard_map/ppermute | solution.py:381
  5.6 4.9 %collective-permute-start.3 = (f32[1,16,1024]{2,1,0:T(8,128)S(1)}, f32[1,16,1024]{2,1,0:T(8,128)S(1)}, u32[]{:S(2)}, u32[]{:S(2)}) collective-permute-start(f32[1,16,1024]{2,1,0:T(8,128)S(1)} %get-tuple-element.19), channel_id=1, source_target_pairs={{0,8},{16,24},{32,40},{48,56},{64,72},{80,88},{96,104},{112,120},{... | collective-permute-start | bytes 196616 | tf_op jit(solution)/shard_map/ppermute | solution.py:381
  10.4 0.7 collective-permute-start
  11.1 2.6 %collective-permute-start.2 = (f32[4,1,1024]{2,1,0:T(1,128)S(1)}, f32[4,1,1024]{2,1,0:T(1,128)S(1)}, u32[]{:S(2)}, u32[]{:S(2)}) collective-permute-start(f32[4,1,1024]{2,1,0:T(1,128)S(1)} %get-tuple-element.18), channel_id=1, source_target_pairs={{0,1},{2,3},{4,5},{6,7},{1,0},{3,2},{5,4},{7,6},{8,9},{10,11},{12,... | collective-permute-start | bytes 49160 | tf_op jit(solution)/shard_map/ppermute | solution.py:381
  13.8 0.0 collective-permute-done.refs_1_
  13.8 1.8 %collective-permute-done.2.refs_3_ = f32[4,1,1024]{2,1,0:T(1,128)S(1)} collective-permute-done((f32[4,1,1024]{2,1,0:T(1,128)S(1)}, f32[4,1,1024]{2,1,0:T(1,128)S(1)}, u32[]{:S(2)}, u32[]{:S(2)}) %collective-permute-start.2) | collective-permute-done | bytes 16416 | tf_op jit(solution)/shard_map/ppermute | solution.py:381
  15.6 0.0 collective-permute-done.1.refs_2_
  15.6 0.0 collective-permute-done.3.refs_4_
  15.6 1.5 %shard_map.18 = (f32[4,16,1024]{2,1,0:T(8,128)S(1)}, f32[768,128]{1,0:T(8,128)}, f32[224,128]{1,0:T(8,128)S(1)}, f32[512,128]{1,0:T(8,128)S(1)}, f32[512,128]{1,0:T(8,128)S(1)}) custom-call(f32[4,16,1024]{2,1,0:T(8,128)S(1)} %copy-done, f32[4,1,1024]{2,1,0:T(1,128)S(1)} %collective-permute-done.refs_1_, f32[1,16,1024]{2,1,0:T(8,128)S(1)} %collective-permute-done.1.refs_2_, ...), custom_call_target="tpu_custom_call" | custom-call | tf_op jit(solution)/shard_map/pallas_call | solution.py:368
  17.1 14.4 %all-to-all-start = ((f32[64,6,2,128]{3,2,1,0:T(2,128)}), f32[64,6,2,128]{3,2,1,0:T(2,128)S(1)}, u32[]{:S(2)}, u32[]{:S(2)}) async-start(f32[64,6,2,128]{3,2,1,0:T(2,128)} %bitcast), calls=%async_computation | async-start | bytes 786432 | tf_op jit(solution)/shard_map/all_to_all | solution.py:409
  31.5 0.0 copy-start.1
  31.5 3.8 %collective-permute-start.4 = (f32[224,128]{1,0:T(8,128)S(1)}, f32[224,128]{1,0:T(8,128)S(1)}, u32[]{:S(2)}, u32[]{:S(2)}) collective-permute-start(f32[224,128]{1,0:T(8,128)S(1)} %get-tuple-element.22.refs_0_), channel_id=1, source_target_pairs={{0,1},{1,0},{2,3},{3,2},{4,5},{5,4},{6,7},{7,6},{8,9},{9,8},{10,11... | collective-permute-start | bytes 344072 | tf_op jit(solution)/shard_map/ppermute | solution.py:414
  35.3 3.1 %collective-permute-done.4.refs_1_ = f32[224,128]{1,0:T(8,128)S(1)} collective-permute-done((f32[224,128]{1,0:T(8,128)S(1)}, f32[224,128]{1,0:T(8,128)S(1)}, u32[]{:S(2)}, u32[]{:S(2)}) %collective-permute-start.4) | collective-permute-done | bytes 114720 | tf_op jit(solution)/shard_map/ppermute | solution.py:414
  38.4 8.6 %collective-permute-start.5 = (f32[224,128]{1,0:T(8,128)S(1)}, f32[224,128]{1,0:T(8,128)S(1)}, u32[]{:S(2)}, u32[]{:S(2)}) collective-permute-start(f32[224,128]{1,0:T(8,128)S(1)} %shard_map.19.refs_0_.refs_2_), channel_id=1, source_target_pairs={{0,2},{1,3},{2,0},{3,1},{4,6},{5,7},{6,4},{7,5},{8,10},{9,11},{10,... | collective-permute-start | bytes 344072 | tf_op jit(solution)/shard_map/ppermute | solution.py:414
  47.0 0.0 copy-done.1
  47.0 1.1 %shard_map.21.refs_7_ = f32[4,16,1024]{2,1,0:T(8,128)S(1)} custom-call(f32[4,16,1024]{2,1,0:T(8,128)S(1)} %copy-done.1, f32[4,16,1024]{2,1,0:T(8,128)S(1)} %get-tuple-element.20.cond), custom_call_target="tpu_custom_call" | custom-call | tf_op jit(solution)/shard_map/pallas_call | solution.py:368
  48.1 1.4 %collective-permute-done.5.refs_1_.refs_3_ = f32[224,128]{1,0:T(8,128)S(1)} collective-permute-done((f32[224,128]{1,0:T(8,128)S(1)}, f32[224,128]{1,0:T(8,128)S(1)}, u32[]{:S(2)}, u32[]{:S(2)}) %collective-permute-start.5) | collective-permute-done | bytes 114720 | tf_op jit(solution)/shard_map/ppermute | solution.py:414
  49.6 0.0 all-to-all-done
  49.6 1.1 %shard_map.22 = f32[256,128]{1,0:T(8,128)} custom-call(f32[768,128]{1,0:T(8,128)S(1)} %bitcast.4), custom_call_target="tpu_custom_call" | custom-call | tf_op jit(solution)/shard_map/pallas_call | solution.py:368
  50.7 11.9 %all-to-all-start.1 = ((f32[64,2,2,128]{3,2,1,0:T(2,128)}), f32[64,2,2,128]{3,2,1,0:T(2,128)S(1)}, u32[]{:S(2)}, u32[]{:S(2)}) async-start(f32[64,2,2,128]{3,2,1,0:T(2,128)} %bitcast.2), calls=%async_computation.1 | async-start | bytes 262144 | tf_op jit(solution)/shard_map/all_to_all | solution.py:439
  62.6 6.7 %collective-permute-start.6 = (f32[96,128]{1,0:T(8,128)S(1)}, f32[96,128]{1,0:T(8,128)S(1)}, u32[]{:S(2)}, u32[]{:S(2)}) collective-permute-start(f32[96,128]{1,0:T(8,128)S(1)} %shard_map.20), channel_id=1, source_target_pairs={{0,4},{1,5},{2,6},{3,7},{4,0},{5,1},{6,2},{7,3},{8,12},{9,13},{10,... | collective-permute-start | bytes 147464 | tf_op jit(solution)/shard_map/ppermute | solution.py:414
  69.3 2.4 %collective-permute-done.6.refs_4_ = f32[96,128]{1,0:T(8,128)S(1)} collective-permute-done((f32[96,128]{1,0:T(8,128)S(1)}, f32[96,128]{1,0:T(8,128)S(1)}, u32[]{:S(2)}, u32[]{:S(2)}) %collective-permute-start.6) | collective-permute-done | bytes 49184 | tf_op jit(solution)/shard_map/ppermute | solution.py:414
  71.6 0.4 shard_map.23.others
  72.0 1.4 %all-to-all-done.1 = f32[64,2,2,128]{3,2,1,0:T(2,128)S(1)} async-done(((f32[64,2,2,128]{3,2,1,0:T(2,128)}), f32[64,2,2,128]{3,2,1,0:T(2,128)S(1)}, u32[]{:S(2)}, u32[]{:S(2)}) %all-to-all-start.1) | async-done | bytes 131104 | tf_op jit(solution)/shard_map/all_to_all | solution.py:439
  73.4 0.8 %shard_map.24 = f32[4,16,1024]{2,1,0:T(8,128)} custom-call(f32[4,16,1024]{2,1,0:T(8,128)S(1)} %copy-done.1, f32[4,16,1024]{2,1,0:T(8,128)S(1)} %get-tuple-element.20.cond, f32[256,128]{1,0:T(8,128)S(1)} %bitcast.5, f32[4,16,1024]{2,1,0:T(8,128)S(1)} %shard_map.23.others), custom_call_target="tpu_custom_call" | custom-call | tf_op jit(solution)/shard_map/pallas_call | solution.py:368
  (3 shorter events, 0.1 us)
Async XLA Ops:
  0.0 0.9 %copy-start = (f32[4,16,1024]{2,1,0:T(8,128)S(1)}, f32[4,16,1024]{2,1,0:T(8,128)}, u32[]{:S(2)}) copy-start(f32[4,16,1024]{2,1,0:T(8,128)} %vol.3) | copy-start | bytes 786436
  1.0 14.6 %collective-permute-start.1 = (f32[1,16,1024]{2,1,0:T(8,128)S(1)}, f32[1,16,1024]{2,1,0:T(8,128)S(1)}, u32[]{:S(2)}, u32[]{:S(2)}) collective-permute-start(f32[1,16,1024]{2,1,0:T(8,128)S(1)} %get-tuple-element.17), channel_id=1, source_target_pairs={{8,16},{24,32},{40,48},{56,64},{72,80},{88,96},{104,112},{120,128}... | collective-permute-start | bytes 196616 | tf_op jit(solution)/shard_map/ppermute | solution.py:381
  5.6 10.0 %collective-permute-start.3 = (f32[1,16,1024]{2,1,0:T(8,128)S(1)}, f32[1,16,1024]{2,1,0:T(8,128)S(1)}, u32[]{:S(2)}, u32[]{:S(2)}) collective-permute-start(f32[1,16,1024]{2,1,0:T(8,128)S(1)} %get-tuple-element.19), channel_id=1, source_target_pairs={{0,8},{16,24},{32,40},{48,56},{64,72},{80,88},{96,104},{112,120},{... | collective-permute-start | bytes 196616 | tf_op jit(solution)/shard_map/ppermute | solution.py:381
  10.4 3.3 %collective-permute-start = (f32[4,1,1024]{2,1,0:T(1,128)S(1)}, f32[4,1,1024]{2,1,0:T(1,128)S(1)}, u32[]{:S(2)}, u32[]{:S(2)}) collective-permute-start(f32[4,1,1024]{2,1,0:T(1,128)S(1)} %get-tuple-element.16), channel_id=1, source_target_pairs={{1,2},{3,4},{5,6},{2,1},{4,3},{6,5},{9,10},{11,12},{13,14},{10,9},... | collective-permute-start | bytes 49160 | tf_op jit(solution)/shard_map/ppermute | solution.py:381
  11.1 4.5 %collective-permute-start.2 = (f32[4,1,1024]{2,1,0:T(1,128)S(1)}, f32[4,1,1024]{2,1,0:T(1,128)S(1)}, u32[]{:S(2)}, u32[]{:S(2)}) collective-permute-start(f32[4,1,1024]{2,1,0:T(1,128)S(1)} %get-tuple-element.18), channel_id=1, source_target_pairs={{0,1},{2,3},{4,5},{6,7},{1,0},{3,2},{5,4},{7,6},{8,9},{10,11},{12,... | collective-permute-start | bytes 49160 | tf_op jit(solution)/shard_map/ppermute | solution.py:381
  17.1 32.5 %all-to-all-start = ((f32[64,6,2,128]{3,2,1,0:T(2,128)}), f32[64,6,2,128]{3,2,1,0:T(2,128)S(1)}, u32[]{:S(2)}, u32[]{:S(2)}) async-start(f32[64,6,2,128]{3,2,1,0:T(2,128)} %bitcast), calls=%async_computation | async-start | bytes 786432 | tf_op jit(solution)/shard_map/all_to_all | solution.py:409
  31.5 15.6 %copy-start.1 = (f32[4,16,1024]{2,1,0:T(8,128)S(1)}, f32[4,16,1024]{2,1,0:T(8,128)}, u32[]{:S(2)}) copy-start(f32[4,16,1024]{2,1,0:T(8,128)} %vol.3) | copy-start | bytes 786436
  31.5 6.9 %collective-permute-start.4 = (f32[224,128]{1,0:T(8,128)S(1)}, f32[224,128]{1,0:T(8,128)S(1)}, u32[]{:S(2)}, u32[]{:S(2)}) collective-permute-start(f32[224,128]{1,0:T(8,128)S(1)} %get-tuple-element.22.refs_0_), channel_id=1, source_target_pairs={{0,1},{1,0},{2,3},{3,2},{4,5},{5,4},{6,7},{7,6},{8,9},{9,8},{10,11... | collective-permute-start | bytes 344072 | tf_op jit(solution)/shard_map/ppermute | solution.py:414
  38.4 11.1 %collective-permute-start.5 = (f32[224,128]{1,0:T(8,128)S(1)}, f32[224,128]{1,0:T(8,128)S(1)}, u32[]{:S(2)}, u32[]{:S(2)}) collective-permute-start(f32[224,128]{1,0:T(8,128)S(1)} %shard_map.19.refs_0_.refs_2_), channel_id=1, source_target_pairs={{0,2},{1,3},{2,0},{3,1},{4,6},{5,7},{6,4},{7,5},{8,10},{9,11},{10,... | collective-permute-start | bytes 344072 | tf_op jit(solution)/shard_map/ppermute | solution.py:414
  50.7 22.8 %all-to-all-start.1 = ((f32[64,2,2,128]{3,2,1,0:T(2,128)}), f32[64,2,2,128]{3,2,1,0:T(2,128)S(1)}, u32[]{:S(2)}, u32[]{:S(2)}) async-start(f32[64,2,2,128]{3,2,1,0:T(2,128)} %bitcast.2), calls=%async_computation.1 | async-start | bytes 262144 | tf_op jit(solution)/shard_map/all_to_all | solution.py:439
  62.6 9.0 %collective-permute-start.6 = (f32[96,128]{1,0:T(8,128)S(1)}, f32[96,128]{1,0:T(8,128)S(1)}, u32[]{:S(2)}, u32[]{:S(2)}) collective-permute-start(f32[96,128]{1,0:T(8,128)S(1)} %shard_map.20), channel_id=1, source_target_pairs={{0,4},{1,5},{2,6},{3,7},{4,0},{5,1},{6,2},{7,3},{8,12},{9,13},{10,... | collective-permute-start | bytes 147464 | tf_op jit(solution)/shard_map/ppermute | solution.py:414

commit v6 on v5

--- a/solution.py
+++ b/solution.py
@@ -86,6 +86,8 @@
         first, last = vol[i, :1], vol[i, CRS - 1 :]
         narrow1[i] = jnp.where(narrow_even, first, last)
         narrow0[i] = jnp.where(narrow_even, last, first)
+    for ref in (narrow1, narrow0):
+        ref[INL:] = jnp.zeros((CRS + 1 - INL, 1, NT), jnp.float32)
 
 
 def prepare_kernel(
@@ -380,10 +382,10 @@
         pairs = [(i, i + 1) for i in range(start, count - 1, 2)]
         return lax.ppermute(layer, axis, pairs + [(j, i) for i, j in pairs])
 
-    inline_face, cross_face = f32(1, CRS, NT), f32(INL, 1, NT)
+    inline_face, longer = f32(1, CRS, NT), f32(CRS + 1, 1, NT)
     narrow1, wide1, narrow0, wide0 = call(
         lambda *refs: faces_kernel(axes, *refs),
-        (cross_face, inline_face, cross_face, inline_face),
+        (longer, inline_face, longer, inline_face),
         volume,
     )
     narrow1 = exchanged(narrow1, narrow_axes, NARROW, 1)
@@ -417,7 +419,7 @@
     joined = call(
         lambda *refs: join_kernel(axes, *refs), f32(PORTS * ROWS, LANES), narrow_ports, beside
     )
-    across = swapped(joined, 2)
+    across = swapped(joined, 3)
     edge = call(lambda *refs: edge_kernel(axes, *refs), f32(3 * ROWS, LANES), joined, across)
     other = swapped(edge, RUN)
     timed = call(
@@ -432,7 +434,7 @@
             (3, NT // 2 // GROUP, LANES),
         ),
     )
-    lines, edge, timed = lax.optimization_barrier((lines, edge, timed))
+    lines, edge = lax.optimization_barrier((lines, edge))
     solved = call(
         wide_kernel, f32(WIDE * 4, LANES), lines.reshape(WIDE * WPORTS * 2, LANES)
     )

time: 74.8 us -> 72.8 us (0.973)
  starting transfers between devices: 58.1 us -> 53.5 us
  waiting for transfers between devices: 10.1 us -> 12.9 us
    ppermute x3, starting transfers between devices: 19.1 us -> 13.6 us  [swapped(): return lax.ppermute(x, narrow_axes, [(n, n ^ step) for n in range(NARROW)])]
    ppermute x3, waiting for transfers between devices: 6.85 us -> 9.62 us  [swapped(): return lax.ppermute(x, narrow_axes, [(n, n ^ step) for n in range(NARROW)])]
    all_to_all x1, starting transfers between devices: 14.4 us -> 15.2 us  [per_device(): lax.all_to_all(wide_ports.reshape(WIDE, WPORTS, 2, LANES), wide_axes, spl...]
  transfers between devices with their start and end apart: 9 -> 9, of which waited for: 5 -> 6; matrix products, arithmetic and copies ran while one was open for 0% -> 0% of each run, Pallas kernels for 2% -> 2%
where the time goes in v6:
time: 72.8 us; the launch traced here: 72.4 us
  starting transfers between devices  53.5 us (73%)
  waiting for transfers between devices  12.9 us (18%)
  Pallas kernels  4.95 us (7%)
  local copies, waits for them, and re-layouts  0.95 us (1%)
    all_to_all x1, starting transfers between devices, per_device(): lax.all_to_all(wide_ports.reshape(WIDE, WPORTS, 2, LANES), wide_axes, spl...  15.2 us
    ppermute x3, starting transfers between devices, swapped(): return lax.ppermute(x, narrow_axes, [(n, n ^ step) for n in range(NARROW)])  13.6 us
    ppermute x4, starting transfers between devices, exchanged(): return lax.ppermute(layer, axis, pairs + [(j, i) for i, j in pairs])  13.3 us
    all_to_all x1, starting transfers between devices, per_device(): lax.all_to_all(solved.reshape(WIDE, 2, 2, LANES), wide_axes, split_axis=0...  11.4 us
    ppermute x3, waiting for transfers between devices, swapped(): return lax.ppermute(x, narrow_axes, [(n, n ^ step) for n in range(NARROW)])  9.62 us
    pallas_call x8, Pallas kernels, call(): pl.pallas_call(kernel, out_shape=out, scratch_shapes=[pltpu.VMEM(s, jnp.f...  4.95 us
  transfers between devices with their start and end apart: 9, of which 6 were waited for; matrix products, arithmetic and copies ran while one was open for 0% of the time, Pallas kernels for 2%

profile of v6, /device:TPU:1, one launch (start us, length us, event | category | flops | bytes accessed | tf_op | source)
XLA Modules:
  0.0 72.4 jit_solution(7511657949294420995)
XLA Ops:
  0.0 0.0 copy-start
  0.0 0.9 %copy-done = f32[4,16,1024]{2,1,0:T(8,128)S(1)} copy-done((f32[4,16,1024]{2,1,0:T(8,128)S(1)}, f32[4,16,1024]{2,1,0:T(8,128)}, u32[]{:S(2)}) %copy-start) | copy-done | bytes 262168
  1.0 0.7 collective-permute-start
  1.7 6.4 %collective-permute-start.2 = (f32[17,1,1024]{2,1,0:T(1,128)S(1)}, f32[17,1,1024]{2,1,0:T(1,128)S(1)}, u32[]{:S(2)}, u32[]{:S(2)}) collective-permute-start(f32[17,1,1024]{2,1,0:T(1,128)S(1)} %get-tuple-element.17), channel_id=1, source_target_pairs={{0,1},{2,3},{4,5},{6,7},{1,0},{3,2},{5,4},{7,6},{8,9},{10,11},{12,... | collective-permute-start | bytes 208904 | tf_op jit(solution)/shard_map/ppermute | solution.py:383
  8.1 4.3 %collective-permute-start.1 = (f32[1,16,1024]{2,1,0:T(8,128)S(1)}, f32[1,16,1024]{2,1,0:T(8,128)S(1)}, u32[]{:S(2)}, u32[]{:S(2)}) collective-permute-start(f32[1,16,1024]{2,1,0:T(8,128)S(1)} %get-tuple-element.16), channel_id=1, source_target_pairs={{8,16},{24,32},{40,48},{56,64},{72,80},{88,96},{104,112},{120,128}... | collective-permute-start | bytes 196616 | tf_op jit(solution)/shard_map/ppermute | solution.py:383
  12.4 1.9 %collective-permute-start.3 = (f32[1,16,1024]{2,1,0:T(8,128)S(1)}, f32[1,16,1024]{2,1,0:T(8,128)S(1)}, u32[]{:S(2)}, u32[]{:S(2)}) collective-permute-start(f32[1,16,1024]{2,1,0:T(8,128)S(1)} %get-tuple-element.18), channel_id=1, source_target_pairs={{0,8},{16,24},{32,40},{48,56},{64,72},{80,88},{96,104},{112,120},{... | collective-permute-start | bytes 196616 | tf_op jit(solution)/shard_map/ppermute | solution.py:383
  14.3 0.0 collective-permute-done.1.refs_2_
  14.3 1.2 %collective-permute-done.3.refs_4_ = f32[1,16,1024]{2,1,0:T(8,128)S(1)} collective-permute-done((f32[1,16,1024]{2,1,0:T(8,128)S(1)}, f32[1,16,1024]{2,1,0:T(8,128)S(1)}, u32[]{:S(2)}, u32[]{:S(2)}) %collective-permute-start.3) | collective-permute-done | bytes 65568 | tf_op jit(solution)/shard_map/ppermute | solution.py:383
  15.5 0.0 collective-permute-done.refs_1_
  15.6 0.0 collective-permute-done.2.refs_3_
  15.6 1.5 %shard_map.18 = (f32[4,16,1024]{2,1,0:T(8,128)S(1)}, f32[768,128]{1,0:T(8,128)}, f32[224,128]{1,0:T(8,128)S(1)}, f32[512,128]{1,0:T(8,128)S(1)}, f32[512,128]{1,0:T(8,128)S(1)}) custom-call(f32[4,16,1024]{2,1,0:T(8,128)S(1)} %copy-done, f32[17,1,1024]{2,1,0:T(1,128)S(1)} %collective-permute-done.refs_1_, f32[1,16,1024]{2,1,0:T(8,128)S(1)} %collective-permute-done.1.refs_2_, ...), custom_call_target="tpu_custom_call" | custom-call | tf_op jit(solution)/shard_map/pallas_call | solution.py:370
  17.0 15.2 %all-to-all-start = ((f32[64,6,2,128]{3,2,1,0:T(2,128)}), f32[64,6,2,128]{3,2,1,0:T(2,128)S(1)}, u32[]{:S(2)}, u32[]{:S(2)}) async-start(f32[64,6,2,128]{3,2,1,0:T(2,128)} %bitcast), calls=%async_computation | async-start | bytes 786432 | tf_op jit(solution)/shard_map/all_to_all | solution.py:411
  32.2 1.9 %collective-permute-start.4 = (f32[224,128]{1,0:T(8,128)S(1)}, f32[224,128]{1,0:T(8,128)S(1)}, u32[]{:S(2)}, u32[]{:S(2)}) collective-permute-start(f32[224,128]{1,0:T(8,128)S(1)} %get-tuple-element.21.refs_0_), channel_id=1, source_target_pairs={{0,1},{1,0},{2,3},{3,2},{4,5},{5,4},{6,7},{7,6},{8,9},{9,8},{10,11... | collective-permute-start | bytes 344072 | tf_op jit(solution)/shard_map/ppermute | solution.py:416
  34.2 4.2 %collective-permute-done.4.refs_1_ = f32[224,128]{1,0:T(8,128)S(1)} collective-permute-done((f32[224,128]{1,0:T(8,128)S(1)}, f32[224,128]{1,0:T(8,128)S(1)}, u32[]{:S(2)}, u32[]{:S(2)}) %collective-permute-start.4) | collective-permute-done | bytes 114720 | tf_op jit(solution)/shard_map/ppermute | solution.py:416
  38.4 6.6 %collective-permute-start.5 = (f32[224,128]{1,0:T(8,128)S(1)}, f32[224,128]{1,0:T(8,128)S(1)}, u32[]{:S(2)}, u32[]{:S(2)}) collective-permute-start(f32[224,128]{1,0:T(8,128)S(1)} %shard_map.19.refs_0_.refs_2_), channel_id=1, source_target_pairs={{0,3},{1,2},{2,1},{3,0},{4,7},{5,6},{6,5},{7,4},{8,11},{9,10},{10,... | collective-permute-start | bytes 344072 | tf_op jit(solution)/shard_map/ppermute | solution.py:416
  45.1 2.5 %collective-permute-done.5.refs_1_.refs_3_ = f32[224,128]{1,0:T(8,128)S(1)} collective-permute-done((f32[224,128]{1,0:T(8,128)S(1)}, f32[224,128]{1,0:T(8,128)S(1)}, u32[]{:S(2)}, u32[]{:S(2)}) %collective-permute-start.5) | collective-permute-done | bytes 114720 | tf_op jit(solution)/shard_map/ppermute | solution.py:416
  47.7 0.7 all-to-all-done
  48.4 1.1 %shard_map.21 = f32[256,128]{1,0:T(8,128)} custom-call(f32[768,128]{1,0:T(8,128)S(1)} %bitcast.4), custom_call_target="tpu_custom_call" | custom-call | tf_op jit(solution)/shard_map/pallas_call | solution.py:370
  49.4 0.0 copy-start.1
  49.4 11.4 %all-to-all-start.1 = ((f32[64,2,2,128]{3,2,1,0:T(2,128)}), f32[64,2,2,128]{3,2,1,0:T(2,128)S(1)}, u32[]{:S(2)}, u32[]{:S(2)}) async-start(f32[64,2,2,128]{3,2,1,0:T(2,128)} %bitcast.2), calls=%async_computation.1 | async-start | bytes 262144 | tf_op jit(solution)/shard_map/all_to_all | solution.py:441
  60.8 5.0 %collective-permute-start.6 = (f32[96,128]{1,0:T(8,128)S(1)}, f32[96,128]{1,0:T(8,128)S(1)}, u32[]{:S(2)}, u32[]{:S(2)}) collective-permute-start(f32[96,128]{1,0:T(8,128)S(1)} %shard_map.20), channel_id=1, source_target_pairs={{0,4},{1,5},{2,6},{3,7},{4,0},{5,1},{6,2},{7,3},{8,12},{9,13},{10,... | collective-permute-start | bytes 147464 | tf_op jit(solution)/shard_map/ppermute | solution.py:416
  65.8 0.0 copy-done.1
  65.8 1.1 %shard_map.22.refs_7_ = f32[4,16,1024]{2,1,0:T(8,128)S(1)} custom-call(f32[4,16,1024]{2,1,0:T(8,128)S(1)} %copy-done.1, f32[4,16,1024]{2,1,0:T(8,128)S(1)} %get-tuple-element.19.cond), custom_call_target="tpu_custom_call" | custom-call | tf_op jit(solution)/shard_map/pallas_call | solution.py:370
  66.9 2.9 %collective-permute-done.6.refs_4_ = f32[96,128]{1,0:T(8,128)S(1)} collective-permute-done((f32[96,128]{1,0:T(8,128)S(1)}, f32[96,128]{1,0:T(8,128)S(1)}, u32[]{:S(2)}, u32[]{:S(2)}) %collective-permute-start.6) | collective-permute-done | bytes 49184 | tf_op jit(solution)/shard_map/ppermute | solution.py:416
  69.8 0.4 shard_map.23.others
  70.2 1.4 %all-to-all-done.1 = f32[64,2,2,128]{3,2,1,0:T(2,128)S(1)} async-done(((f32[64,2,2,128]{3,2,1,0:T(2,128)}), f32[64,2,2,128]{3,2,1,0:T(2,128)S(1)}, u32[]{:S(2)}, u32[]{:S(2)}) %all-to-all-start.1) | async-done | bytes 131104 | tf_op jit(solution)/shard_map/all_to_all | solution.py:441
  71.6 0.8 %shard_map.24 = f32[4,16,1024]{2,1,0:T(8,128)} custom-call(f32[4,16,1024]{2,1,0:T(8,128)S(1)} %copy-done.1, f32[4,16,1024]{2,1,0:T(8,128)S(1)} %get-tuple-element.19.cond, f32[256,128]{1,0:T(8,128)S(1)} %bitcast.5, f32[4,16,1024]{2,1,0:T(8,128)S(1)} %shard_map.23.others), custom_call_target="tpu_custom_call" | custom-call | tf_op jit(solution)/shard_map/pallas_call | solution.py:370
  (3 shorter events, 0.1 us)
Async XLA Ops:
  0.0 0.9 %copy-start = (f32[4,16,1024]{2,1,0:T(8,128)S(1)}, f32[4,16,1024]{2,1,0:T(8,128)}, u32[]{:S(2)}) copy-start(f32[4,16,1024]{2,1,0:T(8,128)} %vol.3) | copy-start | bytes 786436
  1.0 14.6 %collective-permute-start = (f32[17,1,1024]{2,1,0:T(1,128)S(1)}, f32[17,1,1024]{2,1,0:T(1,128)S(1)}, u32[]{:S(2)}, u32[]{:S(2)}) collective-permute-start(f32[17,1,1024]{2,1,0:T(1,128)S(1)} %get-tuple-element.15), channel_id=1, source_target_pairs={{1,2},{3,4},{5,6},{2,1},{4,3},{6,5},{9,10},{11,12},{13,14},{10,9},... | collective-permute-start | bytes 208904 | tf_op jit(solution)/shard_map/ppermute | solution.py:383
  1.7 13.9 %collective-permute-start.2 = (f32[17,1,1024]{2,1,0:T(1,128)S(1)}, f32[17,1,1024]{2,1,0:T(1,128)S(1)}, u32[]{:S(2)}, u32[]{:S(2)}) collective-permute-start(f32[17,1,1024]{2,1,0:T(1,128)S(1)} %get-tuple-element.17), channel_id=1, source_target_pairs={{0,1},{2,3},{4,5},{6,7},{1,0},{3,2},{5,4},{7,6},{8,9},{10,11},{12,... | collective-permute-start | bytes 208904 | tf_op jit(solution)/shard_map/ppermute | solution.py:383
  8.1 6.3 %collective-permute-start.1 = (f32[1,16,1024]{2,1,0:T(8,128)S(1)}, f32[1,16,1024]{2,1,0:T(8,128)S(1)}, u32[]{:S(2)}, u32[]{:S(2)}) collective-permute-start(f32[1,16,1024]{2,1,0:T(8,128)S(1)} %get-tuple-element.16), channel_id=1, source_target_pairs={{8,16},{24,32},{40,48},{56,64},{72,80},{88,96},{104,112},{120,128}... | collective-permute-start | bytes 196616 | tf_op jit(solution)/shard_map/ppermute | solution.py:383
  12.4 3.1 %collective-permute-start.3 = (f32[1,16,1024]{2,1,0:T(8,128)S(1)}, f32[1,16,1024]{2,1,0:T(8,128)S(1)}, u32[]{:S(2)}, u32[]{:S(2)}) collective-permute-start(f32[1,16,1024]{2,1,0:T(8,128)S(1)} %get-tuple-element.18), channel_id=1, source_target_pairs={{0,8},{16,24},{32,40},{48,56},{64,72},{80,88},{96,104},{112,120},{... | collective-permute-start | bytes 196616 | tf_op jit(solution)/shard_map/ppermute | solution.py:383
  17.0 31.3 %all-to-all-start = ((f32[64,6,2,128]{3,2,1,0:T(2,128)}), f32[64,6,2,128]{3,2,1,0:T(2,128)S(1)}, u32[]{:S(2)}, u32[]{:S(2)}) async-start(f32[64,6,2,128]{3,2,1,0:T(2,128)} %bitcast), calls=%async_computation | async-start | bytes 786432 | tf_op jit(solution)/shard_map/all_to_all | solution.py:411
  32.2 6.2 %collective-permute-start.4 = (f32[224,128]{1,0:T(8,128)S(1)}, f32[224,128]{1,0:T(8,128)S(1)}, u32[]{:S(2)}, u32[]{:S(2)}) collective-permute-start(f32[224,128]{1,0:T(8,128)S(1)} %get-tuple-element.21.refs_0_), channel_id=1, source_target_pairs={{0,1},{1,0},{2,3},{3,2},{4,5},{5,4},{6,7},{7,6},{8,9},{9,8},{10,11... | collective-permute-start | bytes 344072 | tf_op jit(solution)/shard_map/ppermute | solution.py:416
  38.4 9.1 %collective-permute-start.5 = (f32[224,128]{1,0:T(8,128)S(1)}, f32[224,128]{1,0:T(8,128)S(1)}, u32[]{:S(2)}, u32[]{:S(2)}) collective-permute-start(f32[224,128]{1,0:T(8,128)S(1)} %shard_map.19.refs_0_.refs_2_), channel_id=1, source_target_pairs={{0,3},{1,2},{2,1},{3,0},{4,7},{5,6},{6,5},{7,4},{8,11},{9,10},{10,... | collective-permute-start | bytes 344072 | tf_op jit(solution)/shard_map/ppermute | solution.py:416
  49.4 16.4 %copy-start.1 = (f32[4,16,1024]{2,1,0:T(8,128)S(1)}, f32[4,16,1024]{2,1,0:T(8,128)}, u32[]{:S(2)}) copy-start(f32[4,16,1024]{2,1,0:T(8,128)} %vol.3) | copy-start | bytes 786436
  49.4 22.2 %all-to-all-start.1 = ((f32[64,2,2,128]{3,2,1,0:T(2,128)}), f32[64,2,2,128]{3,2,1,0:T(2,128)S(1)}, u32[]{:S(2)}, u32[]{:S(2)}) async-start(f32[64,2,2,128]{3,2,1,0:T(2,128)} %bitcast.2), calls=%async_computation.1 | async-start | bytes 262144 | tf_op jit(solution)/shard_map/all_to_all | solution.py:441
  60.8 9.0 %collective-permute-start.6 = (f32[96,128]{1,0:T(8,128)S(1)}, f32[96,128]{1,0:T(8,128)S(1)}, u32[]{:S(2)}, u32[]{:S(2)}) collective-permute-start(f32[96,128]{1,0:T(8,128)S(1)} %shard_map.20), channel_id=1, source_target_pairs={{0,4},{1,5},{2,6},{3,7},{4,0},{5,1},{6,2},{7,3},{8,12},{9,13},{10,... | collective-permute-start | bytes 147464 | tf_op jit(solution)/shard_map/ppermute | solution.py:416

commit v7 on v6

--- a/solution.py
+++ b/solution.py
@@ -90,42 +90,52 @@
         ref[INL:] = jnp.zeros((CRS + 1 - INL, 1, NT), jnp.float32)
 
 
-def prepare_kernel(
-    axes, vol, narrow1, wide1, narrow0, wide0, cond, wide_out, narrow_out, cells_v, cells_c
-):
-    wide_axes, narrow_axes = axes
-    wide_rank, narrow_rank = lax.axis_index(wide_axes), lax.axis_index(narrow_axes)
-    wide_even, narrow_even = lax.rem(wide_rank, 2) == 0, lax.rem(narrow_rank, 2) == 0
+def conductivity(power):
+    return contrast_sq / (contrast_sq + power)
+
+
+def partial_kernel(axes, vol, narrow1, narrow0, partial, cells_v):
+    rank = lax.axis_index(axes[1])
+    even = lax.rem(rank, 2) == 0
     col = iota((CRS, NT), 1)
     row = iota((CRS, NT), 0)
     for i in range(INL):
         here = vol[i]
-        if i == 0:
-            up = jnp.where(wide_even, wide1[0], wide0[0])
-            up = jnp.where(wide_rank == 0, here, up)
-        else:
-            up = vol[i - 1]
-        if i == INL - 1:
-            down = jnp.where(wide_even, wide0[0], wide1[0])
-            down = jnp.where(wide_rank == WIDE - 1, here, down)
-        else:
-            down = vol[i + 1]
-        power = (0.5 * (down - up)) ** 2
-        edge = jnp.where(narrow_even, narrow1[i], narrow0[i])
-        edge = jnp.where(narrow_rank == 0, here[:1], edge)
+        edge = jnp.where(even, narrow1[i], narrow0[i])
+        edge = jnp.where(rank == 0, here[:1], edge)
         lower = jnp.where(row == 0, edge, pltpu.roll(here, 1, 0))
-        edge = jnp.where(narrow_even, narrow0[i], narrow1[i])
-        edge = jnp.where(narrow_rank == NARROW - 1, here[CRS - 1 :], edge)
+        edge = jnp.where(even, narrow0[i], narrow1[i])
+        edge = jnp.where(rank == NARROW - 1, here[CRS - 1 :], edge)
         upper = jnp.where(row == CRS - 1, edge, pltpu.roll(here, CRS - 1, 0))
-        power = power + (0.5 * (upper - lower)) ** 2
+        power = (0.5 * (upper - lower)) ** 2
         earlier = jnp.where(col == 0, here, pltpu.roll(here, 1, 1))
         later = jnp.where(col == NT - 1, here, pltpu.roll(here, NT - 1, 1))
         power = power + (0.5 * (later - earlier)) ** 2
-        value = contrast_sq / (contrast_sq + power)
+        if 0 < i < INL - 1:
+            power = conductivity(power + (0.5 * (vol[i + 1] - vol[i - 1])) ** 2)
+        partial[i] = power
+        for t in range(TILES):
+            cells_v[pl.ds(i * TILES + t, CRS, stride=ROWS), :] = here[:, lane_tile(t)]
+
+
+def prepare_kernel(
+    axes, vol, partial, cells_v, wide1, wide0, cond, wide_out, narrow_out, cells_c
+):
+    rank = lax.axis_index(axes[0])
+    even = lax.rem(rank, 2) == 0
+    for i in range(INL):
+        value = partial[i]
+        if i == 0:
+            up = jnp.where(even, wide1[0], wide0[0])
+            up = jnp.where(rank == 0, vol[0], up)
+            value = conductivity(value + (0.5 * (vol[1] - up)) ** 2)
+        if i == INL - 1:
+            down = jnp.where(even, wide0[0], wide1[0])
+            down = jnp.where(rank == WIDE - 1, vol[INL - 1], down)
+            value = conductivity(value + (0.5 * (down - vol[INL - 2])) ** 2)
         cond[i] = value
         for t in range(TILES):
             where = pl.ds(i * TILES + t, CRS, stride=ROWS)
-            cells_v[where, :] = here[:, lane_tile(t)]
             cells_c[where, :] = value[:, lane_tile(t)]
     ones = jnp.ones((ROWS, LANES), jnp.float32)
     v = [cells_v[pl.ds(c * ROWS, ROWS), :] for c in range(CRS)]
@@ -393,19 +403,25 @@
     narrow0 = exchanged(narrow0, narrow_axes, NARROW, 0)
     wide0 = exchanged(wide0, wide_axes, WIDE, 0)
     cells = CRS * ROWS
-    cond, wide_ports, narrow_ports, cells_v, cells_c = call(
+    partial, cells_v = call(
+        lambda *refs: partial_kernel(axes, *refs),
+        (f32(INL, CRS, NT), f32(cells, LANES)),
+        volume,
+        narrow1,
+        narrow0,
+    )
+    cond, wide_ports, narrow_ports, cells_c = call(
         lambda *refs: prepare_kernel(axes, *refs),
         (
             f32(INL, CRS, NT),
             f32(WIDE * WPORTS * 2, LANES),
             f32(PORTS * ROWS, LANES),
             f32(cells, LANES),
-            f32(cells, LANES),
         ),
         volume,
-        narrow1,
+        partial,
+        cells_v,
         wide1,
-        narrow0,
         wide0,
     )
     lines = lax.all_to_all(

time: 72.8 us -> 72.5 us (level)
    pallas_call x8 -> x9, Pallas kernels: 4.95 us -> 5.04 us  [call(): pl.pallas_call(kernel, out_shape=out, scratch_shapes=[pltpu.VMEM(s, jnp.f...]
  transfers between devices with their start and end apart: 9 -> 9, of which waited for: 6 -> 6; matrix products, arithmetic and copies ran while one was open for 0% -> 0% of each run, Pallas kernels for 2% -> 3%
where the time goes in v7:
time: 72.5 us; the launch traced here: 72.1 us
  starting transfers between devices  53.5 us (74%)
  waiting for transfers between devices  12.5 us (17%)
  Pallas kernels  5.04 us (7%)
  local copies, waits for them, and re-layouts  0.95 us (1%)
    all_to_all x1, starting transfers between devices, per_device(): lax.all_to_all(wide_ports.reshape(WIDE, WPORTS, 2, LANES), wide_axes, spl...  15.2 us
    ppermute x3, starting transfers between devices, swapped(): return lax.ppermute(x, narrow_axes, [(n, n ^ step) for n in range(NARROW)])  13.6 us
    ppermute x4, starting transfers between devices, exchanged(): return lax.ppermute(layer, axis, pairs + [(j, i) for i, j in pairs])  13.3 us
    all_to_all x1, starting transfers between devices, per_device(): lax.all_to_all(solved.reshape(WIDE, 2, 2, LANES), wide_axes, split_axis=0...  11.4 us
    ppermute x3, waiting for transfers between devices, swapped(): return lax.ppermute(x, narrow_axes, [(n, n ^ step) for n in range(NARROW)])  9.62 us
    pallas_call x9, Pallas kernels, call(): pl.pallas_call(kernel, out_shape=out, scratch_shapes=[pltpu.VMEM(s, jnp.f...  5.04 us
  transfers between devices with their start and end apart: 9, of which 6 were waited for; matrix products, arithmetic and copies ran while one was open for 0% of the time, Pallas kernels for 3%

profile of v7, /device:TPU:1, one launch (start us, length us, event | category | flops | bytes accessed | tf_op | source)
XLA Modules:
  0.0 72.1 jit_solution(17831868231207649576)
XLA Ops:
  0.0 0.0 copy-start
  0.0 0.9 %copy-done = f32[4,16,1024]{2,1,0:T(8,128)S(1)} copy-done((f32[4,16,1024]{2,1,0:T(8,128)S(1)}, f32[4,16,1024]{2,1,0:T(8,128)}, u32[]{:S(2)}) %copy-start) | copy-done | bytes 262168
  1.0 0.7 collective-permute-start
  1.7 6.4 %collective-permute-start.1 = (f32[17,1,1024]{2,1,0:T(1,128)S(1)}, f32[17,1,1024]{2,1,0:T(1,128)S(1)}, u32[]{:S(2)}, u32[]{:S(2)}) collective-permute-start(f32[17,1,1024]{2,1,0:T(1,128)S(1)} %get-tuple-element.17), channel_id=1, source_target_pairs={{0,1},{2,3},{4,5},{6,7},{1,0},{3,2},{5,4},{7,6},{8,9},{10,11},{12,... | collective-permute-start | bytes 208904 | tf_op jit(solution)/shard_map/ppermute | solution.py:393
  8.1 4.3 %collective-permute-start.2 = (f32[1,16,1024]{2,1,0:T(8,128)S(1)}, f32[1,16,1024]{2,1,0:T(8,128)S(1)}, u32[]{:S(2)}, u32[]{:S(2)}) collective-permute-start(f32[1,16,1024]{2,1,0:T(8,128)S(1)} %get-tuple-element.20), channel_id=1, source_target_pairs={{8,16},{24,32},{40,48},{56,64},{72,80},{88,96},{104,112},{120,128}... | collective-permute-start | bytes 196616 | tf_op jit(solution)/shard_map/ppermute | solution.py:393
  12.4 1.9 %collective-permute-start.3 = (f32[1,16,1024]{2,1,0:T(8,128)S(1)}, f32[1,16,1024]{2,1,0:T(8,128)S(1)}, u32[]{:S(2)}, u32[]{:S(2)}) collective-permute-start(f32[1,16,1024]{2,1,0:T(8,128)S(1)} %get-tuple-element.21), channel_id=1, source_target_pairs={{0,8},{16,24},{32,40},{48,56},{64,72},{80,88},{96,104},{112,120},{... | collective-permute-start | bytes 196616 | tf_op jit(solution)/shard_map/ppermute | solution.py:393
  14.3 0.0 collective-permute-done.refs_1_
  14.3 0.0 collective-permute-done.1.refs_2_
  14.3 0.4 shard_map.18
  14.8 0.0 collective-permute-done.2.refs_3_
  14.8 0.8 %collective-permute-done.3.refs_4_ = f32[1,16,1024]{2,1,0:T(8,128)S(1)} collective-permute-done((f32[1,16,1024]{2,1,0:T(8,128)S(1)}, f32[1,16,1024]{2,1,0:T(8,128)S(1)}, u32[]{:S(2)}, u32[]{:S(2)}) %collective-permute-start.3) | collective-permute-done | bytes 65568 | tf_op jit(solution)/shard_map/ppermute | solution.py:393
  15.5 1.2 %shard_map.19 = (f32[4,16,1024]{2,1,0:T(8,128)S(1)}, f32[768,128]{1,0:T(8,128)}, f32[224,128]{1,0:T(8,128)S(1)}, f32[512,128]{1,0:T(8,128)S(1)}) custom-call(f32[4,16,1024]{2,1,0:T(8,128)S(1)} %copy-done, f32[4,16,1024]{2,1,0:T(8,128)S(1)} %get-tuple-element.18.refs_1_, f32[512,128]{1,0:T(8,128)S(1)} %get-tuple-element.19.refs_2_.refs_5_, ...), custom_call_target="tpu_custom_call" | custom-call | tf_op jit(solution)/shard_map/pallas_call | solution.py:380
  16.7 15.2 %all-to-all-start = ((f32[64,6,2,128]{3,2,1,0:T(2,128)}), f32[64,6,2,128]{3,2,1,0:T(2,128)S(1)}, u32[]{:S(2)}, u32[]{:S(2)}) async-start(f32[64,6,2,128]{3,2,1,0:T(2,128)} %bitcast), calls=%async_computation | async-start | bytes 786432 | tf_op jit(solution)/shard_map/all_to_all | solution.py:427
  31.9 1.9 %collective-permute-start.4 = (f32[224,128]{1,0:T(8,128)S(1)}, f32[224,128]{1,0:T(8,128)S(1)}, u32[]{:S(2)}, u32[]{:S(2)}) collective-permute-start(f32[224,128]{1,0:T(8,128)S(1)} %get-tuple-element.24.refs_0_), channel_id=1, source_target_pairs={{0,1},{1,0},{2,3},{3,2},{4,5},{5,4},{6,7},{7,6},{8,9},{9,8},{10,11... | collective-permute-start | bytes 344072 | tf_op jit(solution)/shard_map/ppermute | solution.py:432
  33.9 4.2 %collective-permute-done.4.refs_1_ = f32[224,128]{1,0:T(8,128)S(1)} collective-permute-done((f32[224,128]{1,0:T(8,128)S(1)}, f32[224,128]{1,0:T(8,128)S(1)}, u32[]{:S(2)}, u32[]{:S(2)}) %collective-permute-start.4) | collective-permute-done | bytes 114720 | tf_op jit(solution)/shard_map/ppermute | solution.py:432
  38.1 6.6 %collective-permute-start.5 = (f32[224,128]{1,0:T(8,128)S(1)}, f32[224,128]{1,0:T(8,128)S(1)}, u32[]{:S(2)}, u32[]{:S(2)}) collective-permute-start(f32[224,128]{1,0:T(8,128)S(1)} %shard_map.20.refs_0_.refs_2_), channel_id=1, source_target_pairs={{0,3},{1,2},{2,1},{3,0},{4,7},{5,6},{6,5},{7,4},{8,11},{9,10},{10,... | collective-permute-start | bytes 344072 | tf_op jit(solution)/shard_map/ppermute | solution.py:432
  44.8 2.5 %collective-permute-done.5.refs_1_.refs_3_ = f32[224,128]{1,0:T(8,128)S(1)} collective-permute-done((f32[224,128]{1,0:T(8,128)S(1)}, f32[224,128]{1,0:T(8,128)S(1)}, u32[]{:S(2)}, u32[]{:S(2)}) %collective-permute-start.5) | collective-permute-done | bytes 114720 | tf_op jit(solution)/shard_map/ppermute | solution.py:432
  47.3 0.7 all-to-all-done
  48.0 1.1 %shard_map.22 = f32[256,128]{1,0:T(8,128)} custom-call(f32[768,128]{1,0:T(8,128)S(1)} %bitcast.4), custom_call_target="tpu_custom_call" | custom-call | tf_op jit(solution)/shard_map/pallas_call | solution.py:380
  49.1 0.0 copy-start.1
  49.1 11.4 %all-to-all-start.1 = ((f32[64,2,2,128]{3,2,1,0:T(2,128)}), f32[64,2,2,128]{3,2,1,0:T(2,128)S(1)}, u32[]{:S(2)}, u32[]{:S(2)}) async-start(f32[64,2,2,128]{3,2,1,0:T(2,128)} %bitcast.2), calls=%async_computation.1 | async-start | bytes 262144 | tf_op jit(solution)/shard_map/all_to_all | solution.py:457
  60.5 5.0 %collective-permute-start.6 = (f32[96,128]{1,0:T(8,128)S(1)}, f32[96,128]{1,0:T(8,128)S(1)}, u32[]{:S(2)}, u32[]{:S(2)}) collective-permute-start(f32[96,128]{1,0:T(8,128)S(1)} %shard_map.21), channel_id=1, source_target_pairs={{0,4},{1,5},{2,6},{3,7},{4,0},{5,1},{6,2},{7,3},{8,12},{9,13},{10,... | collective-permute-start | bytes 147464 | tf_op jit(solution)/shard_map/ppermute | solution.py:432
  65.5 0.0 copy-done.1
  65.5 1.1 %shard_map.23.refs_7_ = f32[4,16,1024]{2,1,0:T(8,128)S(1)} custom-call(f32[4,16,1024]{2,1,0:T(8,128)S(1)} %copy-done.1, f32[4,16,1024]{2,1,0:T(8,128)S(1)} %get-tuple-element.22.cond), custom_call_target="tpu_custom_call" | custom-call | tf_op jit(solution)/shard_map/pallas_call | solution.py:380
  66.6 2.9 %collective-permute-done.6.refs_4_ = f32[96,128]{1,0:T(8,128)S(1)} collective-permute-done((f32[96,128]{1,0:T(8,128)S(1)}, f32[96,128]{1,0:T(8,128)S(1)}, u32[]{:S(2)}, u32[]{:S(2)}) %collective-permute-start.6) | collective-permute-done | bytes 49184 | tf_op jit(solution)/shard_map/ppermute | solution.py:432
  69.5 0.4 shard_map.24.others
  69.9 1.4 %all-to-all-done.1 = f32[64,2,2,128]{3,2,1,0:T(2,128)S(1)} async-done(((f32[64,2,2,128]{3,2,1,0:T(2,128)}), f32[64,2,2,128]{3,2,1,0:T(2,128)S(1)}, u32[]{:S(2)}, u32[]{:S(2)}) %all-to-all-start.1) | async-done | bytes 131104 | tf_op jit(solution)/shard_map/all_to_all | solution.py:457
  71.3 0.8 %shard_map.25 = f32[4,16,1024]{2,1,0:T(8,128)} custom-call(f32[4,16,1024]{2,1,0:T(8,128)S(1)} %copy-done.1, f32[4,16,1024]{2,1,0:T(8,128)S(1)} %get-tuple-element.22.cond, f32[256,128]{1,0:T(8,128)S(1)} %bitcast.5, f32[4,16,1024]{2,1,0:T(8,128)S(1)} %shard_map.24.others), custom_call_target="tpu_custom_call" | custom-call | tf_op jit(solution)/shard_map/pallas_call | solution.py:380
  (3 shorter events, 0.1 us)
Async XLA Ops:
  0.0 0.9 %copy-start = (f32[4,16,1024]{2,1,0:T(8,128)S(1)}, f32[4,16,1024]{2,1,0:T(8,128)}, u32[]{:S(2)}) copy-start(f32[4,16,1024]{2,1,0:T(8,128)} %vol.3) | copy-start | bytes 786436
  1.0 13.3 %collective-permute-start = (f32[17,1,1024]{2,1,0:T(1,128)S(1)}, f32[17,1,1024]{2,1,0:T(1,128)S(1)}, u32[]{:S(2)}, u32[]{:S(2)}) collective-permute-start(f32[17,1,1024]{2,1,0:T(1,128)S(1)} %get-tuple-element.16), channel_id=1, source_target_pairs={{1,2},{3,4},{5,6},{2,1},{4,3},{6,5},{9,10},{11,12},{13,14},{10,9},... | collective-permute-start | bytes 208904 | tf_op jit(solution)/shard_map/ppermute | solution.py:393
  1.7 12.7 %collective-permute-start.1 = (f32[17,1,1024]{2,1,0:T(1,128)S(1)}, f32[17,1,1024]{2,1,0:T(1,128)S(1)}, u32[]{:S(2)}, u32[]{:S(2)}) collective-permute-start(f32[17,1,1024]{2,1,0:T(1,128)S(1)} %get-tuple-element.17), channel_id=1, source_target_pairs={{0,1},{2,3},{4,5},{6,7},{1,0},{3,2},{5,4},{7,6},{8,9},{10,11},{12,... | collective-permute-start | bytes 208904 | tf_op jit(solution)/shard_map/ppermute | solution.py:393
  8.1 6.7 %collective-permute-start.2 = (f32[1,16,1024]{2,1,0:T(8,128)S(1)}, f32[1,16,1024]{2,1,0:T(8,128)S(1)}, u32[]{:S(2)}, u32[]{:S(2)}) collective-permute-start(f32[1,16,1024]{2,1,0:T(8,128)S(1)} %get-tuple-element.20), channel_id=1, source_target_pairs={{8,16},{24,32},{40,48},{56,64},{72,80},{88,96},{104,112},{120,128}... | collective-permute-start | bytes 196616 | tf_op jit(solution)/shard_map/ppermute | solution.py:393
  12.4 3.1 %collective-permute-start.3 = (f32[1,16,1024]{2,1,0:T(8,128)S(1)}, f32[1,16,1024]{2,1,0:T(8,128)S(1)}, u32[]{:S(2)}, u32[]{:S(2)}) collective-permute-start(f32[1,16,1024]{2,1,0:T(8,128)S(1)} %get-tuple-element.21), channel_id=1, source_target_pairs={{0,8},{16,24},{32,40},{48,56},{64,72},{80,88},{96,104},{112,120},{... | collective-permute-start | bytes 196616 | tf_op jit(solution)/shard_map/ppermute | solution.py:393
  16.7 31.3 %all-to-all-start = ((f32[64,6,2,128]{3,2,1,0:T(2,128)}), f32[64,6,2,128]{3,2,1,0:T(2,128)S(1)}, u32[]{:S(2)}, u32[]{:S(2)}) async-start(f32[64,6,2,128]{3,2,1,0:T(2,128)} %bitcast), calls=%async_computation | async-start | bytes 786432 | tf_op jit(solution)/shard_map/all_to_all | solution.py:427
  31.9 6.2 %collective-permute-start.4 = (f32[224,128]{1,0:T(8,128)S(1)}, f32[224,128]{1,0:T(8,128)S(1)}, u32[]{:S(2)}, u32[]{:S(2)}) collective-permute-start(f32[224,128]{1,0:T(8,128)S(1)} %get-tuple-element.24.refs_0_), channel_id=1, source_target_pairs={{0,1},{1,0},{2,3},{3,2},{4,5},{5,4},{6,7},{7,6},{8,9},{9,8},{10,11... | collective-permute-start | bytes 344072 | tf_op jit(solution)/shard_map/ppermute | solution.py:432
  38.1 9.1 %collective-permute-start.5 = (f32[224,128]{1,0:T(8,128)S(1)}, f32[224,128]{1,0:T(8,128)S(1)}, u32[]{:S(2)}, u32[]{:S(2)}) collective-permute-start(f32[224,128]{1,0:T(8,128)S(1)} %shard_map.20.refs_0_.refs_2_), channel_id=1, source_target_pairs={{0,3},{1,2},{2,1},{3,0},{4,7},{5,6},{6,5},{7,4},{8,11},{9,10},{10,... | collective-permute-start | bytes 344072 | tf_op jit(solution)/shard_map/ppermute | solution.py:432
  49.1 16.4 %copy-start.1 = (f32[4,16,1024]{2,1,0:T(8,128)S(1)}, f32[4,16,1024]{2,1,0:T(8,128)}, u32[]{:S(2)}) copy-start(f32[4,16,1024]{2,1,0:T(8,128)} %vol.3) | copy-start | bytes 786436
  49.1 22.2 %all-to-all-start.1 = ((f32[64,2,2,128]{3,2,1,0:T(2,128)}), f32[64,2,2,128]{3,2,1,0:T(2,128)S(1)}, u32[]{:S(2)}, u32[]{:S(2)}) async-start(f32[64,2,2,128]{3,2,1,0:T(2,128)} %bitcast.2), calls=%async_computation.1 | async-start | bytes 262144 | tf_op jit(solution)/shard_map/all_to_all | solution.py:457
  60.5 9.0 %collective-permute-start.6 = (f32[96,128]{1,0:T(8,128)S(1)}, f32[96,128]{1,0:T(8,128)S(1)}, u32[]{:S(2)}, u32[]{:S(2)}) collective-permute-start(f32[96,128]{1,0:T(8,128)S(1)} %shard_map.21), channel_id=1, source_target_pairs={{0,4},{1,5},{2,6},{3,7},{4,0},{5,1},{6,2},{7,3},{8,12},{9,13},{10,... | collective-permute-start | bytes 147464 | tf_op jit(solution)/shard_map/ppermute | solution.py:432

commit v8 on v7

--- a/solution.py
+++ b/solution.py
@@ -197,7 +197,19 @@
                 out[pl.ds(j * 4 + e * 2 + u, GROUP, stride=part * 4), :] = x[1 + 2 * j + e]
 
 
-def time_kernel(vol, cond, out, cells_v, cells_c, link_s, tmp):
+def time_kernel(vol, cond, out, inner, cells_v, cells_c, link_s, tmp):
+    ones = jnp.ones((GROUP, LANES), jnp.float32)
+    for t in range(TILES):
+        for u in range(CRS // GROUP):
+            at = (slice(u * GROUP, (u + 1) * GROUP), lane_tile(t))
+            v = [vol[(i, *at)] for i in range(INL)]
+            k = [cond[(i, *at)] for i in range(INL)]
+            near, far = condense([ones] * INL, v, links(k))[-1]
+            _, _, _, a1, c1, b1 = near
+            _, _, _, a2, c2, b2 = far
+            found = (b1 + c1 * b2, a1 + c1 * a2, c1 * c2, b2, a2, c2)
+            for p, value in enumerate(found):
+                inner[(p, *at)] = value
     lines = INL * CRS
     half = NT // 2
     blocks = half // LANES
@@ -358,17 +370,18 @@
             )
 
 
-def finish_kernel(vol, cond, ends, others, out):
-    ones = jnp.ones((GROUP, LANES), jnp.float32)
+def finish_kernel(inner, ends, others, out):
     for t in range(TILES):
         for u in range(CRS // GROUP):
             at = (slice(u * GROUP, (u + 1) * GROUP), lane_tile(t))
-            v = [vol[(i, *at)] for i in range(INL)]
-            k = [cond[(i, *at)] for i in range(INL)]
-            steps = condense([ones] * INL, v, links(k))[-1]
             first = ends[pl.ds(t * GROUP * 4 + u, GROUP, stride=4), :]
             last = ends[pl.ds(t * GROUP * 4 + 2 + u, GROUP, stride=4), :]
-            for i, x in enumerate(expand(first, last, steps, INL)):
+            base, to_first, to_last, base2, to_first2, to_last2 = [
+                inner[(p, *at)] for p in range(6)
+            ]
+            second = base + to_first * first + to_last * last
+            third = base2 + to_first2 * first + to_last2 * last
+            for i, x in enumerate((first, second, third, last)):
                 out[(i, *at)] = (x + others[(i, *at)]) * (1.0 / 3.0)
 
 
@@ -438,9 +451,9 @@
     across = swapped(joined, 3)
     edge = call(lambda *refs: edge_kernel(axes, *refs), f32(3 * ROWS, LANES), joined, across)
     other = swapped(edge, RUN)
-    timed = call(
+    timed, inner = call(
         time_kernel,
-        f32(INL, CRS, NT),
+        (f32(INL, CRS, NT), f32(6, CRS, NT)),
         volume,
         cond,
         scratch=(
@@ -471,7 +484,7 @@
         scratch=((cells, LANES),),
     )
     return call(
-        finish_kernel, f32(INL, CRS, NT), volume, cond, ends.reshape(WIDE * 4, LANES), others
+        finish_kernel, f32(INL, CRS, NT), inner, ends.reshape(WIDE * 4, LANES), others
     )
 
 

time: 72.5 us -> 72.5 us (level)
  no operation moved by 1% of the time
where the time goes in v8:
time: 72.5 us; the launch traced here: 72.1 us
  starting transfers between devices  53.5 us (74%)
  waiting for transfers between devices  12.5 us (17%)
  Pallas kernels  5.02 us (7%)
  local copies, waits for them, and re-layouts  0.95 us (1%)
    all_to_all x1, starting transfers between devices, per_device(): lax.all_to_all(wide_ports.reshape(WIDE, WPORTS, 2, LANES), wide_axes, spl...  15.2 us
    ppermute x3, starting transfers between devices, swapped(): return lax.ppermute(x, narrow_axes, [(n, n ^ step) for n in range(NARROW)])  13.6 us
    ppermute x4, starting transfers between devices, exchanged(): return lax.ppermute(layer, axis, pairs + [(j, i) for i, j in pairs])  13.3 us
    all_to_all x1, starting transfers between devices, per_device(): lax.all_to_all(solved.reshape(WIDE, 2, 2, LANES), wide_axes, split_axis=0...  11.4 us
    ppermute x3, waiting for transfers between devices, swapped(): return lax.ppermute(x, narrow_axes, [(n, n ^ step) for n in range(NARROW)])  9.6 us
    pallas_call x9, Pallas kernels, call(): pl.pallas_call(kernel, out_shape=out, scratch_shapes=[pltpu.VMEM(s, jnp.f...  5.02 us
  transfers between devices with their start and end apart: 9, of which 6 were waited for; matrix products, arithmetic and copies ran while one was open for 0% of the time, Pallas kernels for 3%

profile of v8, /device:TPU:1, one launch (start us, length us, event | category | flops | bytes accessed | tf_op | source)
XLA Modules:
  0.0 72.1 jit_solution(12858981374567843530)
XLA Ops:
  0.0 0.0 copy-start
  0.0 0.9 %copy-done = f32[4,16,1024]{2,1,0:T(8,128)S(1)} copy-done((f32[4,16,1024]{2,1,0:T(8,128)S(1)}, f32[4,16,1024]{2,1,0:T(8,128)}, u32[]{:S(2)}) %copy-start) | copy-done | bytes 262168
  1.0 0.7 collective-permute-start
  1.7 6.4 %collective-permute-start.1 = (f32[17,1,1024]{2,1,0:T(1,128)S(1)}, f32[17,1,1024]{2,1,0:T(1,128)S(1)}, u32[]{:S(2)}, u32[]{:S(2)}) collective-permute-start(f32[17,1,1024]{2,1,0:T(1,128)S(1)} %get-tuple-element.19), channel_id=1, source_target_pairs={{0,1},{2,3},{4,5},{6,7},{1,0},{3,2},{5,4},{7,6},{8,9},{10,11},{12,... | collective-permute-start | bytes 208904 | tf_op jit(solution)/shard_map/ppermute | solution.py:406
  8.1 4.3 %collective-permute-start.2 = (f32[1,16,1024]{2,1,0:T(8,128)S(1)}, f32[1,16,1024]{2,1,0:T(8,128)S(1)}, u32[]{:S(2)}, u32[]{:S(2)}) collective-permute-start(f32[1,16,1024]{2,1,0:T(8,128)S(1)} %get-tuple-element.22), channel_id=1, source_target_pairs={{8,16},{24,32},{40,48},{56,64},{72,80},{88,96},{104,112},{120,128}... | collective-permute-start | bytes 196616 | tf_op jit(solution)/shard_map/ppermute | solution.py:406
  12.4 1.9 %collective-permute-start.3 = (f32[1,16,1024]{2,1,0:T(8,128)S(1)}, f32[1,16,1024]{2,1,0:T(8,128)S(1)}, u32[]{:S(2)}, u32[]{:S(2)}) collective-permute-start(f32[1,16,1024]{2,1,0:T(8,128)S(1)} %get-tuple-element.23), channel_id=1, source_target_pairs={{0,8},{16,24},{32,40},{48,56},{64,72},{80,88},{96,104},{112,120},{... | collective-permute-start | bytes 196616 | tf_op jit(solution)/shard_map/ppermute | solution.py:406
  14.3 0.0 collective-permute-done.refs_1_
  14.3 0.0 collective-permute-done.1.refs_2_
  14.3 0.4 shard_map.18
  14.8 0.0 collective-permute-done.2.refs_3_
  14.8 0.8 %collective-permute-done.3.refs_4_ = f32[1,16,1024]{2,1,0:T(8,128)S(1)} collective-permute-done((f32[1,16,1024]{2,1,0:T(8,128)S(1)}, f32[1,16,1024]{2,1,0:T(8,128)S(1)}, u32[]{:S(2)}, u32[]{:S(2)}) %collective-permute-start.3) | collective-permute-done | bytes 65568 | tf_op jit(solution)/shard_map/ppermute | solution.py:406
  15.5 1.2 %shard_map.19 = (f32[4,16,1024]{2,1,0:T(8,128)S(1)}, f32[768,128]{1,0:T(8,128)}, f32[224,128]{1,0:T(8,128)S(1)}, f32[512,128]{1,0:T(8,128)S(1)}) custom-call(f32[4,16,1024]{2,1,0:T(8,128)S(1)} %copy-done, f32[4,16,1024]{2,1,0:T(8,128)S(1)} %get-tuple-element.20.refs_1_, f32[512,128]{1,0:T(8,128)S(1)} %get-tuple-element.21.refs_2_.refs_5_, ...), custom_call_target="tpu_custom_call" | custom-call | tf_op jit(solution)/shard_map/pallas_call | solution.py:393
  16.7 15.2 %all-to-all-start = ((f32[64,6,2,128]{3,2,1,0:T(2,128)}), f32[64,6,2,128]{3,2,1,0:T(2,128)S(1)}, u32[]{:S(2)}, u32[]{:S(2)}) async-start(f32[64,6,2,128]{3,2,1,0:T(2,128)} %bitcast), calls=%async_computation | async-start | bytes 786432 | tf_op jit(solution)/shard_map/all_to_all | solution.py:440
  31.9 1.9 %collective-permute-start.4 = (f32[224,128]{1,0:T(8,128)S(1)}, f32[224,128]{1,0:T(8,128)S(1)}, u32[]{:S(2)}, u32[]{:S(2)}) collective-permute-start(f32[224,128]{1,0:T(8,128)S(1)} %get-tuple-element.27.refs_0_), channel_id=1, source_target_pairs={{0,1},{1,0},{2,3},{3,2},{4,5},{5,4},{6,7},{7,6},{8,9},{9,8},{10,11... | collective-permute-start | bytes 344072 | tf_op jit(solution)/shard_map/ppermute | solution.py:445
  33.9 4.2 %collective-permute-done.4.refs_1_ = f32[224,128]{1,0:T(8,128)S(1)} collective-permute-done((f32[224,128]{1,0:T(8,128)S(1)}, f32[224,128]{1,0:T(8,128)S(1)}, u32[]{:S(2)}, u32[]{:S(2)}) %collective-permute-start.4) | collective-permute-done | bytes 114720 | tf_op jit(solution)/shard_map/ppermute | solution.py:445
  38.1 6.6 %collective-permute-start.5 = (f32[224,128]{1,0:T(8,128)S(1)}, f32[224,128]{1,0:T(8,128)S(1)}, u32[]{:S(2)}, u32[]{:S(2)}) collective-permute-start(f32[224,128]{1,0:T(8,128)S(1)} %shard_map.21.refs_0_.refs_2_), channel_id=1, source_target_pairs={{0,3},{1,2},{2,1},{3,0},{4,7},{5,6},{6,5},{7,4},{8,11},{9,10},{10,... | collective-permute-start | bytes 344072 | tf_op jit(solution)/shard_map/ppermute | solution.py:445
  44.8 2.5 %collective-permute-done.5.refs_1_.refs_3_ = f32[224,128]{1,0:T(8,128)S(1)} collective-permute-done((f32[224,128]{1,0:T(8,128)S(1)}, f32[224,128]{1,0:T(8,128)S(1)}, u32[]{:S(2)}, u32[]{:S(2)}) %collective-permute-start.5) | collective-permute-done | bytes 114720 | tf_op jit(solution)/shard_map/ppermute | solution.py:445
  47.4 0.7 all-to-all-done
  48.1 1.1 %shard_map.23 = f32[256,128]{1,0:T(8,128)} custom-call(f32[768,128]{1,0:T(8,128)S(1)} %bitcast.4), custom_call_target="tpu_custom_call" | custom-call | tf_op jit(solution)/shard_map/pallas_call | solution.py:393
  49.1 0.0 copy-start.1
  49.1 11.4 %all-to-all-start.1 = ((f32[64,2,2,128]{3,2,1,0:T(2,128)}), f32[64,2,2,128]{3,2,1,0:T(2,128)S(1)}, u32[]{:S(2)}, u32[]{:S(2)}) async-start(f32[64,2,2,128]{3,2,1,0:T(2,128)} %bitcast.2), calls=%async_computation.1 | async-start | bytes 262144 | tf_op jit(solution)/shard_map/all_to_all | solution.py:470
  60.5 5.0 %collective-permute-start.6 = (f32[96,128]{1,0:T(8,128)S(1)}, f32[96,128]{1,0:T(8,128)S(1)}, u32[]{:S(2)}, u32[]{:S(2)}) collective-permute-start(f32[96,128]{1,0:T(8,128)S(1)} %shard_map.22), channel_id=1, source_target_pairs={{0,4},{1,5},{2,6},{3,7},{4,0},{5,1},{6,2},{7,3},{8,12},{9,13},{10,... | collective-permute-start | bytes 147464 | tf_op jit(solution)/shard_map/ppermute | solution.py:445
  65.5 0.0 copy-done.1
  65.5 1.1 %shard_map.20 = (f32[4,16,1024]{2,1,0:T(8,128)S(1)}, f32[6,16,1024]{2,1,0:T(8,128)S(1)}) custom-call(f32[4,16,1024]{2,1,0:T(8,128)S(1)} %copy-done.1, f32[4,16,1024]{2,1,0:T(8,128)S(1)} %get-tuple-element.24.cond), custom_call_target="tpu_custom_call" | custom-call | tf_op jit(solution)/shard_map/pallas_call | solution.py:393
  66.7 2.9 %collective-permute-done.6.refs_4_ = f32[96,128]{1,0:T(8,128)S(1)} collective-permute-done((f32[96,128]{1,0:T(8,128)S(1)}, f32[96,128]{1,0:T(8,128)S(1)}, u32[]{:S(2)}, u32[]{:S(2)}) %collective-permute-start.6) | collective-permute-done | bytes 49184 | tf_op jit(solution)/shard_map/ppermute | solution.py:445
  69.5 0.4 shard_map.24.others
  69.9 1.4 %all-to-all-done.1 = f32[64,2,2,128]{3,2,1,0:T(2,128)S(1)} async-done(((f32[64,2,2,128]{3,2,1,0:T(2,128)}), f32[64,2,2,128]{3,2,1,0:T(2,128)S(1)}, u32[]{:S(2)}, u32[]{:S(2)}) %all-to-all-start.1) | async-done | bytes 131104 | tf_op jit(solution)/shard_map/all_to_all | solution.py:470
  71.3 0.8 %shard_map.25 = f32[4,16,1024]{2,1,0:T(8,128)} custom-call(f32[6,16,1024]{2,1,0:T(8,128)S(1)} %get-tuple-element.25.inner, f32[256,128]{1,0:T(8,128)S(1)} %bitcast.5, f32[4,16,1024]{2,1,0:T(8,128)S(1)} %shard_map.24.others), custom_call_target="tpu_custom_call" | custom-call | tf_op jit(solution)/shard_map/pallas_call | solution.py:393
  (3 shorter events, 0.1 us)
Async XLA Ops:
  0.0 0.9 %copy-start = (f32[4,16,1024]{2,1,0:T(8,128)S(1)}, f32[4,16,1024]{2,1,0:T(8,128)}, u32[]{:S(2)}) copy-start(f32[4,16,1024]{2,1,0:T(8,128)} %vol.1) | copy-start | bytes 786436
  1.0 13.3 %collective-permute-start = (f32[17,1,1024]{2,1,0:T(1,128)S(1)}, f32[17,1,1024]{2,1,0:T(1,128)S(1)}, u32[]{:S(2)}, u32[]{:S(2)}) collective-permute-start(f32[17,1,1024]{2,1,0:T(1,128)S(1)} %get-tuple-element.18), channel_id=1, source_target_pairs={{1,2},{3,4},{5,6},{2,1},{4,3},{6,5},{9,10},{11,12},{13,14},{10,9},... | collective-permute-start | bytes 208904 | tf_op jit(solution)/shard_map/ppermute | solution.py:406
  1.7 12.7 %collective-permute-start.1 = (f32[17,1,1024]{2,1,0:T(1,128)S(1)}, f32[17,1,1024]{2,1,0:T(1,128)S(1)}, u32[]{:S(2)}, u32[]{:S(2)}) collective-permute-start(f32[17,1,1024]{2,1,0:T(1,128)S(1)} %get-tuple-element.19), channel_id=1, source_target_pairs={{0,1},{2,3},{4,5},{6,7},{1,0},{3,2},{5,4},{7,6},{8,9},{10,11},{12,... | collective-permute-start | bytes 208904 | tf_op jit(solution)/shard_map/ppermute | solution.py:406
  8.1 6.7 %collective-permute-start.2 = (f32[1,16,1024]{2,1,0:T(8,128)S(1)}, f32[1,16,1024]{2,1,0:T(8,128)S(1)}, u32[]{:S(2)}, u32[]{:S(2)}) collective-permute-start(f32[1,16,1024]{2,1,0:T(8,128)S(1)} %get-tuple-element.22), channel_id=1, source_target_pairs={{8,16},{24,32},{40,48},{56,64},{72,80},{88,96},{104,112},{120,128}... | collective-permute-start | bytes 196616 | tf_op jit(solution)/shard_map/ppermute | solution.py:406
  12.4 3.1 %collective-permute-start.3 = (f32[1,16,1024]{2,1,0:T(8,128)S(1)}, f32[1,16,1024]{2,1,0:T(8,128)S(1)}, u32[]{:S(2)}, u32[]{:S(2)}) collective-permute-start(f32[1,16,1024]{2,1,0:T(8,128)S(1)} %get-tuple-element.23), channel_id=1, source_target_pairs={{0,8},{16,24},{32,40},{48,56},{64,72},{80,88},{96,104},{112,120},{... | collective-permute-start | bytes 196616 | tf_op jit(solution)/shard_map/ppermute | solution.py:406
  16.7 31.3 %all-to-all-start = ((f32[64,6,2,128]{3,2,1,0:T(2,128)}), f32[64,6,2,128]{3,2,1,0:T(2,128)S(1)}, u32[]{:S(2)}, u32[]{:S(2)}) async-start(f32[64,6,2,128]{3,2,1,0:T(2,128)} %bitcast), calls=%async_computation | async-start | bytes 786432 | tf_op jit(solution)/shard_map/all_to_all | solution.py:440
  31.9 6.2 %collective-permute-start.4 = (f32[224,128]{1,0:T(8,128)S(1)}, f32[224,128]{1,0:T(8,128)S(1)}, u32[]{:S(2)}, u32[]{:S(2)}) collective-permute-start(f32[224,128]{1,0:T(8,128)S(1)} %get-tuple-element.27.refs_0_), channel_id=1, source_target_pairs={{0,1},{1,0},{2,3},{3,2},{4,5},{5,4},{6,7},{7,6},{8,9},{9,8},{10,11... | collective-permute-start | bytes 344072 | tf_op jit(solution)/shard_map/ppermute | solution.py:445
  38.1 9.1 %collective-permute-start.5 = (f32[224,128]{1,0:T(8,128)S(1)}, f32[224,128]{1,0:T(8,128)S(1)}, u32[]{:S(2)}, u32[]{:S(2)}) collective-permute-start(f32[224,128]{1,0:T(8,128)S(1)} %shard_map.21.refs_0_.refs_2_), channel_id=1, source_target_pairs={{0,3},{1,2},{2,1},{3,0},{4,7},{5,6},{6,5},{7,4},{8,11},{9,10},{10,... | collective-permute-start | bytes 344072 | tf_op jit(solution)/shard_map/ppermute | solution.py:445
  49.1 16.4 %copy-start.1 = (f32[4,16,1024]{2,1,0:T(8,128)S(1)}, f32[4,16,1024]{2,1,0:T(8,128)}, u32[]{:S(2)}) copy-start(f32[4,16,1024]{2,1,0:T(8,128)} %vol.1) | copy-start | bytes 786436
  49.1 22.2 %all-to-all-start.1 = ((f32[64,2,2,128]{3,2,1,0:T(2,128)}), f32[64,2,2,128]{3,2,1,0:T(2,128)S(1)}, u32[]{:S(2)}, u32[]{:S(2)}) async-start(f32[64,2,2,128]{3,2,1,0:T(2,128)} %bitcast.2), calls=%async_computation.1 | async-start | bytes 262144 | tf_op jit(solution)/shard_map/all_to_all | solution.py:470
  60.5 9.0 %collective-permute-start.6 = (f32[96,128]{1,0:T(8,128)S(1)}, f32[96,128]{1,0:T(8,128)S(1)}, u32[]{:S(2)}, u32[]{:S(2)}) collective-permute-start(f32[96,128]{1,0:T(8,128)S(1)} %shard_map.22), channel_id=1, source_target_pairs={{0,4},{1,5},{2,6},{3,7},{4,0},{5,1},{6,2},{7,3},{8,12},{9,13},{10,... | collective-permute-start | bytes 147464 | tf_op jit(solution)/shard_map/ppermute | solution.py:445

commit v9 on v8

--- a/solution.py
+++ b/solution.py
@@ -463,7 +463,7 @@
             (3, NT // 2 // GROUP, LANES),
         ),
     )
-    lines, edge = lax.optimization_barrier((lines, edge))
+    lines, edge, timed = lax.optimization_barrier((lines, edge, timed))
     solved = call(
         wide_kernel, f32(WIDE * 4, LANES), lines.reshape(WIDE * WPORTS * 2, LANES)
     )

time: 72.5 us -> 72.5 us (level)
  no operation moved by 1% of the time
where the time goes in v9:
time: 72.5 us; the launch traced here: 72.1 us
  starting transfers between devices  53.6 us (74%)
  waiting for transfers between devices  12.3 us (17%)
  Pallas kernels  5.02 us (7%)
  local copies, waits for them, and re-layouts  0.96 us (1%)
    all_to_all x1, starting transfers between devices, per_device(): lax.all_to_all(wide_ports.reshape(WIDE, WPORTS, 2, LANES), wide_axes, spl...  15.2 us
    ppermute x3, starting transfers between devices, swapped(): return lax.ppermute(x, narrow_axes, [(n, n ^ step) for n in range(NARROW)])  13.7 us
    ppermute x4, starting transfers between devices, exchanged(): return lax.ppermute(layer, axis, pairs + [(j, i) for i, j in pairs])  13.3 us
    all_to_all x1, starting transfers between devices, per_device(): lax.all_to_all(solved.reshape(WIDE, 2, 2, LANES), wide_axes, split_axis=0...  11.4 us
    ppermute x3, waiting for transfers between devices, swapped(): return lax.ppermute(x, narrow_axes, [(n, n ^ step) for n in range(NARROW)])  9.6 us
    pallas_call x9, Pallas kernels, call(): pl.pallas_call(kernel, out_shape=out, scratch_shapes=[pltpu.VMEM(s, jnp.f...  5.02 us
  transfers between devices with their start and end apart: 9, of which 6 were waited for; matrix products, arithmetic and copies ran while one was open for 0% of the time, Pallas kernels for 3%

profile of v9, /device:TPU:1, one launch (start us, length us, event | category | flops | bytes accessed | tf_op | source)
XLA Modules:
  0.0 72.1 jit_solution(16718665747442719244)
XLA Ops:
  0.0 0.0 copy-start
  0.0 0.9 %copy-done = f32[4,16,1024]{2,1,0:T(8,128)S(1)} copy-done((f32[4,16,1024]{2,1,0:T(8,128)S(1)}, f32[4,16,1024]{2,1,0:T(8,128)}, u32[]{:S(2)}) %copy-start) | copy-done | bytes 262168
  1.0 0.7 collective-permute-start
  1.7 6.4 %collective-permute-start.1 = (f32[17,1,1024]{2,1,0:T(1,128)S(1)}, f32[17,1,1024]{2,1,0:T(1,128)S(1)}, u32[]{:S(2)}, u32[]{:S(2)}) collective-permute-start(f32[17,1,1024]{2,1,0:T(1,128)S(1)} %get-tuple-element.20), channel_id=1, source_target_pairs={{0,1},{2,3},{4,5},{6,7},{1,0},{3,2},{5,4},{7,6},{8,9},{10,11},{12,... | collective-permute-start | bytes 208904 | tf_op jit(solution)/shard_map/ppermute | solution.py:406
  8.1 4.3 %collective-permute-start.2 = (f32[1,16,1024]{2,1,0:T(8,128)S(1)}, f32[1,16,1024]{2,1,0:T(8,128)S(1)}, u32[]{:S(2)}, u32[]{:S(2)}) collective-permute-start(f32[1,16,1024]{2,1,0:T(8,128)S(1)} %get-tuple-element.23), channel_id=1, source_target_pairs={{8,16},{24,32},{40,48},{56,64},{72,80},{88,96},{104,112},{120,128}... | collective-permute-start | bytes 196616 | tf_op jit(solution)/shard_map/ppermute | solution.py:406
  12.4 1.9 %collective-permute-start.3 = (f32[1,16,1024]{2,1,0:T(8,128)S(1)}, f32[1,16,1024]{2,1,0:T(8,128)S(1)}, u32[]{:S(2)}, u32[]{:S(2)}) collective-permute-start(f32[1,16,1024]{2,1,0:T(8,128)S(1)} %get-tuple-element.24), channel_id=1, source_target_pairs={{0,8},{16,24},{32,40},{48,56},{64,72},{80,88},{96,104},{112,120},{... | collective-permute-start | bytes 196616 | tf_op jit(solution)/shard_map/ppermute | solution.py:406
  14.3 0.0 collective-permute-done.refs_1_
  14.3 0.0 collective-permute-done.1.refs_2_
  14.3 0.4 shard_map.18
  14.8 0.0 collective-permute-done.2.refs_3_
  14.8 0.8 %collective-permute-done.3.refs_4_ = f32[1,16,1024]{2,1,0:T(8,128)S(1)} collective-permute-done((f32[1,16,1024]{2,1,0:T(8,128)S(1)}, f32[1,16,1024]{2,1,0:T(8,128)S(1)}, u32[]{:S(2)}, u32[]{:S(2)}) %collective-permute-start.3) | collective-permute-done | bytes 65568 | tf_op jit(solution)/shard_map/ppermute | solution.py:406
  15.5 1.2 %shard_map.19 = (f32[4,16,1024]{2,1,0:T(8,128)S(1)}, f32[768,128]{1,0:T(8,128)}, f32[224,128]{1,0:T(8,128)S(1)}, f32[512,128]{1,0:T(8,128)S(1)}) custom-call(f32[4,16,1024]{2,1,0:T(8,128)S(1)} %copy-done, f32[4,16,1024]{2,1,0:T(8,128)S(1)} %get-tuple-element.21.refs_1_, f32[512,128]{1,0:T(8,128)S(1)} %get-tuple-element.22.refs_2_.refs_5_, ...), custom_call_target="tpu_custom_call" | custom-call | tf_op jit(solution)/shard_map/pallas_call | solution.py:393
  16.7 15.2 %all-to-all-start = ((f32[64,6,2,128]{3,2,1,0:T(2,128)}), f32[64,6,2,128]{3,2,1,0:T(2,128)S(1)}, u32[]{:S(2)}, u32[]{:S(2)}) async-start(f32[64,6,2,128]{3,2,1,0:T(2,128)} %bitcast), calls=%async_computation | async-start | bytes 786432 | tf_op jit(solution)/shard_map/all_to_all | solution.py:440
  31.9 0.0 copy-start.1
  32.0 2.1 %collective-permute-start.4 = (f32[224,128]{1,0:T(8,128)S(1)}, f32[224,128]{1,0:T(8,128)S(1)}, u32[]{:S(2)}, u32[]{:S(2)}) collective-permute-start(f32[224,128]{1,0:T(8,128)S(1)} %get-tuple-element.28.refs_0_), channel_id=1, source_target_pairs={{0,1},{1,0},{2,3},{3,2},{4,5},{5,4},{6,7},{7,6},{8,9},{9,8},{10,11... | collective-permute-start | bytes 344072 | tf_op jit(solution)/shard_map/ppermute | solution.py:445
  34.0 4.2 %collective-permute-done.4.refs_1_ = f32[224,128]{1,0:T(8,128)S(1)} collective-permute-done((f32[224,128]{1,0:T(8,128)S(1)}, f32[224,128]{1,0:T(8,128)S(1)}, u32[]{:S(2)}, u32[]{:S(2)}) %collective-permute-start.4) | collective-permute-done | bytes 114720 | tf_op jit(solution)/shard_map/ppermute | solution.py:445
  38.3 6.6 %collective-permute-start.5 = (f32[224,128]{1,0:T(8,128)S(1)}, f32[224,128]{1,0:T(8,128)S(1)}, u32[]{:S(2)}, u32[]{:S(2)}) collective-permute-start(f32[224,128]{1,0:T(8,128)S(1)} %shard_map.21.refs_0_.refs_2_), channel_id=1, source_target_pairs={{0,3},{1,2},{2,1},{3,0},{4,7},{5,6},{6,5},{7,4},{8,11},{9,10},{10,... | collective-permute-start | bytes 344072 | tf_op jit(solution)/shard_map/ppermute | solution.py:445
  44.9 0.0 copy-done.1
  44.9 1.1 %shard_map.20 = (f32[4,16,1024]{2,1,0:T(8,128)S(1)}, f32[6,16,1024]{2,1,0:T(8,128)S(1)}) custom-call(f32[4,16,1024]{2,1,0:T(8,128)S(1)} %copy-done.1, f32[4,16,1024]{2,1,0:T(8,128)S(1)} %get-tuple-element.25.cond), custom_call_target="tpu_custom_call" | custom-call | tf_op jit(solution)/shard_map/pallas_call | solution.py:393
  46.1 1.4 %collective-permute-done.5.refs_1_.refs_3_ = f32[224,128]{1,0:T(8,128)S(1)} collective-permute-done((f32[224,128]{1,0:T(8,128)S(1)}, f32[224,128]{1,0:T(8,128)S(1)}, u32[]{:S(2)}, u32[]{:S(2)}) %collective-permute-start.5) | collective-permute-done | bytes 114720 | tf_op jit(solution)/shard_map/ppermute | solution.py:445
  47.5 0.6 all-to-all-done
  48.1 1.1 %shard_map.23 = f32[256,128]{1,0:T(8,128)} custom-call(f32[768,128]{1,0:T(8,128)S(1)} %bitcast.4), custom_call_target="tpu_custom_call" | custom-call | tf_op jit(solution)/shard_map/pallas_call | solution.py:393
  49.1 11.4 %all-to-all-start.1 = ((f32[64,2,2,128]{3,2,1,0:T(2,128)}), f32[64,2,2,128]{3,2,1,0:T(2,128)S(1)}, u32[]{:S(2)}, u32[]{:S(2)}) async-start(f32[64,2,2,128]{3,2,1,0:T(2,128)} %bitcast.2), calls=%async_computation.1 | async-start | bytes 262144 | tf_op jit(solution)/shard_map/all_to_all | solution.py:470
  60.5 5.0 %collective-permute-start.6 = (f32[96,128]{1,0:T(8,128)S(1)}, f32[96,128]{1,0:T(8,128)S(1)}, u32[]{:S(2)}, u32[]{:S(2)}) collective-permute-start(f32[96,128]{1,0:T(8,128)S(1)} %shard_map.22), channel_id=1, source_target_pairs={{0,4},{1,5},{2,6},{3,7},{4,0},{5,1},{6,2},{7,3},{8,12},{9,13},{10,... | collective-permute-start | bytes 147464 | tf_op jit(solution)/shard_map/ppermute | solution.py:445
  65.5 4.0 %collective-permute-done.6.refs_4_ = f32[96,128]{1,0:T(8,128)S(1)} collective-permute-done((f32[96,128]{1,0:T(8,128)S(1)}, f32[96,128]{1,0:T(8,128)S(1)}, u32[]{:S(2)}, u32[]{:S(2)}) %collective-permute-start.6) | collective-permute-done | bytes 49184 | tf_op jit(solution)/shard_map/ppermute | solution.py:445
  69.5 0.4 shard_map.24.others
  69.9 1.4 %all-to-all-done.1 = f32[64,2,2,128]{3,2,1,0:T(2,128)S(1)} async-done(((f32[64,2,2,128]{3,2,1,0:T(2,128)}), f32[64,2,2,128]{3,2,1,0:T(2,128)S(1)}, u32[]{:S(2)}, u32[]{:S(2)}) %all-to-all-start.1) | async-done | bytes 131104 | tf_op jit(solution)/shard_map/all_to_all | solution.py:470
  71.3 0.8 %shard_map.25 = f32[4,16,1024]{2,1,0:T(8,128)} custom-call(f32[6,16,1024]{2,1,0:T(8,128)S(1)} %get-tuple-element.26.inner, f32[256,128]{1,0:T(8,128)S(1)} %bitcast.5, f32[4,16,1024]{2,1,0:T(8,128)S(1)} %shard_map.24.others), custom_call_target="tpu_custom_call" | custom-call | tf_op jit(solution)/shard_map/pallas_call | solution.py:393
  (3 shorter events, 0.1 us)
Async XLA Ops:
  0.0 0.9 %copy-start = (f32[4,16,1024]{2,1,0:T(8,128)S(1)}, f32[4,16,1024]{2,1,0:T(8,128)}, u32[]{:S(2)}) copy-start(f32[4,16,1024]{2,1,0:T(8,128)} %vol.1) | copy-start | bytes 786436
  1.0 13.3 %collective-permute-start = (f32[17,1,1024]{2,1,0:T(1,128)S(1)}, f32[17,1,1024]{2,1,0:T(1,128)S(1)}, u32[]{:S(2)}, u32[]{:S(2)}) collective-permute-start(f32[17,1,1024]{2,1,0:T(1,128)S(1)} %get-tuple-element.19), channel_id=1, source_target_pairs={{1,2},{3,4},{5,6},{2,1},{4,3},{6,5},{9,10},{11,12},{13,14},{10,9},... | collective-permute-start | bytes 208904 | tf_op jit(solution)/shard_map/ppermute | solution.py:406
  1.7 12.7 %collective-permute-start.1 = (f32[17,1,1024]{2,1,0:T(1,128)S(1)}, f32[17,1,1024]{2,1,0:T(1,128)S(1)}, u32[]{:S(2)}, u32[]{:S(2)}) collective-permute-start(f32[17,1,1024]{2,1,0:T(1,128)S(1)} %get-tuple-element.20), channel_id=1, source_target_pairs={{0,1},{2,3},{4,5},{6,7},{1,0},{3,2},{5,4},{7,6},{8,9},{10,11},{12,... | collective-permute-start | bytes 208904 | tf_op jit(solution)/shard_map/ppermute | solution.py:406
  8.1 6.7 %collective-permute-start.2 = (f32[1,16,1024]{2,1,0:T(8,128)S(1)}, f32[1,16,1024]{2,1,0:T(8,128)S(1)}, u32[]{:S(2)}, u32[]{:S(2)}) collective-permute-start(f32[1,16,1024]{2,1,0:T(8,128)S(1)} %get-tuple-element.23), channel_id=1, source_target_pairs={{8,16},{24,32},{40,48},{56,64},{72,80},{88,96},{104,112},{120,128}... | collective-permute-start | bytes 196616 | tf_op jit(solution)/shard_map/ppermute | solution.py:406
  12.4 3.1 %collective-permute-start.3 = (f32[1,16,1024]{2,1,0:T(8,128)S(1)}, f32[1,16,1024]{2,1,0:T(8,128)S(1)}, u32[]{:S(2)}, u32[]{:S(2)}) collective-permute-start(f32[1,16,1024]{2,1,0:T(8,128)S(1)} %get-tuple-element.24), channel_id=1, source_target_pairs={{0,8},{16,24},{32,40},{48,56},{64,72},{80,88},{96,104},{112,120},{... | collective-permute-start | bytes 196616 | tf_op jit(solution)/shard_map/ppermute | solution.py:406
  16.7 31.3 %all-to-all-start = ((f32[64,6,2,128]{3,2,1,0:T(2,128)}), f32[64,6,2,128]{3,2,1,0:T(2,128)S(1)}, u32[]{:S(2)}, u32[]{:S(2)}) async-start(f32[64,6,2,128]{3,2,1,0:T(2,128)} %bitcast), calls=%async_computation | async-start | bytes 786432 | tf_op jit(solution)/shard_map/all_to_all | solution.py:440
  31.9 13.0 %copy-start.1 = (f32[4,16,1024]{2,1,0:T(8,128)S(1)}, f32[4,16,1024]{2,1,0:T(8,128)}, u32[]{:S(2)}) copy-start(f32[4,16,1024]{2,1,0:T(8,128)} %vol.1) | copy-start | bytes 786436
  32.0 6.3 %collective-permute-start.4 = (f32[224,128]{1,0:T(8,128)S(1)}, f32[224,128]{1,0:T(8,128)S(1)}, u32[]{:S(2)}, u32[]{:S(2)}) collective-permute-start(f32[224,128]{1,0:T(8,128)S(1)} %get-tuple-element.28.refs_0_), channel_id=1, source_target_pairs={{0,1},{1,0},{2,3},{3,2},{4,5},{5,4},{6,7},{7,6},{8,9},{9,8},{10,11... | collective-permute-start | bytes 344072 | tf_op jit(solution)/shard_map/ppermute | solution.py:445
  38.3 9.1 %collective-permute-start.5 = (f32[224,128]{1,0:T(8,128)S(1)}, f32[224,128]{1,0:T(8,128)S(1)}, u32[]{:S(2)}, u32[]{:S(2)}) collective-permute-start(f32[224,128]{1,0:T(8,128)S(1)} %shard_map.21.refs_0_.refs_2_), channel_id=1, source_target_pairs={{0,3},{1,2},{2,1},{3,0},{4,7},{5,6},{6,5},{7,4},{8,11},{9,10},{10,... | collective-permute-start | bytes 344072 | tf_op jit(solution)/shard_map/ppermute | solution.py:445
  49.1 22.2 %all-to-all-start.1 = ((f32[64,2,2,128]{3,2,1,0:T(2,128)}), f32[64,2,2,128]{3,2,1,0:T(2,128)S(1)}, u32[]{:S(2)}, u32[]{:S(2)}) async-start(f32[64,2,2,128]{3,2,1,0:T(2,128)} %bitcast.2), calls=%async_computation.1 | async-start | bytes 262144 | tf_op jit(solution)/shard_map/all_to_all | solution.py:470
  60.5 9.0 %collective-permute-start.6 = (f32[96,128]{1,0:T(8,128)S(1)}, f32[96,128]{1,0:T(8,128)S(1)}, u32[]{:S(2)}, u32[]{:S(2)}) collective-permute-start(f32[96,128]{1,0:T(8,128)S(1)} %shard_map.22), channel_id=1, source_target_pairs={{0,4},{1,5},{2,6},{3,7},{4,0},{5,1},{6,2},{7,3},{8,12},{9,13},{10,... | collective-permute-start | bytes 147464 | tf_op jit(solution)/shard_map/ppermute | solution.py:445
